TPU v7x, 32 devices: a whole 2x2x4 slice. The times are simulated.
32 devices in a mesh: leaf: 4 (over z), row: 4 (over y, x), col: 2 (over core).
Axes of the slice: x: 2, y: 2, z: 4, core: 2. Of those that a mesh axis runs over, the one named last changes fastest.
Arguments:
- leaf_rhs: bfloat16 [8192, 1024], P(('leaf', 'col'), 'row'), may hold values from -6 to 6
- leaf_inverse: bfloat16 [8192, 2048], P('leaf', 'col'), may hold values from -0.125 to 0.125
- leaf_below: bfloat16 [8192, 2048], P('leaf', 'col'), may hold values from -0.0625 to 0.0625
- leaf_rows: int32 [4, 16], P('leaf'), may hold values from 16 to 63, as said below
- sep_rhs: bfloat16 [8192, 1024], P(('leaf', 'col'), 'row'), may hold values from -6 to 6
- sep_inverse: bfloat16 [8192, 2048], P('leaf', 'col'), may hold values from -0.125 to 0.125
- sep_below: bfloat16 [4096, 2048], P('leaf', 'col'), may hold values from -0.0625 to 0.0625
- sep_rows: int32 [4, 8], P('leaf'), may hold values from 16 to 63, as said below
- sep_width: int32 [4], replicated, may hold values from 1024 to 2048, as said below
Outputs:
- leaf_solution: bfloat16 [8192, 1024], P(('leaf', 'col'), 'row')
- sep_solution: bfloat16 [8192, 1024], P(('leaf', 'col'), 'row')
Inputs may be any that keep to these rules, and one draw needn't show every extreme that they name: `sep_width`: multiples of 128; slot 4 / 2 (the root) has 2048; entry 0 is not used. `leaf_rows`: row i holds 16 different block rows a * 16 + p of the ancestors a of subtree i, with p * 128 < sep_width[a]. `sep_rows`: row a, for a slot a below the root, holds 8 different block rows b * 16 + p of the slots b at higher levels on the path from a to the root, with p * 128 < sep_width[b]; rows 0 and 2 are not used.
All inputs are finite; a program needn't handle non-finite values.
Results may differ from a plain program's by a relative error of at most 0.0065.
Values sent between devices are 32-bit elements; how exact they have to be, the bound alone decides.
No kernel may reach another device: no remote copies, remote signals or barrier semaphores. Data moves between devices by JAX's collectives and lax.ppermute only.
A program may use at most 128 MiB of HBM per device.

v0:
```python
import jax
import jax.numpy as jnp
from jax import lax
from jax.sharding import PartitionSpec as P

PANEL = 128


def from_partner(value, axis, stride):
    return lax.ppermute(value, axis, [(i, i ^ 1 << stride) for i in range(lax.axis_size(axis))])


def unit_lower(matrix, col_start):
    rows_here = lax.broadcasted_iota(jnp.int32, matrix.shape, 0)
    cols_here = col_start + lax.broadcasted_iota(jnp.int32, matrix.shape, 1)
    kept_lower = jnp.where(rows_here > cols_here, matrix, jnp.zeros_like(matrix))
    return jnp.where(rows_here == cols_here, jnp.ones_like(matrix), kept_lower)


def slot_level(slot_val, levels):
    depth_now = jnp.ones_like(slot_val)
    for bit_pos in range(1, levels + 1):
        depth_now = depth_now + (slot_val % 2**bit_pos == 0).astype(jnp.int32)
    return depth_now


def local_panels(panel_ids, levels, sep_panels):
    slot_val = panel_ids // sep_panels
    return (slot_level(slot_val, levels) - 1) * sep_panels + panel_ids % sep_panels


def leaf_product(inverse, right_side, col_start):
    masked = unit_lower(inverse, col_start)
    return lax.psum_scatter(
        jnp.dot(masked, right_side, preferred_element_type=jnp.float32),
        "col",
        scatter_dimension=0,
        tiled=True,
    )


def sep_product(inverse, right_side, col_start):
    masked = unit_lower(inverse, col_start)
    return lax.psum_scatter(
        jnp.dot(masked, right_side, preferred_element_type=jnp.float32),
        "col",
        scatter_dimension=0,
        tiled=True,
    )


def pair_sum(piece_sum, depth_now):
    for bit_pos in range(depth_now):
        piece_sum = piece_sum + from_partner(piece_sum, "leaf", bit_pos)
    return piece_sum


def on_device(
    leaf_rhs,
    leaf_inverse,
    leaf_below,
    leaf_rows,
    sep_rhs,
    sep_inverse,
    sep_below,
    sep_rows,
    sep_width,
):
    leaves = lax.axis_size("leaf")
    levels = leaves.bit_length() - 1
    leaf_index = lax.axis_index("leaf")
    col_index = lax.axis_index("col")
    sep_cols = sep_inverse.shape[0]
    sep_piece = sep_inverse.shape[1]
    sep_panels = sep_cols // PANEL
    width_rhs = leaf_rhs.shape[1]
    leaf_piece = leaf_inverse.shape[1]
    leaf_sum = leaf_product(leaf_inverse, leaf_rhs, col_index * leaf_piece)
    leaf_solution = leaf_sum.astype(jnp.bfloat16)
    leaf_term = jnp.dot(leaf_below, leaf_solution, preferred_element_type=jnp.float32).reshape(
        -1, PANEL, width_rhs
    )
    pending = jnp.zeros((levels * sep_panels, PANEL, width_rhs), jnp.float32)
    pending = pending.at[local_panels(leaf_rows[0], levels, sep_panels)].add(leaf_term)
    sep_local = local_panels(sep_rows[0], levels, sep_panels)
    slot_ids = jnp.arange(leaves, dtype=jnp.int32)
    columns = col_index * sep_piece + jnp.arange(sep_piece, dtype=jnp.int32)
    sep_solution = jnp.zeros((sep_piece, width_rhs), jnp.bfloat16)
    for level_now in range(1, levels + 1):
        span_now = 2**level_now
        slot_now = leaf_index - leaf_index % span_now + span_now // 2
        is_owner = leaf_index == slot_now
        level_block = pending[(level_now - 1) * sep_panels : level_now * sep_panels].reshape(
            sep_cols, width_rhs
        )
        piece_sum = lax.psum_scatter(level_block, "col", scatter_dimension=0, tiled=True)
        piece_sum = pair_sum(piece_sum, level_now)
        residual = (sep_rhs.astype(jnp.float32) - piece_sum).astype(jnp.bfloat16)
        product = sep_product(sep_inverse, residual, col_index * sep_piece)
        width_now = jnp.sum(jnp.where(slot_ids == slot_now, sep_width, 0))
        solution = jnp.where(columns[:, None] < width_now, product, 0.0).astype(jnp.bfloat16)
        sep_solution = jnp.where(is_owner, solution, sep_solution)
        if level_now < levels:
            update_term = jnp.dot(sep_below, solution, preferred_element_type=jnp.float32).reshape(
                -1, PANEL, width_rhs
            )
            update_term = jnp.where(is_owner, update_term, 0.0)
            pending = pending.at[sep_local].add(update_term)
    return (leaf_solution, sep_solution)


def solution(mesh):
    placed = (
        P(("leaf", "col"), "row"),
        P("leaf", "col"),
        P("leaf", "col"),
        P("leaf", None),
        P(("leaf", "col"), "row"),
        P("leaf", "col"),
        P("leaf", "col"),
        P("leaf", None),
        P(),
    )
    return jax.shard_map(
        on_device,
        mesh=mesh,
        in_specs=placed,
        out_specs=(P(("leaf", "col"), "row"), P(("leaf", "col"), "row")),
        check_vma=False,
    )
```

profile of v0, /device:TPU:21, one launch (start us, length us, event | category | flops | bytes accessed | tf_op | source)
XLA Modules:
  0.0 221.3 jit_solution(11858572847206982528)
XLA Ops:
  7.2 0.0 copy-start
  7.2 0.0 reduce-scatter.6.cloned.1.call-start
  7.2 0.0 copy-start.4
  7.3 5.9 %fusion.4 = f32[2048,256]{1,0:T(8,128)} fusion(bf16[1024,256]{1,0:T(8,128)(2,1)} %param.9, bf16[2048,1024]{1,0:T(8,128)(2,1)} %param.10, s32[1024]{0:T(1024)S(1)} %iota_add_fusion), kind=kOutput, calls=%fused_computation.8 | convolution fusion | flops 1082130432 | bytes 6819840 | tf_op jit(solution)/shard_map/dot_general | solution.py:35
  13.2 0.0 reduce-scatter.6.cloned.1.call-update
  13.2 0.0 reduce-scatter.8.cloned.1.call-start
  13.2 0.0 copy-done.4
  13.3 11.4 %reduce-scatter.6.cloned.1.call-done = f32[1024,256]{1,0:T(8,128)} async-done(((f32[2048,256]{1,0:T(8,128)}), f32[1024,256]{1,0:T(8,128)}) %reduce-scatter.6.cloned.1.call-update) | async-done | bytes 1048592 | tf_op jit(solution)/shard_map/reduce_scatter | solution.py:34
  24.7 1.3 convert_element_type.59
  26.0 0.0 copy-start.2
  26.0 0.8 copy-done.2
  26.8 4.9 %convolution_bitcast_fusion = f32[2048,256]{0,1:T(8,128)} fusion(bf16[1024,256]{1,0:T(8,128)(2,1)S(1)} %convert_element_type.59, bf16[2048,1024]{1,0:T(8,128)(2,1)} %param.11), kind=kOutput, calls=%fused_computation.10 | convolution fusion | flops 1073741824 | bytes 6815744 | tf_op jit(solution)/shard_map/dot_general | solution.py:80
  31.6 2.9 %copy.13 = f32[2048,256]{1,0:T(8,128)} copy(f32[2048,256]{0,1:T(8,128)} %convolution_bitcast_fusion) | data formatting | bytes 4194304 | tf_op jit(solution)/shard_map/reshape | solution.py:80
  34.6 2.4 %broadcast_in_dim.39 = f32[32,128,256]{2,1,0:T(8,128)} broadcast(f32[]{:T(128)} %constant.111.clone.1), dimensions={} | broadcast | bytes 4194308 | tf_op jit(solution)/shard_map/broadcast_in_dim | solution.py:83
  37.0 5.3 %scatter_fusion = f32[32,128,256]{2,1,0:T(8,128)} fusion(f32[32,128,256]{2,1,0:T(8,128)} %broadcast_in_dim.39, s32[16]{0:T(128)S(1)} %fusion.34, f32[16,128,256]{2,1,0:T(8,128)} %bitcast.46), kind=kCustom, calls=%fused_computation | custom fusion | flops 524288 | bytes 6291520 | tf_op jit(solution)/shard_map/scatter-add | solution.py:84
  42.3 3.1 %slice.8 = f32[16,128,256]{2,1,0:T(8,128)} slice(f32[32,128,256]{2,1,0:T(8,128)} %scatter_fusion), slice={[0:16], [0:128], [0:256]} | slice | bytes 4194304 | tf_op jit(solution)/shard_map/slice | solution.py:93
  45.4 0.0 reduce-scatter.8.cloned.1.call-update
  45.4 0.0 copy-start.3
  45.5 0.0 copy-start.5
  45.5 0.0 reduce-scatter.10.cloned.1.call-start
  45.5 10.9 %reduce-scatter.8.cloned.1.call-done = f32[1024,256]{1,0:T(8,128)} async-done(((f32[2048,256]{1,0:T(8,128)}), f32[1024,256]{1,0:T(8,128)}) %reduce-scatter.8.cloned.1.call-update) | async-done | bytes 1048592 | tf_op jit(solution)/shard_map/reduce_scatter | solution.py:96
  56.4 1.2 collective-permute-start
  57.6 23.5 %collective-permute-done = f32[1024,256]{1,0:T(8,128)S(1)} collective-permute-done((f32[1024,256]{1,0:T(8,128)}, f32[1024,256]{1,0:T(8,128)S(1)}, u32[]{:S(2)}, u32[]{:S(2)}) %collective-permute-start) | collective-permute-done | bytes 1048608 | tf_op jit(solution)/shard_map/ppermute | solution.py:10
  81.1 6.2 %fusion.10 = f32[2048,256]{1,0:T(8,128)} fusion(bf16[2048,1024]{1,0:T(8,128)(2,1)} %param.14, s32[1024]{0:T(1024)S(1)} %iota_add_fusion, bf16[1024,256]{1,0:T(8,128)(2,1)} %param.13, f32[1024,256]{1,0:T(8,128)} %reduce-scatter.8.cloned.1.call-done, f32[1024,256]{1,0:T(8,128)S(1)} %collective-permute-done), kind=kOutput, calls=%fused_computation.12 | convolution fusion | flops 1083179008 | bytes 8916992 | tf_op jit(solution)/shard_map/dot_general | solution.py:45
  87.3 0.0 reduce-scatter.10.cloned.1.call-update
  87.4 0.0 reduce-scatter.12.cloned.1.call-start
  87.4 0.0 copy-done.3
  87.5 0.7 fusion.28
  88.2 0.7 fusion.24
  88.9 0.0 copy-done.5
  88.9 10.2 %reduce-scatter.10.cloned.1.call-done = f32[1024,256]{1,0:T(8,128)} async-done(((f32[2048,256]{1,0:T(8,128)}), f32[1024,256]{1,0:T(8,128)}) %reduce-scatter.10.cloned.1.call-update) | async-done | bytes 1048592 | tf_op jit(solution)/shard_map/reduce_scatter | solution.py:44
  99.1 2.2 fusion.18
  101.4 1.3 copy.14
  102.7 3.7 %scatter_fusion.1 = f32[32,128,256]{2,1,0:T(8,128)} fusion(f32[32,128,256]{2,1,0:T(8,128)} %scatter_fusion, s32[8]{0:T(128)S(1)} %fusion.35, f32[8,128,256]{2,1,0:T(8,128)} %bitcast.49), kind=kCustom, calls=%fused_computation.1 | custom fusion | flops 262144 | bytes 3145760 | tf_op jit(solution)/shard_map/scatter-add | solution.py:108
  106.4 3.1 %slice.9 = f32[16,128,256]{2,1,0:T(8,128)} slice(f32[32,128,256]{2,1,0:T(8,128)} %scatter_fusion.1), slice={[16:32], [0:128], [0:256]} | slice | bytes 4194304 | tf_op jit(solution)/shard_map/slice | solution.py:93
  109.5 0.0 reduce-scatter.12.cloned.1.call-update
  109.5 0.2 reduce-scatter.14.cloned.1.call-start
  109.8 10.7 %reduce-scatter.12.cloned.1.call-done = f32[1024,256]{1,0:T(8,128)} async-done(((f32[2048,256]{1,0:T(8,128)}), f32[1024,256]{1,0:T(8,128)}) %reduce-scatter.12.cloned.1.call-update) | async-done | bytes 1048592 | tf_op jit(solution)/shard_map/reduce_scatter | solution.py:96
  120.4 1.2 collective-permute-start.1
  121.6 23.5 %collective-permute-done.1 = f32[1024,256]{1,0:T(8,128)S(1)} collective-permute-done((f32[1024,256]{1,0:T(8,128)}, f32[1024,256]{1,0:T(8,128)S(1)}, u32[]{:S(2)}, u32[]{:S(2)}) %collective-permute-start.1) | collective-permute-done | bytes 1048608 | tf_op jit(solution)/shard_map/ppermute | solution.py:10
  145.2 1.4 add.237
  146.5 0.3 collective-permute-start.2
  146.8 44.4 %collective-permute-done.2 = f32[1024,256]{1,0:T(8,128)S(1)} collective-permute-done((f32[1024,256]{1,0:T(8,128)S(1)}, f32[1024,256]{1,0:T(8,128)S(1)}, u32[]{:S(2)}, u32[]{:S(2)}) %collective-permute-start.2) | collective-permute-done | bytes 1048608 | tf_op jit(solution)/shard_map/ppermute | solution.py:10
  191.2 5.9 %fusion.8 = f32[2048,256]{1,0:T(8,128)} fusion(bf16[2048,1024]{1,0:T(8,128)(2,1)} %param.14, s32[1024]{0:T(1024)S(1)} %iota_add_fusion, bf16[1024,256]{1,0:T(8,128)(2,1)} %param.13, f32[1024,256]{1,0:T(8,128)S(1)} %add.237, f32[1024,256]{1,0:T(8,128)S(1)} %collective-permute-done.2), kind=kOutput, calls=%fused_computation.11 | convolution fusion | flops 1083179008 | bytes 8916992 | tf_op jit(solution)/shard_map/dot_general | solution.py:45
  197.1 0.0 reduce-scatter.14.cloned.1.call-update
  197.1 0.7 fusion.25
  197.8 14.4 %reduce-scatter.14.cloned.1.call-done = f32[1024,256]{1,0:T(8,128)} async-done(((f32[2048,256]{1,0:T(8,128)}), f32[1024,256]{1,0:T(8,128)}) %reduce-scatter.14.cloned.1.call-update) | async-done | bytes 1048592 | tf_op jit(solution)/shard_map/reduce_scatter | solution.py:44
  212.2 2.6 %fusion.21 = bf16[1024,256]{1,0:T(8,128)(2,1)} fusion(f32[1024,256]{1,0:T(8,128)} %reduce-scatter.14.cloned.1.call-done, pred[1024]{0:T(1024)(128)(4,1)S(1)} %fusion.25, pred[]{:T(512)S(6)} %eq.82, pred[]{:T(512)S(6)} %eq.75, f32[1024,256]{1,0:T(8,128)S(1)} %copy-done.1, pred[1024]{0:T(1024)(128)(4,1)S(1)} %fusion.24), kind=kLoop, calls=%fused_computation.27 | loop fusion | flops 1048576 | bytes 2623490 | tf_op jit(solution)/shard_map/jit(_where)/select_n | solution.py:102
  (6 shorter events, 0.1 us)
Async XLA Ops:
  7.2 92.0 %copy-start = (bf16[1024,1024]{1,0:T(8,128)(2,1)S(1)}, bf16[1024,1024]{1,0:T(8,128)(2,1)}, u32[]{:S(2)}) copy-start(bf16[1024,1024]{1,0:T(8,128)(2,1)} %param.15) | copy-start | bytes 6291460
  7.2 17.5 %reduce-scatter.6.cloned.1.call-start = ((), (), s32[]{:S(2)}) async-start(), calls=%async_computation.5 | async-start | bytes 3145728 | tf_op jit(solution)/shard_map/reduce_scatter | solution.py:34
  7.2 6.0 %copy-start.4 = (s32[1,16]{1,0:T(1,128)S(1)}, s32[1,16]{1,0:T(1,128)}, u32[]{:S(2)}) copy-start(s32[1,16]{1,0:T(1,128)} %param.12) | copy-start | bytes 196
  13.2 43.2 %reduce-scatter.8.cloned.1.call-start = ((), (), s32[]{:S(2)}) async-start(), calls=%async_computation.6 | async-start | bytes 3145728 | tf_op jit(solution)/shard_map/reduce_scatter | solution.py:96
  26.0 0.8 copy-start.2
  45.4 42.0 %copy-start.3 = (s32[4]{0:T(128)S(1)}, s32[4]{0:T(128)}, u32[]{:S(2)}) copy-start(s32[4]{0:T(128)} %param.17) | copy-start | bytes 52
  45.5 43.4 %copy-start.5 = (s32[1,8]{1,0:T(1,128)S(1)}, s32[1,8]{1,0:T(1,128)}, u32[]{:S(2)}) copy-start(s32[1,8]{1,0:T(1,128)} %param.16) | copy-start | bytes 100
  45.5 53.7 %reduce-scatter.10.cloned.1.call-start = ((), (), s32[]{:S(2)}) async-start(), calls=%async_computation.7 | async-start | bytes 3145728 | tf_op jit(solution)/shard_map/reduce_scatter | solution.py:44
  56.4 24.7 %collective-permute-start = (f32[1024,256]{1,0:T(8,128)}, f32[1024,256]{1,0:T(8,128)S(1)}, u32[]{:S(2)}, u32[]{:S(2)}) collective-permute-start(f32[1024,256]{1,0:T(8,128)} %reduce-scatter.8.cloned.1.call-done), channel_id=1, source_target_pairs={{0,8},{8,0},{16,24},{24,16},{1,9},{9,1},{17,25},{25,17},{2,10},{10... | collective-permute-start | bytes 3145736 | tf_op jit(solution)/shard_map/ppermute | solution.py:10
  87.4 33.1 %reduce-scatter.12.cloned.1.call-start = ((), (), s32[]{:S(2)}) async-start(), calls=%async_computation.8 | async-start | bytes 3145728 | tf_op jit(solution)/shard_map/reduce_scatter | solution.py:96
  109.5 102.7 %reduce-scatter.14.cloned.1.call-start = ((), (), s32[]{:S(2)}) async-start(), calls=%async_computation.9 | async-start | bytes 3145728 | tf_op jit(solution)/shard_map/reduce_scatter | solution.py:44
  120.4 24.7 %collective-permute-start.1 = (f32[1024,256]{1,0:T(8,128)}, f32[1024,256]{1,0:T(8,128)S(1)}, u32[]{:S(2)}, u32[]{:S(2)}) collective-permute-start(f32[1024,256]{1,0:T(8,128)} %reduce-scatter.12.cloned.1.call-done), channel_id=1, source_target_pairs={{0,8},{8,0},{16,24},{24,16},{1,9},{9,1},{17,25},{25,17},{2,10},{10... | collective-permute-start | bytes 3145736 | tf_op jit(solution)/shard_map/ppermute | solution.py:10
  146.5 65.7 %copy-start.1 = (f32[1024,256]{1,0:T(8,128)S(1)}, f32[1024,256]{1,0:T(8,128)}, u32[]{:S(2)}) copy-start(f32[1024,256]{1,0:T(8,128)} %reduce-scatter.10.cloned.1.call-done) | copy-start | bytes 3145732
  146.5 44.7 %collective-permute-start.2 = (f32[1024,256]{1,0:T(8,128)S(1)}, f32[1024,256]{1,0:T(8,128)S(1)}, u32[]{:S(2)}, u32[]{:S(2)}) collective-permute-start(f32[1024,256]{1,0:T(8,128)S(1)} %add.237), channel_id=1, source_target_pairs={{0,16},{8,24},{16,0},{24,8},{1,17},{9,25},{17,1},{25,9},{2,18},{10... | collective-permute-start | bytes 3145736 | tf_op jit(solution)/shard_map/ppermute | solution.py:10
Sparse Core Ops, SparseCore 0:
  13.3 11.3 reduce-scatter.5
  45.6 10.7 reduce-scatter.7
  87.5 11.5 reduce-scatter.9
  109.7 10.7 reduce-scatter.11
  197.2 14.9 reduce-scatter.13
where the time goes:
time: 223 us; the launch traced here: 221 us
  waiting for transfers between devices  149 us (67%)
  matrix products  25.1 us (11%)
  other arithmetic  16.4 us (7%)
  between operations  13.9 us (6%)
  local copies, waits for them, and re-layouts  13.7 us (6%)
  starting transfers between devices  3.12 us (1%)
    ppermute x3, waiting for transfers between devices, from_partner(): lax.ppermute(value, axis, [(i, i ^ 1 << stride) for i in range(lax.axis_s...  91.4 us
    reduce_scatter x2, waiting for transfers between devices, sep_product(): lax.psum_scatter(jnp.dot(masked, right_side, preferred_element_type=jnp.f...  24.7 us
    reduce_scatter x2, waiting for transfers between devices, on_device(): lax.psum_scatter(level_block, 'col', scatter_dimension=0, tiled=True)  21.5 us
    dot_general x2, matrix products, sep_product(): jnp.dot(masked, right_side, preferred_element_type=jnp.float32)  12.1 us
    reduce_scatter x1, waiting for transfers between devices, leaf_product(): lax.psum_scatter(jnp.dot(masked, right_side, preferred_element_type=jnp.f...  11.4 us
    slice x2, local copies, waits for them, and re-layouts, on_device(): pending[(level_now - 1) * sep_panels:level_now * sep_panels]  6.21 us
    dot_general x1, matrix products, leaf_product(): jnp.dot(masked, right_side, preferred_element_type=jnp.float32)  5.9 us
    scatter-add x1, other arithmetic, on_device(): pending.at[local_panels(leaf_rows[0], levels, sep_panels)].add(leaf_term)  5.35 us
  transfers between devices with their start and end apart: 8, of which 8 were waited for; matrix products, arithmetic and copies ran while one was open for 1% of the time, Pallas kernels for 0%

commit v1 on v0

v1 whole, which is shorter than its diff:
```python
import functools

import jax
import jax.numpy as jnp
from jax import lax
from jax.experimental import pallas as pl
from jax.experimental.pallas import tpu as pltpu
from jax.sharding import PartitionSpec as P

PANEL = 128
TILE = 256
TAGS = 128
F32 = jnp.float32
BF16 = jnp.bfloat16
ANY = pl.BlockSpec(memory_space=pl.ANY)
VMEM = pl.BlockSpec(memory_space=pltpu.VMEM)
SMEM = pl.BlockSpec(memory_space=pltpu.SMEM)


def dot(left, right):
    return jnp.dot(left, right, preferred_element_type=F32)


def call(body, ins, specs, outs, out_specs, scratch=(), flops=0, moved=0):
    return pl.pallas_call(
        body,
        out_shape=outs,
        in_specs=specs,
        out_specs=out_specs,
        scratch_shapes=list(scratch),
        compiler_params=pltpu.CompilerParams(vmem_limit_bytes=40 * 2**20),
        cost_estimate=pl.CostEstimate(flops=flops, bytes_accessed=moved, transcendentals=0),
    )(*ins)


def shape(rows, cols, kind=F32):
    return jax.ShapeDtypeStruct((rows, cols), kind)


def masked_diag(tile):
    rows_here = lax.broadcasted_iota(jnp.int32, tile.shape, 0)
    cols_here = lax.broadcasted_iota(jnp.int32, tile.shape, 1)
    wide = tile.astype(F32)
    wide = jnp.where(rows_here > cols_here, wide, 0.0)
    return jnp.where(rows_here == cols_here, 1.0, wide).astype(BF16)


def lower_rows(read, rhs, tile_idx):
    lo, hi = tile_idx * TILE, (tile_idx + 1) * TILE
    total = dot(masked_diag(read(lo, hi, lo, hi)), rhs[lo:hi])
    if tile_idx:
        total = total + dot(read(lo, hi, 0, lo), rhs[0:lo])
    return total


def bottom_kernel(piece, inverse, rhs, out, buf, sems):
    steps = piece // TILE
    copies = [
        pltpu.make_async_copy(
            inverse.at[pl.ds(piece + t * TILE, TILE)], buf.at[pl.ds(t * TILE, TILE)], sems.at[t]
        )
        for t in range(steps)
    ]
    for one in copies:
        one.start()
    right = rhs[...]
    for t in range(steps):
        copies[t].wait()
        out[t * TILE : (t + 1) * TILE] = dot(buf[t * TILE : (t + 1) * TILE], right)


def key_of(row, levels, sep_panels):
    slot = row // sep_panels
    zeros = jnp.int32(0)
    for bit_pos in range(1, levels + 1):
        zeros = zeros + jnp.where(slot % 2**bit_pos == 0, 1, 0)
    return jnp.where(zeros == 0, levels - 1, zeros - 1) * sep_panels + row % sep_panels


def diagonal_kernel(piece, levels, sep_panels, inverse, rhs, leaf_rows, sep_rows, out, tags, buf, sems):
    steps = piece // TILE
    start = pl.multiple_of(lax.axis_index("col") * piece, piece)
    copies = [
        pltpu.make_async_copy(
            inverse.at[pl.ds(start + t * TILE, TILE)], buf.at[pl.ds(t * TILE, TILE)], sems.at[t]
        )
        for t in range(steps)
    ]
    for one in copies:
        one.start()
    n_leaf, n_sep = leaf_rows.shape[1], sep_rows.shape[1]
    keys = [key_of(leaf_rows[0, j], levels, sep_panels) for j in range(n_leaf)]
    for j in range(n_leaf):
        rank = jnp.int32(0)
        for i in range(n_leaf):
            if i != j:
                rank = rank + jnp.where(keys[i] < keys[j], 1, 0)
        tags[0, rank] = keys[j]
        tags[0, n_leaf + n_sep + rank] = jnp.int32(j)
    for j in range(n_sep):
        tags[0, n_leaf + j] = key_of(sep_rows[0, j], levels, sep_panels)
    right = rhs[...]
    for t in range(steps):
        copies[t].wait()
        out[t * TILE : (t + 1) * TILE] = lower_rows(lambda a, b, c, d: buf[a:b, c:d], right, t)


def below_kernel(first, j0, j1, order_at, *refs):
    if first:
        diag, other, below, tags, sol, keep, send, buf, sems = refs
    else:
        sol, below, tags, keep, send, buf, sems = refs
    copies = []
    for j in range(j0, j1):
        source = pl.multiple_of(tags[0, order_at + j] * PANEL, PANEL)
        copies.append(
            pltpu.make_async_copy(
                below.at[pl.ds(source, PANEL)], buf.at[pl.ds((j - j0) * PANEL, PANEL)], sems.at[j - j0]
            )
        )
    for one in copies:
        one.start()
    if first:
        sol[...] = (diag[...] + other[...]).astype(BF16)
    right = sol[...]
    half = right.shape[1] // 2
    is_first = lax.axis_index("col") == 0
    for t in range(0, j1 - j0, 2):
        copies[t].wait()
        copies[t + 1].wait()
        both = dot(buf[t * PANEL : (t + 2) * PANEL], right)
        left_half, right_half = both[:, :half], both[:, half:]
        keep[t * PANEL : (t + 2) * PANEL] = jnp.where(is_first, left_half, right_half)
        send[t * PANEL : (t + 2) * PANEL] = jnp.where(is_first, right_half, left_half)


def relay_kernel(chunk, per_chunk, *refs):
    count = chunk + 1
    mine, theirs = refs[:count], refs[count : 2 * count]
    my_tags, their_tags, out = refs[2 * count :]
    out[...] = jnp.zeros_like(out)
    for group, tags in ((mine, my_tags), (theirs, their_tags)):
        for i in range(count * per_chunk):
            place = tags[0, i] - chunk * per_chunk

            @pl.when((place >= 0) & (place < per_chunk))
            def _():
                at = pl.ds(pl.multiple_of(place * PANEL, PANEL), PANEL)
                inside = i % per_chunk
                out[at] += group[i // per_chunk][inside * PANEL : (inside + 1) * PANEL]


def rest_kernel(n_compact, per_array, n_dense, base, *refs):
    arrays = refs[:n_compact]
    tags = refs[n_compact : 2 * n_compact]
    firsts = per_array
    dense = refs[2 * n_compact : 2 * n_compact + n_dense]
    out = refs[-1]
    panels = out.shape[0] // PANEL
    if n_dense:
        out[...] = dense[0][...] + dense[1][...]
    else:
        out[...] = jnp.zeros_like(out)
    for array, tag, (tag_at, count) in zip(arrays, tags, firsts):
        for i in range(count):
            place = tag[0, tag_at + i] - base

            @pl.when((place >= 0) & (place < panels))
            def _():
                at = pl.ds(pl.multiple_of(place * PANEL, PANEL), PANEL)
                out[at] += array[i * PANEL : (i + 1) * PANEL]


def narrow_kernel(wide, out):
    out[...] = wide[...].astype(BF16)


def solve_kernel(plan, *refs):
    refs = list(refs)

    def take(count):
        got = refs[:count]
        del refs[:count]
        return got

    compact = take(plan["n_compact"])
    tags = take(plan["n_compact"])
    dense = take(plan["n_dense"])
    rhs_mine, rhs_theirs, widths, inverse, from_top, from_bottom = take(6)
    below, from_below = take(2) if plan["update"] else (None, None)
    before = take(2) if plan["before"] else None
    keep, send = take(2)
    update = take(1)[0] if plan["update"] else None
    tri, acc, res, sol, sems = take(5)
    if plan["update"]:
        low, low_sems = take(2)
    piece = rhs_mine.shape[0]
    half = rhs_theirs.shape[1]
    is_first = lax.axis_index("col") == 0
    leaf = lax.axis_index("leaf")
    span = 2 ** plan["level"]
    is_owner = leaf % span == span // 2
    steps = piece // TILE

    def fetch(source, row0, buf, at, sem):
        return pltpu.make_async_copy(source.at[pl.ds(row0, TILE)], buf.at[at, pl.ds(row0 % piece, TILE)], sem)

    sources = ((inverse, 0, from_top, 0), (inverse, piece, from_bottom, 0), (from_bottom, 0, inverse, piece))
    for t in range(steps):
        for q, (src0, off0, src1, off1) in enumerate(sources):

            @pl.when(is_first)
            def _():
                fetch(src0, off0 + t * TILE, tri, q, sems.at[q, t]).start()

            @pl.when(jnp.logical_not(is_first))
            def _():
                fetch(src1, off1 + t * TILE, tri, q, sems.at[q, t]).start()

    if plan["update"]:
        low_steps = below.shape[0] // TILE
        for t in range(low_steps):
            for q, (src0, src1) in enumerate(((below, from_below), (from_below, below))):

                @pl.when(is_first)
                def _():
                    fetch(src0, t * TILE, low, q, low_sems.at[q, t]).start()

                @pl.when(jnp.logical_not(is_first))
                def _():
                    fetch(src1, t * TILE, low, q, low_sems.at[q, t]).start()

    @pl.when(is_first)
    def _():
        acc[0:piece] = rhs_mine[:, 0:half].astype(F32)
        acc[piece : 2 * piece] = rhs_theirs[...]

    @pl.when(jnp.logical_not(is_first))
    def _():
        acc[0:piece] = rhs_theirs[...]
        acc[piece : 2 * piece] = rhs_mine[:, half : 2 * half].astype(F32)

    pieces = len(dense) // 2
    at_row = 0
    for d in range(pieces):
        rows = min(dense[d].shape[0], 2 * piece - at_row)
        acc[at_row : at_row + rows] -= dense[d][0:rows] + dense[pieces + d][0:rows]
        at_row += rows
    panels = 2 * piece // PANEL
    for array, tag, (tag_at, count) in zip(compact, tags, plan["firsts"]):
        for i in range(count):
            place = tag[0, tag_at + i] - plan["base"]

            @pl.when((place >= 0) & (place < panels))
            def _():
                at = pl.ds(pl.multiple_of(place * PANEL, PANEL), PANEL)
                acc[at] -= array[i * PANEL : (i + 1) * PANEL]

    res[...] = acc[...].astype(BF16)
    slot = leaf - leaf % span + span // 2
    width = widths[slot]
    row_ids = lax.broadcasted_iota(jnp.int32, (TILE, half), 0)

    def finish(total, row0):
        total = jnp.where(row_ids + row0 < width, total, 0.0)
        acc[row0 : row0 + TILE] = total
        sol[row0 : row0 + TILE] = total.astype(BF16)

    upper, lower = res[0:piece], res[piece : 2 * piece]
    for t in range(steps):
        fetch(inverse, t * TILE, tri, 0, sems.at[0, t]).wait()
        finish(lower_rows(lambda a, b, c, d: tri[0, a:b, c:d], upper, t), t * TILE)
    for t in range(steps):
        fetch(inverse, t * TILE, tri, 1, sems.at[1, t]).wait()
        fetch(inverse, t * TILE, tri, 2, sems.at[2, t]).wait()
        total = lower_rows(lambda a, b, c, d: tri[2, a:b, c:d], lower, t)
        total = total + dot(tri[1, t * TILE : (t + 1) * TILE], upper)
        finish(total, piece + t * TILE)
    if plan["update"]:
        upper, lower = sol[0:piece], sol[piece : 2 * piece]
        for t in range(low_steps):
            fetch(below, t * TILE, low, 0, low_sems.at[0, t]).wait()
            fetch(below, t * TILE, low, 1, low_sems.at[1, t]).wait()
            at = slice(t * TILE, (t + 1) * TILE)
            update[at] = dot(low[0, at], upper) + dot(low[1, at], lower)
    kept_at = pl.ds(pl.multiple_of(lax.axis_index("col") * piece, piece), piece)
    sent_at = pl.ds(pl.multiple_of((1 - lax.axis_index("col")) * piece, piece), piece)

    @pl.when(is_owner)
    def _():
        keep[...] = acc[kept_at]
        send[...] = acc[sent_at]

    @pl.when(jnp.logical_not(is_owner))
    def _():
        if before is None:
            keep[...] = jnp.zeros_like(keep)
            send[...] = jnp.zeros_like(send)
        else:
            keep[...] = before[0][...]
            send[...] = before[1][...]


def join_kernel(keep, other, out):
    half = keep.shape[1]
    is_first = lax.axis_index("col") == 0

    @pl.when(is_first)
    def _():
        out[:, 0:half] = keep[...].astype(BF16)
        out[:, half : 2 * half] = other[...].astype(BF16)

    @pl.when(jnp.logical_not(is_first))
    def _():
        out[:, 0:half] = other[...].astype(BF16)
        out[:, half : 2 * half] = keep[...].astype(BF16)


def on_device(
    leaf_rhs, leaf_inverse, leaf_below, leaf_rows, sep_rhs, sep_inverse, sep_below, sep_rows, sep_width
):
    leaves = lax.axis_size("leaf")
    levels = leaves.bit_length() - 1
    piece, width_rhs = leaf_rhs.shape
    half = width_rhs // 2
    sep_cols = sep_inverse.shape[0]
    sep_piece = sep_inverse.shape[1]
    sep_panels = sep_cols // PANEL
    n_leaf, n_sep = leaf_rows.shape[1], sep_rows.shape[1]
    col = lax.axis_index("col")
    swap = [(0, 1), (1, 0)]

    steps = piece // TILE
    weights = 2 * piece * piece
    bottom = call(
        functools.partial(bottom_kernel, piece),
        (leaf_inverse, leaf_rhs),
        [ANY, VMEM],
        shape(piece, width_rhs),
        VMEM,
        [pltpu.VMEM((piece, piece), BF16), pltpu.SemaphoreType.DMA((steps,))],
        weights * width_rhs,
        weights,
    )
    from_left = lax.ppermute(bottom, "col", [(0, 1)])
    diag, tags = call(
        functools.partial(diagonal_kernel, piece, levels, sep_panels),
        (leaf_inverse, leaf_rhs, leaf_rows, sep_rows),
        [ANY, VMEM, SMEM, SMEM],
        (shape(piece, width_rhs), shape(1, TAGS, jnp.int32)),
        (VMEM, SMEM),
        [pltpu.VMEM((piece, piece), BF16), pltpu.SemaphoreType.DMA((steps,))],
        weights * width_rhs,
        weights,
    )

    per_chunk = 4
    n_chunks = n_leaf // per_chunk
    order_at = n_leaf + n_sep

    def below(first, j0, j1, ins):
        rows = (j1 - j0) * PANEL
        outs = (shape(rows, half), shape(rows, half))
        specs = [VMEM, VMEM, ANY, SMEM] if first else [VMEM, ANY, SMEM]
        if first:
            outs = (shape(piece, width_rhs, BF16),) + outs
        return call(
            functools.partial(below_kernel, first, j0, j1, order_at),
            ins,
            specs,
            outs,
            (VMEM,) * len(outs),
            [pltpu.VMEM((rows, piece), BF16), pltpu.SemaphoreType.DMA((j1 - j0,))],
            2 * rows * piece * width_rhs,
            2 * rows * piece,
        )

    leaf_solution, keep0, send0 = below(True, 0, per_chunk, (diag, from_left, leaf_below, tags))
    mine = [keep0 + lax.ppermute(send0, "col", swap)]
    keep1, send1 = below(False, per_chunk, n_leaf, (leaf_solution, leaf_below, tags))
    got1 = lax.ppermute(send1, "col", swap)
    for chunk in range(1, n_chunks):
        at = slice((chunk - 1) * per_chunk * PANEL, chunk * per_chunk * PANEL)
        mine.append(keep1[at] + got1[at])

    up = [(i, i + 1) for i in range(0, leaves, 2)]
    their_tags = lax.ppermute(tags, "leaf", up)
    theirs = [lax.ppermute(one, "leaf", up) for one in mine]

    rhs_out = jnp.where(col == 0, sep_rhs[:, half:], sep_rhs[:, :half]).astype(F32)
    rhs_theirs = lax.ppermute(rhs_out, "col", swap)

    def narrow(wide):
        return call(narrow_kernel, (wide,), [VMEM], shape(*wide.shape, BF16), VMEM, (), 0, 6 * wide.size)

    from_bottom = narrow(lax.ppermute(sep_inverse[sep_piece:].astype(F32), "col", swap))
    from_top = narrow(lax.ppermute(sep_inverse[:sep_piece].astype(F32), "col", [(0, 1)]))
    from_below = narrow(lax.ppermute(sep_below.astype(F32), "col", swap))

    dense = []
    for chunk in range(n_chunks):
        dense.append(
            call(
                functools.partial(relay_kernel, chunk, per_chunk),
                (*mine[: chunk + 1], *theirs[: chunk + 1], tags, their_tags),
                [VMEM] * (2 * chunk + 2) + [SMEM] * 2,
                shape(per_chunk * PANEL, half),
                VMEM,
                (),
                0,
                3 * per_chunk * PANEL * half * 4,
            )
        )
    chunk_firsts = [(c * per_chunk, per_chunk) for c in range(n_chunks)] * 2

    def rest(base, arrays, tag_list, firsts, parts):
        rows = (levels - 1) * sep_cols - base * PANEL
        if not rows:
            return None
        return call(
            functools.partial(rest_kernel, len(arrays), firsts, len(parts), base),
            (*arrays, *tag_list, *parts),
            [VMEM] * len(arrays) + [SMEM] * len(tag_list) + [VMEM] * len(parts),
            shape(rows, half),
            VMEM,
        )

    def solve(level, arrays, tag_list, firsts, parts, base, before):
        update = level < levels
        plan = dict(
            level=level,
            n_compact=len(arrays),
            n_dense=len(parts),
            firsts=firsts,
            base=base,
            update=update,
            before=before is not None,
        )
        ins = [*arrays, *tag_list, *parts, sep_rhs, rhs_theirs, sep_width, sep_inverse, from_top, from_bottom]
        specs = [VMEM] * len(arrays) + [SMEM] * len(tag_list) + [VMEM] * (len(parts) + 2) + [SMEM] + [ANY] * 3
        outs = [shape(sep_piece, half), shape(sep_piece, half)]
        scratch = [
            pltpu.VMEM((3, sep_piece, sep_piece), BF16),
            pltpu.VMEM((sep_cols, half), F32),
            pltpu.VMEM((sep_cols, half), BF16),
            pltpu.VMEM((sep_cols, half), BF16),
            pltpu.SemaphoreType.DMA((3, sep_piece // TILE)),
        ]
        if update:
            ins += [sep_below, from_below]
            specs += [ANY] * 2
            outs.append(shape(sep_below.shape[0], half))
            scratch += [
                pltpu.VMEM((2, sep_below.shape[0], sep_piece), BF16),
                pltpu.SemaphoreType.DMA((2, sep_below.shape[0] // TILE)),
            ]
        if before is not None:
            ins += list(before)
            specs += [VMEM] * 2
        got = call(
            functools.partial(solve_kernel, plan),
            ins,
            specs,
            tuple(outs),
            (VMEM,) * len(outs),
            scratch,
            2 * sep_cols * sep_cols * half,
            2 * sep_cols * sep_cols,
        )
        return got[:2], got[2] if update else None

    compact, compact_tags = mine + theirs, [tags] * n_chunks + [their_tags] * n_chunks
    held, update = solve(
        1, compact, compact_tags, chunk_firsts, [], (levels - 1) * sep_panels, None
    )
    above = rest(sep_panels, compact, compact_tags, chunk_firsts, [])
    for level in range(2, levels + 1):
        span = 2**level
        owners = range(span // 2, leaves, span)
        step = span // 4
        lists = [[(a - step, a) for a in owners], [(a + step, a) for a in owners]]
        parts = dense + ([above] if above is not None else [])
        came = [[lax.ppermute(one, "leaf", pairs) for one in parts] for pairs in lists]
        came_tags = [lax.ppermute(tags, "leaf", pairs) for pairs in lists]
        came_update = [lax.ppermute(update, "leaf", pairs) for pairs in lists]
        firsts = [(n_leaf, n_sep)] * 2
        head = [one[: len(dense)] for one in came]
        base = (level - 2) * sep_panels
        held, update = solve(level, came_update, came_tags, firsts, head[0] + head[1], base, held)
        if level < levels:
            tails = [one[-1] for one in came]
            above = rest((level - 1) * sep_panels, came_update, came_tags, firsts, tails)
            dense, above = [above[:sep_cols]], above[sep_cols:] if level < levels - 1 else None
    other = lax.ppermute(held[1], "col", swap)
    sep_solution = call(join_kernel, (held[0], other), [VMEM] * 2, shape(sep_piece, width_rhs, BF16), VMEM)
    return leaf_solution, sep_solution


def solution(mesh):
    placed = (
        P(("leaf", "col"), "row"),
        P("leaf", "col"),
        P("leaf", "col"),
        P("leaf", None),
        P(("leaf", "col"), "row"),
        P("leaf", "col"),
        P("leaf", "col"),
        P("leaf", None),
        P(),
    )
    return jax.shard_map(
        on_device,
        mesh=mesh,
        in_specs=placed,
        out_specs=(P(("leaf", "col"), "row"), P(("leaf", "col"), "row")),
        check_vma=False,
    )
```

time: 223 us -> 136 us (0.61)
  waiting for transfers between devices: 149 us -> 45.5 us
  starting transfers between devices: 3.12 us -> 42.4 us
  Pallas kernels: 0 us -> 33.5 us
  matrix products: 25.1 us -> 0 us
  between operations: 13.9 us -> 1.08 us
  local copies, waits for them, and re-layouts: 13.7 us -> 2.08 us
  other arithmetic: 16.4 us -> 10.3 us
    reduce_scatter x5 -> x0, waiting for transfers between devices: 57.6 us -> none  [the longest x2 24.7 us: sep_product(): lax.psum_scatter(jnp.dot(masked, right_side, preferred_element_type=jnp.f...]
    ppermute x3 -> x25, waiting for transfers between devices: 91.4 us -> 45.5 us  [the longest x8 25.1 us: on_device(): lax.ppermute(one, 'leaf', pairs)]
    ppermute x3 -> x25, starting transfers between devices: 2.73 us -> 42.4 us  [the longest x4 12.2 us: on_device(): theirs = [lax.ppermute(one, 'leaf', up) for one in mine]]
    pallas_call x0 -> x14, Pallas kernels: none -> 33.5 us  [call(): pl.pallas_call(body, out_shape=outs, in_specs=specs, out_specs=out_specs,...]
    dot_general x5 -> x0, matrix products: 25.1 us -> none  [the longest x2 12.1 us: sep_product(): jnp.dot(masked, right_side, preferred_element_type=jnp.float32)]
    scatter-add x2 -> x0, other arithmetic: 9.09 us -> none  [the longest x1 5.35 us: on_device(): pending.at[local_panels(leaf_rows[0], levels, sep_panels)].add(leaf_term)]
    convert_element_type x1 -> x3, other arithmetic: 1.28 us -> 9.35 us  [the longest x1 6.82 us: on_device(): sep_inverse[sep_piece:].astype(F32)]
    slice x2 -> x0, local copies, waits for them, and re-layouts: 6.21 us -> none  [on_device(): pending[(level_now - 1) * sep_panels:level_now * sep_panels]]
  transfers between devices with their start and end apart: 8 -> 25, of which waited for: 8 -> 12; matrix products, arithmetic and copies ran while one was open for 1% -> 3% of each run, Pallas kernels for 0% -> 21%
where the time goes in v1:
time: 136 us; the launch traced here: 135 us
  waiting for transfers between devices  45.5 us (33%)
  starting transfers between devices  42.4 us (31%)
  Pallas kernels  33.5 us (25%)
  other arithmetic  10.3 us (8%)
  local copies, waits for them, and re-layouts  2.08 us (2%)
    pallas_call x14, Pallas kernels, call(): pl.pallas_call(body, out_shape=outs, in_specs=specs, out_specs=out_specs,...  33.5 us
    ppermute x8, waiting for transfers between devices, on_device(): lax.ppermute(one, 'leaf', pairs)  25.1 us
    ppermute x4, starting transfers between devices, on_device(): theirs = [lax.ppermute(one, 'leaf', up) for one in mine]  12.2 us
    ppermute x4, waiting for transfers between devices, on_device(): theirs = [lax.ppermute(one, 'leaf', up) for one in mine]  11.6 us
    ppermute x8, starting transfers between devices, on_device(): lax.ppermute(one, 'leaf', pairs)  10.3 us
    convert_element_type x1, other arithmetic, on_device(): sep_inverse[sep_piece:].astype(F32)  6.82 us
    ppermute x1, waiting for transfers between devices, on_device(): from_left = lax.ppermute(bottom, 'col', [(0, 1)])  5.14 us
    ppermute x1, starting transfers between devices, on_device(): other = lax.ppermute(held[1], 'col', swap)  3.32 us
  transfers between devices with their start and end apart: 25, of which 12 were waited for; matrix products, arithmetic and copies ran while one was open for 3% of the time, Pallas kernels for 21%

profile of v1, /device:TPU:21, one launch (start us, length us, event | category | flops | bytes accessed | tf_op | source)
XLA Modules:
  0.0 134.8 jit_solution(16916414397213441437)
XLA Ops:
  0.6 6.8 %slice_convert_fusion = (f32[1024,1024]{1,0:T(8,128)}, f32[1024,1024]{1,0:T(8,128)}) fusion(bf16[2048,1024]{1,0:T(8,128)(2,1)} %refs_15_.1), kind=kLoop, calls=%fused_computation | loop fusion | flops 2097152 | bytes 12582912 | tf_op jit(solution)/shard_map/convert_element_type | solution.py:396
  7.5 1.5 %collective-permute-start.9 = (f32[1024,1024]{1,0:T(8,128)}, f32[1024,1024]{1,0:T(8,128)}, u32[]{:S(2)}, u32[]{:S(2)}) collective-permute-start(f32[1024,1024]{1,0:T(8,128)} %get-tuple-element.27), channel_id=1, source_target_pairs={{0,1},{2,3},{4,5},{6,7},{8,9},{10,11},{12,13},{14,15},{16,17},{18,... | collective-permute-start | bytes 12582920 | tf_op jit(solution)/shard_map/ppermute | solution.py:397
  9.0 3.3 %collective-permute-start.10 = (f32[1024,1024]{1,0:T(8,128)}, f32[1024,1024]{1,0:T(8,128)}, u32[]{:S(2)}, u32[]{:S(2)}) collective-permute-start(f32[1024,1024]{1,0:T(8,128)} %get-tuple-element.26), channel_id=1, source_target_pairs={{0,1},{1,0},{2,3},{3,2},{4,5},{5,4},{6,7},{7,6},{8,9},{9,8},{10,11... | collective-permute-start | bytes 12582920 | tf_op jit(solution)/shard_map/ppermute | solution.py:396
  12.3 2.5 %convert_element_type.15 = f32[1024,1024]{1,0:T(8,128)} convert(bf16[1024,1024]{1,0:T(8,128)(2,1)S(1)} %copy-done.2) | non-fusion elementwise | flops 1048576 | bytes 6291456 | tf_op jit(solution)/shard_map/convert_element_type | solution.py:398
  14.8 1.9 %shard_map.105 = f32[1024,256]{1,0:T(8,128)S(1)} custom-call(bf16[2048,1024]{1,0:T(8,128)(2,1)S(1)} %copy-done, bf16[1024,256]{1,0:T(8,128)(2,1)S(1)} %copy-done.7), custom_call_target="tpu_custom_call" | custom-call | flops 536870912 | bytes 2097152 | tf_op jit(solution)/shard_map/pallas_call | solution.py:25
  16.7 1.3 collective-permute-start
  18.0 2.7 %shard_map.104 = (f32[1024,256]{1,0:T(8,128)S(1)}, s32[1,128]{1,0:T(1,128)S(1)}) custom-call(bf16[2048,1024]{1,0:T(8,128)(2,1)S(1)} %copy-done, bf16[1024,256]{1,0:T(8,128)(2,1)S(1)} %copy-done.7, s32[1,16]{1,0:T(1,128)S(1)} %copy-done.10, s32[1,8]{1,0:T(1,128)S(1)} %copy-done.11), custom_call_target="tpu_custom_call" | custom-call | flops 536870912 | bytes 2097152 | tf_op jit(solution)/shard_map/pallas_call | solution.py:25
  20.8 5.1 %collective-permute-done.refs_1_ = f32[1024,256]{1,0:T(8,128)S(1)} collective-permute-done((f32[1024,256]{1,0:T(8,128)S(1)}, f32[1024,256]{1,0:T(8,128)S(1)}, u32[]{:S(2)}, u32[]{:S(2)}) %collective-permute-start) | collective-permute-done | bytes 1048608 | tf_op jit(solution)/shard_map/ppermute | solution.py:345
  25.9 2.0 %shard_map.106 = (bf16[1024,256]{1,0:T(8,128)(2,1)}, f32[512,128]{1,0:T(8,128)S(1)}, f32[512,128]{1,0:T(8,128)S(1)}) custom-call(f32[1024,256]{1,0:T(8,128)S(1)} %get-tuple-element.14.refs_0_, f32[1024,256]{1,0:T(8,128)S(1)} %collective-permute-done.refs_1_, bf16[2048,1024]{1,0:T(8,128)(2,1)S(1)} %copy-done.1, ...), custom_call_target="tpu_custom_call" | custom-call | flops 268435456 | bytes 1048576 | tf_op jit(solution)/shard_map/pallas_call | solution.py:25
  29.0 3.4 %shard_map.107 = (f32[1536,128]{1,0:T(8,128)S(1)}, f32[1536,128]{1,0:T(8,128)S(1)}) custom-call(bf16[1024,256]{1,0:T(8,128)(2,1)S(1)} %copy-done.8, bf16[2048,1024]{1,0:T(8,128)(2,1)S(1)} %copy-done.1, s32[1,128]{1,0:T(1,128)S(1)} %get-tuple-element.15.refs_3_.refs_2_.refs_8_.refs_9_.refs_10_.refs_11_.refs_4_.refs_6_), custom_call_target="tpu_custom_call" | custom-call | flops 805306368 | bytes 3145728 | tf_op jit(solution)/shard_map/pallas_call | solution.py:25
  33.1 2.1 %collective-permute-done.1 = f32[512,128]{1,0:T(8,128)S(1)} collective-permute-done((f32[512,128]{1,0:T(8,128)S(1)}, f32[512,128]{1,0:T(8,128)S(1)}, u32[]{:S(2)}, u32[]{:S(2)}) %collective-permute-start.1) | collective-permute-done | bytes 262176 | tf_op jit(solution)/shard_map/ppermute | solution.py:379
  35.2 3.2 %collective-permute-start.7 = (s32[1,128]{1,0:T(1,128)S(1)}, s32[1,128]{1,0:T(1,128)S(1)}, u32[]{:S(2)}, u32[]{:S(2)}) collective-permute-start(s32[1,128]{1,0:T(1,128)S(1)} %get-tuple-element.15.refs_3_.refs_2_.refs_8_.refs_9_.refs_10_.refs_11_.refs_4_.refs_6_), channel_id=1, source_target_pairs={{0,8},{16,24},{1,9},{17,25},{2,10},{18,26},{3,11},{19,27},{4,12},{... | collective-permute-start | bytes 1544 | tf_op jit(solution)/shard_map/ppermute | solution.py:387
  38.5 1.3 collective-permute-start.3
  40.7 2.8 %collective-permute-start.4 = (f32[512,128]{1,0:T(8,128)S(1)}, f32[512,128]{1,0:T(8,128)}, u32[]{:S(2)}, u32[]{:S(2)}) collective-permute-start(f32[512,128]{1,0:T(8,128)S(1)} %get-tuple-element.30.refs_1_), channel_id=1, source_target_pairs={{0,8},{16,24},{1,9},{17,25},{2,10},{18,26},{3,11},{19,27},{4,12},{... | collective-permute-start | bytes 786440 | tf_op jit(solution)/shard_map/ppermute | solution.py:388
  43.4 1.9 %collective-permute-done.3.refs_4_.refs_1_.refs_2_.refs_3_ = f32[512,128]{1,0:T(8,128)S(1)} collective-permute-done((f32[512,128]{1,0:T(8,128)S(1)}, f32[512,128]{1,0:T(8,128)S(1)}, u32[]{:S(2)}, u32[]{:S(2)}) %collective-permute-start.3) | collective-permute-done | bytes 262176 | tf_op jit(solution)/shard_map/ppermute | solution.py:388
  45.3 4.1 %collective-permute-start.5 = (f32[512,128]{1,0:T(8,128)}, f32[512,128]{1,0:T(8,128)S(1)}, u32[]{:S(2)}, u32[]{:S(2)}) collective-permute-start(f32[512,128]{1,0:T(8,128)} %get-tuple-element.29.refs_2_), channel_id=1, source_target_pairs={{0,8},{16,24},{1,9},{17,25},{2,10},{18,26},{3,11},{19,27},{4,12},{... | collective-permute-start | bytes 786440 | tf_op jit(solution)/shard_map/ppermute | solution.py:388
  49.5 1.4 %collective-permute-done.4.refs_5_.refs_3_.refs_4_ = f32[512,128]{1,0:T(8,128)} collective-permute-done((f32[512,128]{1,0:T(8,128)S(1)}, f32[512,128]{1,0:T(8,128)}, u32[]{:S(2)}, u32[]{:S(2)}) %collective-permute-start.4) | collective-permute-done | bytes 262176 | tf_op jit(solution)/shard_map/ppermute | solution.py:388
  50.9 1.5 %collective-permute-start.8 = (f32[1024,128]{1,0:T(8,128)S(1)}, f32[1024,128]{1,0:T(8,128)S(1)}, u32[]{:S(2)}, u32[]{:S(2)}) collective-permute-start(f32[1024,128]{1,0:T(8,128)S(1)} %select_convert_fusion), channel_id=1, source_target_pairs={{0,1},{1,0},{2,3},{3,2},{4,5},{5,4},{6,7},{7,6},{8,9},{9,8},{10,11... | collective-permute-start | bytes 1572872 | tf_op jit(solution)/shard_map/ppermute | solution.py:391
  52.4 4.1 %collective-permute-done.5.refs_6_.refs_5_ = f32[512,128]{1,0:T(8,128)S(1)} collective-permute-done((f32[512,128]{1,0:T(8,128)}, f32[512,128]{1,0:T(8,128)S(1)}, u32[]{:S(2)}, u32[]{:S(2)}) %collective-permute-start.5) | collective-permute-done | bytes 262176 | tf_op jit(solution)/shard_map/ppermute | solution.py:388
  56.5 4.0 %collective-permute-start.6 = (f32[512,128]{1,0:T(8,128)}, f32[512,128]{1,0:T(8,128)S(1)}, u32[]{:S(2)}, u32[]{:S(2)}) collective-permute-start(f32[512,128]{1,0:T(8,128)} %get-tuple-element.28.refs_3_), channel_id=1, source_target_pairs={{0,8},{16,24},{1,9},{17,25},{2,10},{18,26},{3,11},{19,27},{4,12},{... | collective-permute-start | bytes 786440 | tf_op jit(solution)/shard_map/ppermute | solution.py:388
  61.2 4.2 %collective-permute-done.6.refs_7_ = f32[512,128]{1,0:T(8,128)S(1)} collective-permute-done((f32[512,128]{1,0:T(8,128)}, f32[512,128]{1,0:T(8,128)S(1)}, u32[]{:S(2)}, u32[]{:S(2)}) %collective-permute-start.6) | collective-permute-done | bytes 262176 | tf_op jit(solution)/shard_map/ppermute | solution.py:388
  65.4 1.3 collective-permute-start.16
  66.7 1.3 collective-permute-start.20
  68.0 1.1 shard_map.113
  70.1 1.2 shard_map.114
  71.3 1.3 shard_map.115
  72.6 2.4 %shard_map.108.refs_20_.refs_16_ = bf16[1024,1024]{1,0:T(8,128)(2,1)S(1)} custom-call(f32[1024,1024]{1,0:T(8,128)} %collective-permute-done.9.wide), custom_call_target="tpu_custom_call" | custom-call | bytes 6291456 | tf_op jit(solution)/shard_map/pallas_call | solution.py:25
  75.0 1.3 collective-permute-start.14
  76.3 2.4 %shard_map.109.refs_21_.refs_17_ = bf16[1024,1024]{1,0:T(8,128)(2,1)S(1)} custom-call(f32[1024,1024]{1,0:T(8,128)} %collective-permute-done.10.wide), custom_call_target="tpu_custom_call" | custom-call | bytes 6291456 | tf_op jit(solution)/shard_map/pallas_call | solution.py:25
  78.7 1.3 collective-permute-start.15
  80.0 2.4 %shard_map.110.refs_23_ = bf16[1024,1024]{1,0:T(8,128)(2,1)S(1)} custom-call(f32[1024,1024]{1,0:T(8,128)} %collective-permute-done.11.wide), custom_call_target="tpu_custom_call" | custom-call | bytes 6291456 | tf_op jit(solution)/shard_map/pallas_call | solution.py:25
  82.4 1.3 collective-permute-start.17
  83.7 7.0 %shard_map.111 = (f32[1024,128]{1,0:T(8,128)S(1)}, f32[1024,128]{1,0:T(8,128)S(1)}, f32[1024,128]{1,0:T(8,128)S(1)}) custom-call(f32[512,128]{1,0:T(8,128)S(1)} %add.12.refs_0_, f32[512,128]{1,0:T(8,128)S(1)} %get-tuple-element.30.refs_1_, f32[512,128]{1,0:T(8,128)S(1)} %copy-done.5, f32[512,128]{1,0:T(8,128)S(1)} %copy-done.6, ...), custom_call_target="tpu_custom_call" | custom-call | flops 1073741824 | bytes 8388608 | tf_op jit(solution)/shard_map/pallas_call | solution.py:25
  90.7 1.3 collective-permute-start.18
  92.0 1.3 collective-permute-start.19
  93.3 1.3 collective-permute-start.12
  94.6 1.3 collective-permute-start.13
  96.0 1.3 collective-permute-start.21
  97.3 1.3 collective-permute-done.18.refs_6_
  98.5 1.3 collective-permute-start.22
  99.8 4.3 %collective-permute-done.19.refs_7_ = f32[512,128]{1,0:T(8,128)S(1)} collective-permute-done((f32[512,128]{1,0:T(8,128)S(1)}, f32[512,128]{1,0:T(8,128)S(1)}, u32[]{:S(2)}, u32[]{:S(2)}) %collective-permute-start.19) | collective-permute-done | bytes 262176 | tf_op jit(solution)/shard_map/ppermute | solution.py:483
  104.1 1.3 collective-permute-start.23
  105.4 8.2 %collective-permute-done.21.refs_9_ = f32[512,128]{1,0:T(8,128)S(1)} collective-permute-done((f32[512,128]{1,0:T(8,128)S(1)}, f32[512,128]{1,0:T(8,128)S(1)}, u32[]{:S(2)}, u32[]{:S(2)}) %collective-permute-start.21) | collective-permute-done | bytes 262176 | tf_op jit(solution)/shard_map/ppermute | solution.py:483
  113.7 5.6 %collective-permute-done.22.refs_10_ = f32[512,128]{1,0:T(8,128)S(1)} collective-permute-done((f32[512,128]{1,0:T(8,128)S(1)}, f32[512,128]{1,0:T(8,128)S(1)}, u32[]{:S(2)}, u32[]{:S(2)}) %collective-permute-start.22) | collective-permute-done | bytes 262176 | tf_op jit(solution)/shard_map/ppermute | solution.py:483
  119.3 5.6 %collective-permute-done.23.refs_11_ = f32[512,128]{1,0:T(8,128)S(1)} collective-permute-done((f32[512,128]{1,0:T(8,128)S(1)}, f32[512,128]{1,0:T(8,128)S(1)}, u32[]{:S(2)}, u32[]{:S(2)}) %collective-permute-start.23) | collective-permute-done | bytes 262176 | tf_op jit(solution)/shard_map/ppermute | solution.py:483
  124.9 4.2 %shard_map.116 = (f32[1024,128]{1,0:T(8,128)S(1)}, f32[1024,128]{1,0:T(8,128)S(1)}) custom-call(f32[1024,128]{1,0:T(8,128)S(1)} %collective-permute-done.12.refs_0_, f32[1024,128]{1,0:T(8,128)S(1)} %collective-permute-done.13.refs_1_, s32[1,128]{1,0:T(1,128)S(1)} %collective-permute-done.14.refs_2_, s32[1,128]{1,0:T(1,128)S(1)} %collective-permute-done.15.refs_3_, ...), custom_call_target="tpu_custom_call" | custom-call | flops 1073741824 | bytes 8388608 | tf_op jit(solution)/shard_map/pallas_call | solution.py:25
  129.1 3.3 %collective-permute-start.24 = (f32[1024,128]{1,0:T(8,128)S(1)}, f32[1024,128]{1,0:T(8,128)S(1)}, u32[]{:S(2)}, u32[]{:S(2)}) collective-permute-start(f32[1024,128]{1,0:T(8,128)S(1)} %get-tuple-element.25), channel_id=1, source_target_pairs={{0,1},{1,0},{2,3},{3,2},{4,5},{5,4},{6,7},{7,6},{8,9},{9,8},{10,11... | collective-permute-start | bytes 1572872 | tf_op jit(solution)/shard_map/ppermute | solution.py:494
  132.4 1.5 %collective-permute-done.24.other = f32[1024,128]{1,0:T(8,128)S(1)} collective-permute-done((f32[1024,128]{1,0:T(8,128)S(1)}, f32[1024,128]{1,0:T(8,128)S(1)}, u32[]{:S(2)}, u32[]{:S(2)}) %collective-permute-start.24) | collective-permute-done | bytes 524320 | tf_op jit(solution)/shard_map/ppermute | solution.py:494
  (45 shorter events, 5.2 us)
Async XLA Ops:
  0.6 11.7 %copy-start.2 = (bf16[1024,1024]{1,0:T(8,128)(2,1)S(1)}, bf16[1024,1024]{1,0:T(8,128)(2,1)}, u32[]{:S(2)}) copy-start(bf16[1024,1024]{1,0:T(8,128)(2,1)} %refs_22_.1) | copy-start | bytes 6291460
  7.5 7.4 %copy-start = (bf16[2048,1024]{1,0:T(8,128)(2,1)S(1)}, bf16[2048,1024]{1,0:T(8,128)(2,1)}, u32[]{:S(2)}) copy-start(bf16[2048,1024]{1,0:T(8,128)(2,1)} %inverse.3) | copy-start | bytes 12582916
  7.5 7.4 %copy-start.7 = (bf16[1024,256]{1,0:T(8,128)(2,1)S(1)}, bf16[1024,256]{1,0:T(8,128)(2,1)}, u32[]{:S(2)}) copy-start(bf16[1024,256]{1,0:T(8,128)(2,1)} %rhs.3) | copy-start | bytes 1572868
  7.5 59.2 %collective-permute-start.9 = (f32[1024,1024]{1,0:T(8,128)}, f32[1024,1024]{1,0:T(8,128)}, u32[]{:S(2)}, u32[]{:S(2)}) collective-permute-start(f32[1024,1024]{1,0:T(8,128)} %get-tuple-element.27), channel_id=1, source_target_pairs={{0,1},{2,3},{4,5},{6,7},{8,9},{10,11},{12,13},{14,15},{16,17},{18,... | collective-permute-start | bytes 12582920 | tf_op jit(solution)/shard_map/ppermute | solution.py:397
  9.0 66.0 %collective-permute-start.10 = (f32[1024,1024]{1,0:T(8,128)}, f32[1024,1024]{1,0:T(8,128)}, u32[]{:S(2)}, u32[]{:S(2)}) collective-permute-start(f32[1024,1024]{1,0:T(8,128)} %get-tuple-element.26), channel_id=1, source_target_pairs={{0,1},{1,0},{2,3},{3,2},{4,5},{5,4},{6,7},{7,6},{8,9},{9,8},{10,11... | collective-permute-start | bytes 12582920 | tf_op jit(solution)/shard_map/ppermute | solution.py:396
  14.8 3.2 %copy-start.10 = (s32[1,16]{1,0:T(1,128)S(1)}, s32[1,16]{1,0:T(1,128)}, u32[]{:S(2)}) copy-start(s32[1,16]{1,0:T(1,128)} %leaf_rows.1) | copy-start | bytes 196
  14.8 3.2 %copy-start.11 = (s32[1,8]{1,0:T(1,128)S(1)}, s32[1,8]{1,0:T(1,128)}, u32[]{:S(2)}) copy-start(s32[1,8]{1,0:T(1,128)} %sep_rows.1) | copy-start | bytes 100
  14.8 11.1 %copy-start.1 = (bf16[2048,1024]{1,0:T(8,128)(2,1)S(1)}, bf16[2048,1024]{1,0:T(8,128)(2,1)}, u32[]{:S(2)}) copy-start(bf16[2048,1024]{1,0:T(8,128)(2,1)} %refs_1_.1) | copy-start | bytes 12582916
  14.8 63.9 %collective-permute-start.11 = (f32[1024,1024]{1,0:T(8,128)}, f32[1024,1024]{1,0:T(8,128)}, u32[]{:S(2)}, u32[]{:S(2)}) collective-permute-start(f32[1024,1024]{1,0:T(8,128)} %convert_element_type.15), channel_id=1, source_target_pairs={{0,1},{1,0},{2,3},{3,2},{4,5},{5,4},{6,7},{7,6},{8,9},{9,8},{10,11... | collective-permute-start | bytes 12582920 | tf_op jit(solution)/shard_map/ppermute | solution.py:398
  16.7 9.2 %collective-permute-start = (f32[1024,256]{1,0:T(8,128)S(1)}, f32[1024,256]{1,0:T(8,128)S(1)}, u32[]{:S(2)}, u32[]{:S(2)}) collective-permute-start(f32[1024,256]{1,0:T(8,128)S(1)} %shard_map.105), channel_id=1, source_target_pairs={{0,1},{2,3},{4,5},{6,7},{8,9},{10,11},{12,13},{14,15},{16,17},{18,... | collective-permute-start | bytes 3145736 | tf_op jit(solution)/shard_map/ppermute | solution.py:345
  27.9 21.5 %copy-start.3 = (bf16[1024,256]{1,0:T(8,128)(2,1)S(1)}, bf16[1024,256]{1,0:T(8,128)(2,1)}, u32[]{:S(2)}) copy-start(bf16[1024,256]{1,0:T(8,128)(2,1)} %refs_12_.1) | copy-start | bytes 1572868
  27.9 1.1 copy-start.8
  32.5 6.0 %collective-permute-start.2 = (f32[1536,128]{1,0:T(8,128)S(1)}, f32[1536,128]{1,0:T(8,128)S(1)}, u32[]{:S(2)}, u32[]{:S(2)}) collective-permute-start(f32[1536,128]{1,0:T(8,128)S(1)} %get-tuple-element.20), channel_id=1, source_target_pairs={{0,1},{1,0},{2,3},{3,2},{4,5},{5,4},{6,7},{7,6},{8,9},{9,8},{10,11... | collective-permute-start | bytes 2359304 | tf_op jit(solution)/shard_map/ppermute | solution.py:381
  32.7 2.5 %collective-permute-start.1 = (f32[512,128]{1,0:T(8,128)S(1)}, f32[512,128]{1,0:T(8,128)S(1)}, u32[]{:S(2)}, u32[]{:S(2)}) collective-permute-start(f32[512,128]{1,0:T(8,128)S(1)} %get-tuple-element.18), channel_id=1, source_target_pairs={{0,1},{1,0},{2,3},{3,2},{4,5},{5,4},{6,7},{7,6},{8,9},{9,8},{10,11... | collective-permute-start | bytes 786440 | tf_op jit(solution)/shard_map/ppermute | solution.py:379
  35.2 5.4 %collective-permute-start.7 = (s32[1,128]{1,0:T(1,128)S(1)}, s32[1,128]{1,0:T(1,128)S(1)}, u32[]{:S(2)}, u32[]{:S(2)}) collective-permute-start(s32[1,128]{1,0:T(1,128)S(1)} %get-tuple-element.15.refs_3_.refs_2_.refs_8_.refs_9_.refs_10_.refs_11_.refs_4_.refs_6_), channel_id=1, source_target_pairs={{0,8},{16,24},{1,9},{17,25},{2,10},{18,26},{3,11},{19,27},{4,12},{... | collective-permute-start | bytes 1544 | tf_op jit(solution)/shard_map/ppermute | solution.py:387
  38.5 6.8 %collective-permute-start.3 = (f32[512,128]{1,0:T(8,128)S(1)}, f32[512,128]{1,0:T(8,128)S(1)}, u32[]{:S(2)}, u32[]{:S(2)}) collective-permute-start(f32[512,128]{1,0:T(8,128)S(1)} %add.12.refs_0_), channel_id=1, source_target_pairs={{0,8},{16,24},{1,9},{17,25},{2,10},{18,26},{3,11},{19,27},{4,12},{... | collective-permute-start | bytes 786440 | tf_op jit(solution)/shard_map/ppermute | solution.py:388
  40.7 10.3 %collective-permute-start.4 = (f32[512,128]{1,0:T(8,128)S(1)}, f32[512,128]{1,0:T(8,128)}, u32[]{:S(2)}, u32[]{:S(2)}) collective-permute-start(f32[512,128]{1,0:T(8,128)S(1)} %get-tuple-element.30.refs_1_), channel_id=1, source_target_pairs={{0,8},{16,24},{1,9},{17,25},{2,10},{18,26},{3,11},{19,27},{4,12},{... | collective-permute-start | bytes 786440 | tf_op jit(solution)/shard_map/ppermute | solution.py:388
  43.4 27.9 %copy-start.5 = (f32[512,128]{1,0:T(8,128)S(1)}, f32[512,128]{1,0:T(8,128)}, u32[]{:S(2)}) copy-start(f32[512,128]{1,0:T(8,128)} %get-tuple-element.29.refs_2_) | copy-start | bytes 786436
  43.4 27.9 %copy-start.6 = (f32[512,128]{1,0:T(8,128)S(1)}, f32[512,128]{1,0:T(8,128)}, u32[]{:S(2)}) copy-start(f32[512,128]{1,0:T(8,128)} %get-tuple-element.28.refs_3_) | copy-start | bytes 786436
  45.3 11.2 %collective-permute-start.5 = (f32[512,128]{1,0:T(8,128)}, f32[512,128]{1,0:T(8,128)S(1)}, u32[]{:S(2)}, u32[]{:S(2)}) collective-permute-start(f32[512,128]{1,0:T(8,128)} %get-tuple-element.29.refs_2_), channel_id=1, source_target_pairs={{0,8},{16,24},{1,9},{17,25},{2,10},{18,26},{3,11},{19,27},{4,12},{... | collective-permute-start | bytes 786440 | tf_op jit(solution)/shard_map/ppermute | solution.py:388
  50.9 31.5 %collective-permute-start.8 = (f32[1024,128]{1,0:T(8,128)S(1)}, f32[1024,128]{1,0:T(8,128)S(1)}, u32[]{:S(2)}, u32[]{:S(2)}) collective-permute-start(f32[1024,128]{1,0:T(8,128)S(1)} %select_convert_fusion), channel_id=1, source_target_pairs={{0,1},{1,0},{2,3},{3,2},{4,5},{5,4},{6,7},{7,6},{8,9},{9,8},{10,11... | collective-permute-start | bytes 1572872 | tf_op jit(solution)/shard_map/ppermute | solution.py:391
  56.5 8.8 %collective-permute-start.6 = (f32[512,128]{1,0:T(8,128)}, f32[512,128]{1,0:T(8,128)S(1)}, u32[]{:S(2)}, u32[]{:S(2)}) collective-permute-start(f32[512,128]{1,0:T(8,128)} %get-tuple-element.28.refs_3_), channel_id=1, source_target_pairs={{0,8},{16,24},{1,9},{17,25},{2,10},{18,26},{3,11},{19,27},{4,12},{... | collective-permute-start | bytes 786440 | tf_op jit(solution)/shard_map/ppermute | solution.py:388
  65.4 27.9 %collective-permute-start.16 = (f32[512,128]{1,0:T(8,128)S(1)}, f32[512,128]{1,0:T(8,128)S(1)}, u32[]{:S(2)}, u32[]{:S(2)}) collective-permute-start(f32[512,128]{1,0:T(8,128)S(1)} %shard_map.112), channel_id=1, source_target_pairs={{8,16},{9,17},{10,18},{11,19},{12,20},{13,21},{14,22},{15,23}} | collective-permute-start | bytes 786440 | tf_op jit(solution)/shard_map/ppermute | solution.py:483
  66.7 28.0 %collective-permute-start.20 = (f32[512,128]{1,0:T(8,128)S(1)}, f32[512,128]{1,0:T(8,128)S(1)}, u32[]{:S(2)}, u32[]{:S(2)}) collective-permute-start(f32[512,128]{1,0:T(8,128)S(1)} %shard_map.112), channel_id=1, source_target_pairs={{24,16},{25,17},{26,18},{27,19},{28,20},{29,21},{30,22},{31,23}} | collective-permute-start | bytes 786440 | tf_op jit(solution)/shard_map/ppermute | solution.py:483
  69.1 1.0 copy-start.4
  75.0 15.7 %collective-permute-start.14 = (s32[1,128]{1,0:T(1,128)S(1)}, s32[1,128]{1,0:T(1,128)S(1)}, u32[]{:S(2)}, u32[]{:S(2)}) collective-permute-start(s32[1,128]{1,0:T(1,128)S(1)} %get-tuple-element.15.refs_3_.refs_2_.refs_8_.refs_9_.refs_10_.refs_11_.refs_4_.refs_6_), channel_id=1, source_target_pairs={{8,16},{9,17},{10,18},{11,19},{12,20},{13,21},{14,22},{15,23}} | collective-permute-start | bytes 1544 | tf_op jit(solution)/shard_map/ppermute | solution.py:484
  78.7 5.0 %copy-start.9 = (s32[4]{0:T(128)S(1)}, s32[4]{0:T(128)}, u32[]{:S(2)}) copy-start(s32[4]{0:T(128)} %refs_14_.1) | copy-start | bytes 52
  78.7 13.3 %collective-permute-start.15 = (s32[1,128]{1,0:T(1,128)S(1)}, s32[1,128]{1,0:T(1,128)S(1)}, u32[]{:S(2)}, u32[]{:S(2)}) collective-permute-start(s32[1,128]{1,0:T(1,128)S(1)} %get-tuple-element.15.refs_3_.refs_2_.refs_8_.refs_9_.refs_10_.refs_11_.refs_4_.refs_6_), channel_id=1, source_target_pairs={{24,16},{25,17},{26,18},{27,19},{28,20},{29,21},{30,22},{31,23}} | collective-permute-start | bytes 1544 | tf_op jit(solution)/shard_map/ppermute | solution.py:484
  82.4 13.5 %collective-permute-start.17 = (f32[512,128]{1,0:T(8,128)S(1)}, f32[512,128]{1,0:T(8,128)S(1)}, u32[]{:S(2)}, u32[]{:S(2)}) collective-permute-start(f32[512,128]{1,0:T(8,128)S(1)} %shard_map.113), channel_id=1, source_target_pairs={{8,16},{9,17},{10,18},{11,19},{12,20},{13,21},{14,22},{15,23}} | collective-permute-start | bytes 786440 | tf_op jit(solution)/shard_map/ppermute | solution.py:483
  90.7 7.8 %collective-permute-start.18 = (f32[512,128]{1,0:T(8,128)S(1)}, f32[512,128]{1,0:T(8,128)S(1)}, u32[]{:S(2)}, u32[]{:S(2)}) collective-permute-start(f32[512,128]{1,0:T(8,128)S(1)} %shard_map.114), channel_id=1, source_target_pairs={{8,16},{9,17},{10,18},{11,19},{12,20},{13,21},{14,22},{15,23}} | collective-permute-start | bytes 786440 | tf_op jit(solution)/shard_map/ppermute | solution.py:483
  92.0 12.1 %collective-permute-start.19 = (f32[512,128]{1,0:T(8,128)S(1)}, f32[512,128]{1,0:T(8,128)S(1)}, u32[]{:S(2)}, u32[]{:S(2)}) collective-permute-start(f32[512,128]{1,0:T(8,128)S(1)} %shard_map.115), channel_id=1, source_target_pairs={{8,16},{9,17},{10,18},{11,19},{12,20},{13,21},{14,22},{15,23}} | collective-permute-start | bytes 786440 | tf_op jit(solution)/shard_map/ppermute | solution.py:483
  93.3 31.6 %collective-permute-start.12 = (f32[1024,128]{1,0:T(8,128)S(1)}, f32[1024,128]{1,0:T(8,128)S(1)}, u32[]{:S(2)}, u32[]{:S(2)}) collective-permute-start(f32[1024,128]{1,0:T(8,128)S(1)} %get-tuple-element.21), channel_id=1, source_target_pairs={{8,16},{9,17},{10,18},{11,19},{12,20},{13,21},{14,22},{15,23}} | collective-permute-start | bytes 1572872 | tf_op jit(solution)/shard_map/ppermute | solution.py:485
  94.6 30.3 %collective-permute-start.13 = (f32[1024,128]{1,0:T(8,128)S(1)}, f32[1024,128]{1,0:T(8,128)S(1)}, u32[]{:S(2)}, u32[]{:S(2)}) collective-permute-start(f32[1024,128]{1,0:T(8,128)S(1)} %get-tuple-element.21), channel_id=1, source_target_pairs={{24,16},{25,17},{26,18},{27,19},{28,20},{29,21},{30,22},{31,23}} | collective-permute-start | bytes 1572872 | tf_op jit(solution)/shard_map/ppermute | solution.py:485
  96.0 17.7 %collective-permute-start.21 = (f32[512,128]{1,0:T(8,128)S(1)}, f32[512,128]{1,0:T(8,128)S(1)}, u32[]{:S(2)}, u32[]{:S(2)}) collective-permute-start(f32[512,128]{1,0:T(8,128)S(1)} %shard_map.113), channel_id=1, source_target_pairs={{24,16},{25,17},{26,18},{27,19},{28,20},{29,21},{30,22},{31,23}} | collective-permute-start | bytes 786440 | tf_op jit(solution)/shard_map/ppermute | solution.py:483
  98.5 20.8 %collective-permute-start.22 = (f32[512,128]{1,0:T(8,128)S(1)}, f32[512,128]{1,0:T(8,128)S(1)}, u32[]{:S(2)}, u32[]{:S(2)}) collective-permute-start(f32[512,128]{1,0:T(8,128)S(1)} %shard_map.114), channel_id=1, source_target_pairs={{24,16},{25,17},{26,18},{27,19},{28,20},{29,21},{30,22},{31,23}} | collective-permute-start | bytes 786440 | tf_op jit(solution)/shard_map/ppermute | solution.py:483
  104.1 20.8 %collective-permute-start.23 = (f32[512,128]{1,0:T(8,128)S(1)}, f32[512,128]{1,0:T(8,128)S(1)}, u32[]{:S(2)}, u32[]{:S(2)}) collective-permute-start(f32[512,128]{1,0:T(8,128)S(1)} %shard_map.115), channel_id=1, source_target_pairs={{24,16},{25,17},{26,18},{27,19},{28,20},{29,21},{30,22},{31,23}} | collective-permute-start | bytes 786440 | tf_op jit(solution)/shard_map/ppermute | solution.py:483
  129.1 4.9 %collective-permute-start.24 = (f32[1024,128]{1,0:T(8,128)S(1)}, f32[1024,128]{1,0:T(8,128)S(1)}, u32[]{:S(2)}, u32[]{:S(2)}) collective-permute-start(f32[1024,128]{1,0:T(8,128)S(1)} %get-tuple-element.25), channel_id=1, source_target_pairs={{0,1},{1,0},{2,3},{3,2},{4,5},{5,4},{6,7},{7,6},{8,9},{9,8},{10,11... | collective-permute-start | bytes 1572872 | tf_op jit(solution)/shard_map/ppermute | solution.py:494

commit v2 on v0

v2 whole, which is shorter than its diff:
```python
import functools

import jax
import jax.numpy as jnp
from jax import lax
from jax.experimental import pallas as pl
from jax.experimental.pallas import tpu as pltpu
from jax.sharding import PartitionSpec as P

PANEL = 128
TILE = 256
TAGS = 128
COST = 1000
CUTS, PARTS = (0, 5, 9, 16), 16
VMEM_MIB = 8
LEAF_COST = 2 * 10**9
OWN_PART = 13
SPLIT = 4
PINNED = 2
BASE_COST = 10**12
F32 = jnp.float32
BF16 = jnp.bfloat16
ANY = pl.BlockSpec(memory_space=pl.ANY)
VMEM = pl.BlockSpec(memory_space=pltpu.VMEM)
SMEM = pl.BlockSpec(memory_space=pltpu.SMEM)
HBM = pl.BlockSpec(memory_space=pltpu.HBM)


def dot(left, right):
    return jnp.dot(left, right, preferred_element_type=F32)


def call(body, ins, specs, outs, out_specs, scratch=(), after=(), flops=COST, moved=1):
    count, extra = len(ins), len(after)

    def trimmed(*refs):
        body(*refs[:count], *refs[count + extra :])

    return pl.pallas_call(
        trimmed,
        out_shape=outs,
        in_specs=list(specs) + [ANY] * extra,
        out_specs=out_specs,
        scratch_shapes=list(scratch),
        compiler_params=pltpu.CompilerParams(vmem_limit_bytes=VMEM_MIB * 2**20),
        cost_estimate=pl.CostEstimate(flops=flops, bytes_accessed=moved, transcendentals=0),
    )(*ins, *after)


def shape(rows, cols, kind=F32):
    return jax.ShapeDtypeStruct((rows, cols), kind)


def masked_diag(tile):
    rows_here = lax.broadcasted_iota(jnp.int32, tile.shape, 0)
    cols_here = lax.broadcasted_iota(jnp.int32, tile.shape, 1)
    wide = tile.astype(F32)
    wide = jnp.where(rows_here > cols_here, wide, 0.0)
    return jnp.where(rows_here == cols_here, 1.0, wide).astype(BF16)


def lower_rows(read, rhs, tile_idx):
    lo, hi = tile_idx * TILE, (tile_idx + 1) * TILE
    total = dot(masked_diag(read(lo, hi, lo, hi)), rhs[lo:hi])
    if tile_idx:
        total = total + dot(read(lo, hi, 0, lo), rhs[0:lo])
    return total


def key_of(row, levels, sep_panels):
    slot = lax.div(row, jnp.int32(sep_panels))
    zeros = jnp.int32(0)
    for bit_pos in range(1, levels + 1):
        zeros = zeros + jnp.where(slot & (2**bit_pos - 1) == 0, 1, 0)
    return jnp.where(zeros == 0, levels - 1, zeros - 1) * sep_panels + row - slot * sep_panels


def tags_kernel(levels, sep_panels, leaf_rows, sep_rows, tags):
    n_leaf, n_sep = leaf_rows.shape[1], sep_rows.shape[1]
    keys = [key_of(leaf_rows[0, j], levels, sep_panels) for j in range(n_leaf)]
    ranks = [jnp.int32(0)] * n_leaf
    for j in range(n_leaf):
        for i in range(j):
            less = jnp.where(keys[i] < keys[j], 1, 0)
            ranks[j] = ranks[j] + less
            ranks[i] = ranks[i] + 1 - less
    for j in range(n_leaf):
        tags[0, ranks[j]] = keys[j]
        tags[0, n_leaf + n_sep + ranks[j]] = jnp.int32(j)
    for j in range(n_sep):
        tags[0, n_leaf + j] = key_of(sep_rows[0, j], levels, sep_panels)


def diagonal_kernel(piece, inverse, rhs, out):
    right = rhs[...]

    def product(first):
        for t in range(piece // TILE):
            out[t * TILE : (t + 1) * TILE] = lower_rows(lambda a, b, c, d: inverse[first + a : first + b, c:d], right, t)

    @pl.when(lax.axis_index("col") == 0)
    def _():
        product(0)

    @pl.when(lax.axis_index("col") != 0)
    def _():
        product(piece)


def leaf_sum(diag, other):
    return (diag[...] + jnp.where(lax.axis_index("col") == 0, 0.0, other[...])).astype(BF16)


def sum_kernel(diag, other, out, token):
    out[...] = leaf_sum(diag, other)
    token[...] = diag[0:8, 0:128]


def below_kernel(order_at, diag, other, below, tags, keep, send):
    right = leaf_sum(diag, other)
    half = keep.shape[1]
    is_first = lax.axis_index("col") == 0
    for t in range(keep.shape[0] // PANEL):
        source = pl.multiple_of(tags[0, order_at + t] * PANEL, PANEL)
        both = dot(below[pl.ds(source, PANEL)], right)
        left_half, right_half = both[:, :half], both[:, half:]
        keep[t * PANEL : (t + 1) * PANEL] = jnp.where(is_first, left_half, right_half)
        send[t * PANEL : (t + 1) * PANEL] = jnp.where(is_first, right_half, left_half)


def gather_kernel(firsts, keep, there, tags, *outs):
    chunks, owns = outs[: len(firsts)], outs[len(firsts) :]
    for chunk, (first, count) in zip(chunks, firsts):
        at = slice(first * PANEL, (first + count) * PANEL)
        chunk[...] = keep[at] + there[at]
    base = 0
    for own in owns:
        own[...] = jnp.zeros_like(own)
        add_rows(own, base, own.shape[0] // PANEL, chunks, [tags] * len(chunks), firsts, 1)
        base += own.shape[0] // PANEL


def add_rows(out, base, panels, arrays, tags, firsts, sign):
    for array, tag, (tag_at, count) in zip(arrays, tags, firsts):
        for i in range(count):
            place = tag[0, tag_at + i] - base

            @pl.when((place >= 0) & (place < panels))
            def _():
                at = pl.ds(pl.multiple_of(place * PANEL, PANEL), PANEL)
                rows = array[i * PANEL : (i + 1) * PANEL]
                out[at] = out[at] + rows if sign > 0 else out[at] - rows


def scatter_kernel(base, firsts, start, *refs):
    arrays, tags = refs[: len(firsts)], refs[len(firsts) : 2 * len(firsts)]
    dense = refs[2 * len(firsts) : -1]
    out = refs[-1]
    if not dense:
        out[...] = jnp.zeros_like(out)
    at, low, high = 0, start, start + out.shape[0]
    for one in dense:
        first, last = max(low - at, 0), min(high - at, one.shape[0])
        if first < last:
            out[at + first - low : at + last - low] = one[first:last]
        at += one.shape[0]
    add_rows(out, base, out.shape[0] // PANEL, arrays, tags, firsts, 1)


def base_kernel(base, firsts, n_dense, *refs):
    refs = list(refs)
    arrays, tags = refs[: len(firsts)], refs[len(firsts) : 2 * len(firsts)]
    dense = refs[2 * len(firsts) : 2 * len(firsts) + n_dense]
    mine, theirs, out = refs[2 * len(firsts) + n_dense :]
    piece, half = theirs.shape
    is_first = lax.axis_index("col") == 0

    @pl.when(is_first)
    def _():
        out[0:piece] = mine[:, 0:half].astype(F32)
        out[piece : 2 * piece] = theirs[...]

    @pl.when(jnp.logical_not(is_first))
    def _():
        out[0:piece] = theirs[...]
        out[piece : 2 * piece] = mine[:, half : 2 * half].astype(F32)

    at_row = 0
    for one in dense:
        rows = min(one.shape[0], 2 * piece)
        out[at_row : at_row + rows] -= one[0:rows]
        at_row = (at_row + rows) % (2 * piece)
    add_rows(out, base, 2 * piece // PANEL, arrays, tags, firsts, -1)


def residual_kernel(base, firsts, *refs):
    arrays, tags = refs[: len(firsts)], refs[len(firsts) : 2 * len(firsts)]
    right, keep, send, acc = refs[2 * len(firsts) :]
    acc[...] = right[...]
    add_rows(acc, base, acc.shape[0] // PANEL, arrays, tags, firsts, -1)
    piece = keep.shape[0]
    is_first = lax.axis_index("col") == 0

    @pl.when(is_first)
    def _():
        keep[...] = acc[0:piece]
        send[...] = acc[piece : 2 * piece]

    @pl.when(jnp.logical_not(is_first))
    def _():
        keep[...] = acc[piece : 2 * piece]
        send[...] = acc[0:piece]


def across_kernel(mine, theirs, inverse, right, *outs):
    piece, half = mine.shape
    is_first = lax.axis_index("col") == 0
    one, two = mine[...].astype(BF16), theirs[...].astype(BF16)
    right[:, 0:half] = jnp.where(is_first, one, two)
    right[:, half : 2 * half] = jnp.where(is_first, two, one)
    held = right[...]
    per = piece // len(outs)
    for t in range(piece // TILE):
        out, at = outs[t * TILE // per], t * TILE % per
        out[at : at + TILE] = dot(inverse[piece + t * TILE : piece + (t + 1) * TILE], held)


def finish_kernel(plan, *refs):
    refs = list(refs)

    def take(count):
        got = refs[:count]
        del refs[:count]
        return got

    diag = take(1)[0]
    others = take(plan["split"])
    widths = take(1)[0]
    below = take(1)[0] if plan["update"] else None
    before = take(1)[0] if plan["before"] else None
    out = take(1)[0]
    piece, half = out.shape[0], out.shape[1] // 2
    is_first = lax.axis_index("col") == 0
    leaf = lax.axis_index("leaf")
    span = 2 ** plan["level"]
    is_owner = leaf % span == span // 2
    width = widths[leaf - leaf % span + span // 2] - jnp.where(is_first, 0, piece)
    row_ids = lax.broadcasted_iota(jnp.int32, out.shape, 0)
    other = jnp.concatenate([one[...] for one in others], 0)
    total = diag[...] + jnp.where(is_first, 0.0, other)
    sol = jnp.where(row_ids < width, total, 0.0).astype(BF16)
    if plan["update"]:
        keep, *sends = take(1 + plan["split"])
        per = sends[0].shape[0]
        for t in range(0, below.shape[0], TILE):
            both = dot(below[t : t + TILE], sol)
            left_half, right_half = both[:, :half], both[:, half:]
            keep[t : t + TILE] = jnp.where(is_first, left_half, right_half)
            sends[t // per][t % per : t % per + TILE] = jnp.where(is_first, right_half, left_half)

    if before is None:
        out[...] = jnp.where(is_owner, sol, jnp.zeros_like(sol))
    else:
        out[...] = jnp.where(is_owner, sol, before[...])


def sum_two_kernel(one, two, out):
    out[...] = one[...] + two[...]


def sum_parts_kernel(whole, *refs):
    *parts, out = refs
    at = 0
    for part in parts:
        here = slice(at, at + part.shape[0])
        out[here] = whole[here] + part[...]
        at += part.shape[0]


def sum_two(one, two):
    return call(sum_two_kernel, (one, two), [VMEM] * 2, shape(*one.shape), VMEM)


def on_device(
    leaf_rhs, leaf_inverse, leaf_below, leaf_rows, sep_rhs, sep_inverse, sep_below, sep_rows, sep_width
):
    leaves = lax.axis_size("leaf")
    levels = leaves.bit_length() - 1
    piece, width_rhs = leaf_rhs.shape
    half = width_rhs // 2
    sep_cols = sep_inverse.shape[0]
    sep_piece = sep_inverse.shape[1]
    sep_panels = sep_cols // PANEL
    n_leaf, n_sep = leaf_rows.shape[1], sep_rows.shape[1]
    col = lax.axis_index("col")
    swap = [(0, 1), (1, 0)]

    bottom = dot(leaf_inverse[piece:], leaf_rhs)
    other = lax.ppermute(bottom, "col", swap)
    tags = call(
        functools.partial(tags_kernel, levels, sep_panels),
        (leaf_rows, sep_rows),
        [SMEM, SMEM],
        shape(1, TAGS, jnp.int32),
        SMEM,
        after=[bottom],
        flops=LEAF_COST,
    )
    diag = call(
        functools.partial(diagonal_kernel, piece),
        (leaf_inverse, leaf_rhs),
        [VMEM, VMEM],
        shape(piece, width_rhs),
        VMEM,
        after=[tags],
        flops=LEAF_COST,
    )

    tags_swap = lax.ppermute(tags, "leaf", [(i, i ^ 1) for i in range(leaves)])
    up = [(a - 1, a) for a in range(2, leaves, 4)]
    tags_up = lax.ppermute(tags, "leaf", up)

    rhs_out = jnp.where(col == 0, sep_rhs[:, half:], sep_rhs[:, :half]).astype(F32)
    rhs_theirs = lax.ppermute(rhs_out, "col", swap)

    starts = [n_leaf * part // PARTS for part in CUTS]
    counts = [(a, b - a) for a, b in zip(starts, starts[1:])]
    chunks = len(counts)
    keep, send = call(
        functools.partial(below_kernel, n_leaf + n_sep),
        (diag, other, leaf_below, tags),
        [VMEM] * 3 + [SMEM],
        (shape(n_leaf * PANEL, half),) * 2,
        (VMEM,) * 2,
        after=[rhs_theirs],
    )
    own_rows = sep_panels * OWN_PART // PARTS * PANEL
    got = call(
        functools.partial(gather_kernel, counts),
        (keep, lax.ppermute(send, "col", swap), tags),
        [VMEM] * 2 + [SMEM],
        (*(shape(count * PANEL, half) for first, count in counts), shape(own_rows, half), shape(sep_cols - own_rows, half)),
        (VMEM,) * (chunks + 2),
        after=[tags_swap],
    )
    mine, own = list(got[:chunks]), list(got[chunks:])

    theirs = [lax.ppermute(one, "leaf", [(i, i + 1) for i in range(0, leaves, 2)]) for one in mine]

    def scatter(rows, base, arrays, tag_list, firsts, dense, start, after):
        return call(
            functools.partial(scatter_kernel, base, firsts, start),
            (*arrays, *tag_list, *dense),
            [VMEM] * len(arrays) + [SMEM] * len(tag_list) + [VMEM] * len(dense),
            shape(rows, half),
            VMEM,
            after=after,
        )

    def right_side(base, arrays, tag_list, firsts, dense, after, flops=COST):
        return call(
            functools.partial(base_kernel, base, firsts, len(dense)),
            (*arrays, *tag_list, *dense, sep_rhs, rhs_theirs),
            [VMEM] * len(arrays) + [SMEM] * len(tag_list) + [VMEM] * (len(dense) + 2),
            shape(sep_cols, half),
            VMEM,
            after=after,
            flops=flops,
        )

    def solve(level, arrays, tag_list, firsts, base, right, before, after, after_late=(), split=1):
        update = level < levels
        keep, send = call(
            functools.partial(residual_kernel, base, firsts),
            (*arrays, *tag_list, right),
            [VMEM] * len(arrays) + [SMEM] * len(tag_list) + [VMEM],
            (shape(sep_piece, half),) * 2,
            (VMEM,) * 2,
            [pltpu.VMEM((sep_cols, half), F32)],
            after=after,
        )
        residual, *across = call(
            across_kernel,
            (keep, lax.ppermute(send, "col", swap), sep_inverse),
            [VMEM] * 3,
            (shape(sep_piece, width_rhs, BF16), *(shape(sep_piece // split, width_rhs),) * split),
            (VMEM,) * (1 + split),
        )
        other = [lax.ppermute(one, "col", swap) for one in across]
        diag = call(
            functools.partial(diagonal_kernel, sep_piece),
            (sep_inverse, residual),
            [VMEM] * 2,
            shape(sep_piece, width_rhs),
            VMEM,
        )
        plan = dict(level=level, update=update, before=before is not None, split=split)
        ins = [diag, *other, sep_width]
        outs = [shape(sep_piece, width_rhs, BF16)]
        if update:
            ins.append(sep_below)
            outs += [shape(sep_below.shape[0], half)] + [shape(sep_below.shape[0] // split, half)] * split
        if before is not None:
            ins.append(before)
        got = call(
            functools.partial(finish_kernel, plan),
            ins,
            [VMEM] * (1 + split) + [SMEM] + [VMEM] * (len(ins) - 2 - split),
            tuple(outs),
            (VMEM,) * len(outs),
        )
        if not update:
            return got[0], None
        there = [lax.ppermute(one, "col", swap) for one in got[2:]]
        total = call(
            sum_parts_kernel, (got[1], *there), [VMEM] * (1 + split), shape(*got[1].shape), VMEM, after=after_late
        )
        return got[0], total

    down = [(i + 1, i) for i in range(2, leaves, 4)]
    own_right = [lax.ppermute(one, "leaf", down) for one in own]
    right = right_side((levels - 1) * sep_panels, mine, [tags] * chunks, counts, [], own[:1])
    leaf_solution, last = call(
        sum_kernel,
        (diag, other),
        [VMEM] * 2,
        (shape(piece, width_rhs, BF16), shape(8, 128)),
        (VMEM, VMEM),
        after=[right],
    )

    came = []
    for n in range(chunks):
        one = scatter(
            counts[n][1] * PANEL,
            starts[n],
            theirs[: n + 1],
            [tags_swap] * (n + 1),
            counts[: n + 1],
            own,
            starts[n] * PANEL,
            [last, tags_up] if n == 0 else [last, *came[: n - 1]],
        )
        came.append(lax.ppermute(one, "leaf", up))
        last = one
    pinned = [last, *own_right[:PINNED], *came[:-1]]
    held, update = solve(
        1, theirs, [tags_swap] * chunks, counts, (levels - 1) * sep_panels, right, None, pinned, [], SPLIT
    )
    above_left = above_right = None
    if levels > 2:
        rows = (levels - 2) * sep_cols
        above_right = scatter(rows, sep_panels, mine, [tags] * chunks, counts, [], 0, [])
        above_left = scatter(rows, sep_panels, theirs, [tags_swap] * chunks, counts, [above_right], 0, [])
    for level in range(2, levels + 1):
        span = 2**level
        owners = range(span // 2, leaves, span)
        step = span // 4
        pairs = [[(a - step, a) for a in owners], [(a + step, a) for a in owners]]
        base = (level - 2) * sep_panels
        if level == 2:
            dense, tag_pair = [*came, *own_right], [tags_up, tags_swap]
            own_rows, own_tags, own_counts = mine, [tags] * chunks, counts
        else:
            dense = [lax.ppermute(dense_now, "leaf", one) for one in pairs]
            tag_pair = [lax.ppermute(tags, "leaf", one) for one in pairs]
            own_rows, own_tags, own_counts = [], [], []
        came_update = [lax.ppermute(update, "leaf", one) for one in pairs]
        firsts = [(n_leaf, n_sep)] * 2
        right = right_side(base, own_rows, own_tags, own_counts, dense, [update], BASE_COST)
        if level < levels:
            parts = (above_left, above_right) if level == 2 else (above_now, above_now)
            parts = [lax.ppermute(part, "leaf", one) for part, one in zip(parts, pairs)]
            rows = (levels - level) * sep_cols
            total = scatter(
                rows,
                base + sep_panels,
                [*own_rows, *came_update],
                [*own_tags, *tag_pair],
                [*own_counts, *firsts],
                [sum_two(*parts)],
                0,
                [],
            )
            dense_now, above_now = total[:sep_cols], total[sep_cols:]
        held, update = solve(level, came_update, tag_pair, firsts, base, right, held, [])
    return leaf_solution, held


def solution(mesh):
    placed = (
        P(("leaf", "col"), "row"),
        P("leaf", "col"),
        P("leaf", "col"),
        P("leaf", None),
        P(("leaf", "col"), "row"),
        P("leaf", "col"),
        P("leaf", "col"),
        P("leaf", None),
        P(),
    )
    return jax.shard_map(
        on_device,
        mesh=mesh,
        in_specs=placed,
        out_specs=(P(("leaf", "col"), "row"), P(("leaf", "col"), "row")),
        check_vma=False,
    )
```

time: 223 us -> 81.7 us (0.37)
  waiting for transfers between devices: 149 us -> 30.6 us
  starting transfers between devices: 3.12 us -> 26.8 us
  matrix products: 25.1 us -> 2.44 us
  Pallas kernels: 0 us -> 18.5 us
  other arithmetic: 16.4 us -> 0.04 us
  between operations: 13.9 us -> 0.95 us
  local copies, waits for them, and re-layouts: 13.7 us -> 2.08 us
    ppermute x3 -> x26, waiting for transfers between devices: 91.4 us -> 30.6 us  [the longest x2 11.3 us: on_device(): came_update = [lax.ppermute(update, 'leaf', one) for one in pairs]]
    reduce_scatter x5 -> x0, waiting for transfers between devices: 57.6 us -> none  [the longest x2 24.7 us: sep_product(): lax.psum_scatter(jnp.dot(masked, right_side, preferred_element_type=jnp.f...]
    ppermute x3 -> x26, starting transfers between devices: 2.73 us -> 26.8 us  [the longest x3 6.68 us: on_device(): lax.ppermute(one, 'leaf', [(i, i + 1) for i in range(0, leaves, 2)])]
    dot_general x5 -> x1, matrix products: 25.1 us -> 2.44 us  [dot(): return jnp.dot(left, right, preferred_element_type=F32)]
    pallas_call x0 -> x19, Pallas kernels: none -> 18.5 us  [call(): pl.pallas_call(trimmed, out_shape=outs, in_specs=list(specs) + [ANY] * ex...]
    scatter-add x2 -> x0, other arithmetic: 9.09 us -> none  [the longest x1 5.35 us: on_device(): pending.at[local_panels(leaf_rows[0], levels, sep_panels)].add(leaf_term)]
    slice x2 -> x0, local copies, waits for them, and re-layouts: 6.21 us -> none  [on_device(): pending[(level_now - 1) * sep_panels:level_now * sep_panels]]
    reshape x1 -> x0, local copies, waits for them, and re-layouts: 2.93 us -> none  [on_device(): jnp.dot(leaf_below, leaf_solution, preferred_element_type=jnp.float32)]
  transfers between devices with their start and end apart: 8 -> 26, of which waited for: 8 -> 20; matrix products, arithmetic and copies ran while one was open for 1% -> 0% of each run, Pallas kernels for 0% -> 13%
where the time goes in v2:
time: 81.7 us; the launch traced here: 81.4 us
  waiting for transfers between devices  30.6 us (37%)
  starting transfers between devices  26.8 us (33%)
  Pallas kernels  18.5 us (23%)
  matrix products  2.44 us (3%)
  local copies, waits for them, and re-layouts  2.08 us (3%)
  between operations  0.95 us (1%)
    pallas_call x19, Pallas kernels, call(): pl.pallas_call(trimmed, out_shape=outs, in_specs=list(specs) + [ANY] * ex...  18.5 us
    ppermute x2, waiting for transfers between devices, on_device(): came_update = [lax.ppermute(update, 'leaf', one) for one in pairs]  11.3 us
    ppermute x3, waiting for transfers between devices, on_device(): lax.ppermute(one, 'leaf', [(i, i + 1) for i in range(0, leaves, 2)])  8.07 us
    ppermute x3, starting transfers between devices, on_device(): lax.ppermute(one, 'leaf', [(i, i + 1) for i in range(0, leaves, 2)])  6.68 us
    ppermute x2, starting transfers between devices, solve(): lax.ppermute(send, 'col', swap)  4.63 us
    ppermute x3, starting transfers between devices, on_device(): came.append(lax.ppermute(one, 'leaf', up))  4.13 us
    ppermute x5, waiting for transfers between devices, solve(): other = [lax.ppermute(one, 'col', swap) for one in across]  2.82 us
    ppermute x2, starting transfers between devices, on_device(): own_right = [lax.ppermute(one, 'leaf', down) for one in own]  2.58 us
  transfers between devices with their start and end apart: 26, of which 20 were waited for; matrix products, arithmetic and copies ran while one was open for 0% of the time, Pallas kernels for 13%

profile of v2, /device:TPU:21, one launch (start us, length us, event | category | flops | bytes accessed | tf_op | source)
XLA Modules:
  0.0 81.4 jit_solution(11030816889597592119)
XLA Ops:
  0.7 2.4 %fusion.refs_2_ = f32[1024,256]{1,0:T(8,128)S(1)} fusion(bf16[1024,256]{1,0:T(8,128)(2,1)} %refs_1_.3, bf16[2048,1024]{1,0:T(8,128)(2,1)} %refs_0_.5), kind=kOutput, calls=%fused_computation | convolution fusion | flops 536870912 | bytes 3670016 | tf_op jit(solution)/shard_map/dot_general | solution.py:30
  3.1 0.7 collective-permute-start
  4.0 1.5 %shard_map.104.refs_2_.refs_3_.refs_4_.refs_5_ = s32[1,128]{1,0:T(1,128)S(1)} custom-call(s32[1,16]{1,0:T(1,128)S(1)} %copy-done.11, s32[1,8]{1,0:T(1,128)S(1)} %copy-done.12, f32[1024,256]{1,0:T(8,128)S(1)} %fusion.refs_2_), custom_call_target="tpu_custom_call" | custom-call | flops 2000000000 | bytes 1 | tf_op jit(solution)/shard_map/pallas_call | solution.py:39
  5.6 0.5 copy-done.9
  6.2 0.6 shard_map.105.refs_0_
  6.9 1.5 %copy-done.1 = bf16[2048,1024]{1,0:T(8,128)(2,1)S(1)} copy-done((bf16[2048,1024]{1,0:T(8,128)(2,1)S(1)}, bf16[2048,1024]{1,0:T(8,128)(2,1)}, u32[]{:S(2)}) %copy-start.1) | copy-done | bytes 4194328
  8.3 1.9 %shard_map.106 = (f32[2048,128]{1,0:T(8,128)S(1)}, f32[2048,128]{1,0:T(8,128)S(1)}) custom-call(f32[1024,256]{1,0:T(8,128)S(1)} %shard_map.105.refs_0_, f32[1024,256]{1,0:T(8,128)S(1)} %collective-permute-done.refs_1_, bf16[2048,1024]{1,0:T(8,128)(2,1)S(1)} %copy-done.1, s32[1,128]{1,0:T(1,128)S(1)} %shard_map.104.refs_2_.refs_3_.refs_4_.refs_5_, ...), custom_call_target="tpu_custom_call" | custom-call | flops 1000 | bytes 1 | tf_op jit(solution)/shard_map/pallas_call | solution.py:39
  10.4 1.4 %collective-permute-start.3 = (s32[1,128]{1,0:T(1,128)S(1)}, s32[1,128]{1,0:T(1,128)S(1)}, u32[]{:S(2)}, u32[]{:S(2)}) collective-permute-start(s32[1,128]{1,0:T(1,128)S(1)} %shard_map.104.refs_2_.refs_3_.refs_4_.refs_5_), channel_id=1, source_target_pairs={{0,8},{8,0},{16,24},{24,16},{1,9},{9,1},{17,25},{25,17},{2,10},{10... | collective-permute-start | bytes 1544 | tf_op jit(solution)/shard_map/ppermute | solution.py:319
  11.7 1.1 %collective-permute-done.3.refs_3_.refs_1_.refs_2_.refs_4_.refs_5_ = s32[1,128]{1,0:T(1,128)S(1)} collective-permute-done((s32[1,128]{1,0:T(1,128)S(1)}, s32[1,128]{1,0:T(1,128)S(1)}, u32[]{:S(2)}, u32[]{:S(2)}) %collective-permute-start.3) | collective-permute-done | bytes 544 | tf_op jit(solution)/shard_map/ppermute | solution.py:319
  13.0 1.0 %shard_map.107 = (f32[640,128]{1,0:T(8,128)S(1)}, f32[512,128]{1,0:T(8,128)S(1)}, f32[896,128]{1,0:T(8,128)S(1)}, f32[1664,128]{1,0:T(8,128)S(1)}, f32[384,128]{1,0:T(8,128)S(1)}) custom-call(f32[2048,128]{1,0:T(8,128)S(1)} %get-tuple-element.28.refs_0_, f32[2048,128]{1,0:T(8,128)S(1)} %collective-permute-done.2.refs_1_, ...), custom_call_target="tpu_custom_call" | custom-call | flops 1000 | bytes 1 | tf_op jit(solution)/shard_map/pallas_call | solution.py:39
  14.1 1.3 %collective-permute-start.9 = (f32[1664,128]{1,0:T(8,128)S(1)}, f32[1664,128]{1,0:T(8,128)S(1)}, u32[]{:S(2)}, u32[]{:S(2)}) collective-permute-start(f32[1664,128]{1,0:T(8,128)S(1)} %get-tuple-element.33.refs_8_.refs_2_.refs_4_.refs_6_), channel_id=1, source_target_pairs={{24,16},{25,17},{26,18},{27,19},{28,20},{29,21},{30,22},{31,23}} | collective-permute-start | bytes 2555912 | tf_op jit(solution)/shard_map/ppermute | solution.py:421
  15.4 4.1 %collective-permute-start.4 = (f32[640,128]{1,0:T(8,128)S(1)}, f32[640,128]{1,0:T(8,128)S(1)}, u32[]{:S(2)}, u32[]{:S(2)}) collective-permute-start(f32[640,128]{1,0:T(8,128)S(1)} %get-tuple-element.30.refs_0_), channel_id=1, source_target_pairs={{0,8},{16,24},{1,9},{17,25},{2,10},{18,26},{3,11},{19,27},{4,12},{... | collective-permute-start | bytes 983048 | tf_op jit(solution)/shard_map/ppermute | solution.py:348
  19.4 1.3 %collective-permute-start.5 = (f32[512,128]{1,0:T(8,128)S(1)}, f32[512,128]{1,0:T(8,128)S(1)}, u32[]{:S(2)}, u32[]{:S(2)}) collective-permute-start(f32[512,128]{1,0:T(8,128)S(1)} %get-tuple-element.31.refs_1_), channel_id=1, source_target_pairs={{0,8},{16,24},{1,9},{17,25},{2,10},{18,26},{3,11},{19,27},{4,12},{... | collective-permute-start | bytes 786440 | tf_op jit(solution)/shard_map/ppermute | solution.py:348
  20.7 1.3 %collective-permute-start.6 = (f32[896,128]{1,0:T(8,128)S(1)}, f32[896,128]{1,0:T(8,128)S(1)}, u32[]{:S(2)}, u32[]{:S(2)}) collective-permute-start(f32[896,128]{1,0:T(8,128)S(1)} %get-tuple-element.32.refs_2_), channel_id=1, source_target_pairs={{0,8},{16,24},{1,9},{17,25},{2,10},{18,26},{3,11},{19,27},{4,12},{... | collective-permute-start | bytes 1376264 | tf_op jit(solution)/shard_map/ppermute | solution.py:348
  22.1 1.3 %collective-permute-start.7 = (s32[1,128]{1,0:T(1,128)S(1)}, s32[1,128]{1,0:T(1,128)S(1)}, u32[]{:S(2)}, u32[]{:S(2)}) collective-permute-start(s32[1,128]{1,0:T(1,128)S(1)} %shard_map.104.refs_2_.refs_3_.refs_4_.refs_5_), channel_id=1, source_target_pairs={{8,16},{9,17},{10,18},{11,19},{12,20},{13,21},{14,22},{15,23}} | collective-permute-start | bytes 1544 | tf_op jit(solution)/shard_map/ppermute | solution.py:321
  23.4 0.8 %shard_map.108.refs_2_.refs_6_ = f32[2048,128]{1,0:T(8,128)S(1)} custom-call(f32[640,128]{1,0:T(8,128)S(1)} %get-tuple-element.30.refs_0_, f32[512,128]{1,0:T(8,128)S(1)} %get-tuple-element.31.refs_1_, f32[896,128]{1,0:T(8,128)S(1)} %get-tuple-element.32.refs_2_, s32[1,128]{1,0:T(1,128)S(1)} %shard_map.104.refs_2_.refs_3_.refs_4_.refs_5_, ...), custom_call_target="tpu_custom_call" | custom-call | flops 1000 | bytes 1 | tf_op jit(solution)/shard_map/pallas_call | solution.py:39
  24.2 0.9 %shard_map.109 = (bf16[1024,256]{1,0:T(8,128)(2,1)}, f32[8,128]{1,0:T(8,128)S(1)}) custom-call(f32[1024,256]{1,0:T(8,128)S(1)} %shard_map.105.refs_0_, f32[1024,256]{1,0:T(8,128)S(1)} %collective-permute-done.refs_1_, f32[2048,128]{1,0:T(8,128)S(1)} %shard_map.108.refs_2_.refs_6_), custom_call_target="tpu_custom_call" | custom-call | flops 1000 | bytes 1 | tf_op jit(solution)/shard_map/pallas_call | solution.py:39
  25.1 1.5 %collective-permute-done.7.refs_5_.refs_2_ = s32[1,128]{1,0:T(1,128)S(1)} collective-permute-done((s32[1,128]{1,0:T(1,128)S(1)}, s32[1,128]{1,0:T(1,128)S(1)}, u32[]{:S(2)}, u32[]{:S(2)}) %collective-permute-start.7) | collective-permute-done | bytes 544 | tf_op jit(solution)/shard_map/ppermute | solution.py:321
  26.7 0.6 shard_map.110.refs_6_
  27.3 1.3 %collective-permute-start.8 = (f32[640,128]{1,0:T(8,128)S(1)}, f32[640,128]{1,0:T(8,128)S(1)}, u32[]{:S(2)}, u32[]{:S(2)}) collective-permute-start(f32[640,128]{1,0:T(8,128)S(1)} %shard_map.110.refs_6_), channel_id=1, source_target_pairs={{8,16},{9,17},{10,18},{11,19},{12,20},{13,21},{14,22},{15,23}} | collective-permute-start | bytes 983048 | tf_op jit(solution)/shard_map/ppermute | solution.py:444
  28.6 1.8 %collective-permute-done.5.refs_1_ = f32[512,128]{1,0:T(8,128)S(1)} collective-permute-done((f32[512,128]{1,0:T(8,128)S(1)}, f32[512,128]{1,0:T(8,128)S(1)}, u32[]{:S(2)}, u32[]{:S(2)}) %collective-permute-start.5) | collective-permute-done | bytes 262176 | tf_op jit(solution)/shard_map/ppermute | solution.py:348
  30.3 0.6 shard_map.111.refs_8_
  31.0 1.6 %collective-permute-start.11 = (f32[512,128]{1,0:T(8,128)S(1)}, f32[512,128]{1,0:T(8,128)S(1)}, u32[]{:S(2)}, u32[]{:S(2)}) collective-permute-start(f32[512,128]{1,0:T(8,128)S(1)} %shard_map.111.refs_8_), channel_id=1, source_target_pairs={{8,16},{9,17},{10,18},{11,19},{12,20},{13,21},{14,22},{15,23}} | collective-permute-start | bytes 786440 | tf_op jit(solution)/shard_map/ppermute | solution.py:444
  32.6 1.3 %collective-permute-start.10 = (f32[384,128]{1,0:T(8,128)S(1)}, f32[384,128]{1,0:T(8,128)S(1)}, u32[]{:S(2)}, u32[]{:S(2)}) collective-permute-start(f32[384,128]{1,0:T(8,128)S(1)} %get-tuple-element.35.refs_3_.refs_5_.refs_7_), channel_id=1, source_target_pairs={{24,16},{25,17},{26,18},{27,19},{28,20},{29,21},{30,22},{31,23}} | collective-permute-start | bytes 589832 | tf_op jit(solution)/shard_map/ppermute | solution.py:421
  33.9 6.3 %collective-permute-done.6.refs_2_ = f32[896,128]{1,0:T(8,128)S(1)} collective-permute-done((f32[896,128]{1,0:T(8,128)S(1)}, f32[896,128]{1,0:T(8,128)S(1)}, u32[]{:S(2)}, u32[]{:S(2)}) %collective-permute-start.6) | collective-permute-done | bytes 458784 | tf_op jit(solution)/shard_map/ppermute | solution.py:348
  40.2 0.7 shard_map.112.refs_7_
  40.9 0.5 collective-permute-done.11.refs_11_.refs_7_
  41.4 0.9 %shard_map.113 = (f32[1024,128]{1,0:T(8,128)S(1)}, f32[1024,128]{1,0:T(8,128)S(1)}) custom-call(f32[640,128]{1,0:T(8,128)S(1)} %collective-permute-done.4.refs_0_, f32[512,128]{1,0:T(8,128)S(1)} %collective-permute-done.5.refs_1_, f32[896,128]{1,0:T(8,128)S(1)} %collective-permute-done.6.refs_2_, ...), custom_call_target="tpu_custom_call" | custom-call | flops 1000 | bytes 1 | tf_op jit(solution)/shard_map/pallas_call | solution.py:39
  42.3 3.6 %collective-permute-start.12 = (f32[1024,128]{1,0:T(8,128)S(1)}, f32[1024,128]{1,0:T(8,128)S(1)}, u32[]{:S(2)}, u32[]{:S(2)}) collective-permute-start(f32[1024,128]{1,0:T(8,128)S(1)} %get-tuple-element.38), channel_id=1, source_target_pairs={{0,1},{1,0},{2,3},{3,2},{4,5},{5,4},{6,7},{7,6},{8,9},{9,8},{10,11... | collective-permute-start | bytes 1572872 | tf_op jit(solution)/shard_map/ppermute | solution.py:384
  45.9 1.3 %collective-permute-start.23 = (f32[896,128]{1,0:T(8,128)S(1)}, f32[896,128]{1,0:T(8,128)S(1)}, u32[]{:S(2)}, u32[]{:S(2)}) collective-permute-start(f32[896,128]{1,0:T(8,128)S(1)} %shard_map.112.refs_7_), channel_id=1, source_target_pairs={{8,16},{9,17},{10,18},{11,19},{12,20},{13,21},{14,22},{15,23}} | collective-permute-start | bytes 1376264 | tf_op jit(solution)/shard_map/ppermute | solution.py:444
  47.4 0.8 shard_map.114
  49.3 0.5 shard_map.115.refs_0_
  51.0 1.3 %shard_map.116 = (bf16[1024,256]{1,0:T(8,128)(2,1)S(1)}, f32[1024,128]{1,0:T(8,128)S(1)}, f32[256,128]{1,0:T(8,128)S(1)}, f32[256,128]{1,0:T(8,128)S(1)}, f32[25...) custom-call(f32[1024,256]{1,0:T(8,128)S(1)} %shard_map.115.refs_0_, f32[256,256]{1,0:T(8,128)S(1)} %collective-permute-done.13.refs_1_, ...), custom_call_target="tpu_custom_call" | custom-call | flops 1000 | bytes 1 | tf_op jit(solution)/shard_map/pallas_call | solution.py:39
  54.6 0.8 %shard_map.117.refs_13_ = f32[1024,128]{1,0:T(8,128)} custom-call(f32[1024,128]{1,0:T(8,128)S(1)} %get-tuple-element.44.refs_0_, f32[256,128]{1,0:T(8,128)S(1)} %collective-permute-done.17.refs_1_, f32[256,128]{1,0:T(8,128)S(1)} %collective-permute-done.18.refs_2_, f32[256,128]{1,0:T(8,128)S(1)} %collective-permute-done.19.refs_3_, ...), custom_call_target="tpu_custom_call" | custom-call | flops 1000 | bytes 1 | tf_op jit(solution)/shard_map/pallas_call | solution.py:39
  55.4 1.3 %collective-permute-start.21 = (f32[1024,128]{1,0:T(8,128)}, f32[1024,128]{1,0:T(8,128)}, u32[]{:S(2)}, u32[]{:S(2)}) collective-permute-start(f32[1024,128]{1,0:T(8,128)} %shard_map.117.refs_13_), channel_id=1, source_target_pairs={{8,16},{9,17},{10,18},{11,19},{12,20},{13,21},{14,22},{15,23}} | collective-permute-start | bytes 1572872 | tf_op jit(solution)/shard_map/ppermute | solution.py:468
  56.7 1.3 %collective-permute-start.22 = (f32[1024,128]{1,0:T(8,128)}, f32[1024,128]{1,0:T(8,128)}, u32[]{:S(2)}, u32[]{:S(2)}) collective-permute-start(f32[1024,128]{1,0:T(8,128)} %shard_map.117.refs_13_), channel_id=1, source_target_pairs={{24,16},{25,17},{26,18},{27,19},{28,20},{29,21},{30,22},{31,23}} | collective-permute-start | bytes 1572872 | tf_op jit(solution)/shard_map/ppermute | solution.py:468
  58.0 1.9 %collective-permute-done.23.refs_8_ = f32[896,128]{1,0:T(8,128)S(1)} collective-permute-done((f32[896,128]{1,0:T(8,128)S(1)}, f32[896,128]{1,0:T(8,128)S(1)}, u32[]{:S(2)}, u32[]{:S(2)}) %collective-permute-start.23) | collective-permute-done | bytes 458784 | tf_op jit(solution)/shard_map/ppermute | solution.py:444
  59.9 1.0 %shard_map.118.refs_4_ = f32[2048,128]{1,0:T(8,128)S(1)} custom-call(f32[640,128]{1,0:T(8,128)S(1)} %get-tuple-element.30.refs_0_, f32[512,128]{1,0:T(8,128)S(1)} %get-tuple-element.31.refs_1_, f32[896,128]{1,0:T(8,128)S(1)} %get-tuple-element.32.refs_2_, s32[1,128]{1,0:T(1,128)S(1)} %shard_map.104.refs_2_.refs_3_.refs_4_.refs_5_, ...), custom_call_target="tpu_custom_call" | custom-call | flops 999999995904 | bytes 1 | tf_op jit(solution)/shard_map/pallas_call | solution.py:39
  61.0 10.2 %collective-permute-done.21.refs_0_ = f32[1024,128]{1,0:T(8,128)} collective-permute-done((f32[1024,128]{1,0:T(8,128)}, f32[1024,128]{1,0:T(8,128)}, u32[]{:S(2)}, u32[]{:S(2)}) %collective-permute-start.21) | collective-permute-done | bytes 524320 | tf_op jit(solution)/shard_map/ppermute | solution.py:468
  71.2 1.1 %collective-permute-done.22.refs_1_ = f32[1024,128]{1,0:T(8,128)} collective-permute-done((f32[1024,128]{1,0:T(8,128)}, f32[1024,128]{1,0:T(8,128)}, u32[]{:S(2)}, u32[]{:S(2)}) %collective-permute-start.22) | collective-permute-done | bytes 524320 | tf_op jit(solution)/shard_map/ppermute | solution.py:468
  72.3 1.6 %shard_map.119 = (f32[1024,128]{1,0:T(8,128)S(1)}, f32[1024,128]{1,0:T(8,128)S(1)}) custom-call(f32[1024,128]{1,0:T(8,128)} %collective-permute-done.21.refs_0_, f32[1024,128]{1,0:T(8,128)} %collective-permute-done.22.refs_1_, s32[1,128]{1,0:T(1,128)S(1)} %copy-done.8, s32[1,128]{1,0:T(1,128)S(1)} %copy-done.5, f32[2048,128]{1,0:T(8,128)S(1)} %shard_map.118.refs_4_), custom_call_target="tpu_custom_call" | custom-call | flops 1000 | bytes 1 | tf_op jit(solution)/shard_map/pallas_call | solution.py:39
  73.8 1.1 %collective-permute-start.24 = (f32[1024,128]{1,0:T(8,128)S(1)}, f32[1024,128]{1,0:T(8,128)S(1)}, u32[]{:S(2)}, u32[]{:S(2)}) collective-permute-start(f32[1024,128]{1,0:T(8,128)S(1)} %get-tuple-element.50), channel_id=1, source_target_pairs={{0,1},{1,0},{2,3},{3,2},{4,5},{5,4},{6,7},{7,6},{8,9},{9,8},{10,11... | collective-permute-start | bytes 1572872 | tf_op jit(solution)/shard_map/ppermute | solution.py:384
  74.9 1.5 %collective-permute-done.24.refs_1_ = f32[1024,128]{1,0:T(8,128)S(1)} collective-permute-done((f32[1024,128]{1,0:T(8,128)S(1)}, f32[1024,128]{1,0:T(8,128)S(1)}, u32[]{:S(2)}, u32[]{:S(2)}) %collective-permute-start.24) | collective-permute-done | bytes 524320 | tf_op jit(solution)/shard_map/ppermute | solution.py:384
  76.4 0.7 shard_map.120
  77.2 0.4 collective-permute-start.25
  77.6 0.5 shard_map.121.refs_0_
  78.2 1.7 %collective-permute-done.25.refs_1_ = f32[1024,256]{1,0:T(8,128)S(1)} collective-permute-done((f32[1024,256]{1,0:T(8,128)S(1)}, f32[1024,256]{1,0:T(8,128)S(1)}, u32[]{:S(2)}, u32[]{:S(2)}) %collective-permute-start.25) | collective-permute-done | bytes 1048608 | tf_op jit(solution)/shard_map/ppermute | solution.py:389
  79.9 1.5 %shard_map.122 = bf16[1024,256]{1,0:T(8,128)(2,1)} custom-call(f32[1024,256]{1,0:T(8,128)S(1)} %shard_map.121.refs_0_, f32[1024,256]{1,0:T(8,128)S(1)} %collective-permute-done.25.refs_1_, s32[4]{0:T(128)S(1)} %copy-done.6, bf16[1024,256]{1,0:T(8,128)(2,1)S(1)} %get-tuple-element.53.refs_3_), custom_call_target="tpu_custom_call" | custom-call | flops 1000 | bytes 1 | tf_op jit(solution)/shard_map/pallas_call | solution.py:39
  (51 shorter events, 5.5 us)
Async XLA Ops:
  0.6 3.2 %copy-start.2 = (bf16[1024,256]{1,0:T(8,128)(2,1)S(1)}, bf16[1024,256]{1,0:T(8,128)(2,1)}, u32[]{:S(2)}) copy-start(bf16[1024,256]{1,0:T(8,128)(2,1)} %refs_11_.1) | copy-start | bytes 1572868
  0.6 3.4 %copy-start.11 = (s32[1,16]{1,0:T(1,128)S(1)}, s32[1,16]{1,0:T(1,128)}, u32[]{:S(2)}) copy-start(s32[1,16]{1,0:T(1,128)} %refs_0_.4) | copy-start | bytes 196
  0.7 3.4 %copy-start.12 = (s32[1,8]{1,0:T(1,128)S(1)}, s32[1,8]{1,0:T(1,128)}, u32[]{:S(2)}) copy-start(s32[1,8]{1,0:T(1,128)} %refs_1_.2) | copy-start | bytes 100
  3.1 3.8 %collective-permute-start = (f32[1024,256]{1,0:T(8,128)S(1)}, f32[1024,256]{1,0:T(8,128)S(1)}, u32[]{:S(2)}, u32[]{:S(2)}) collective-permute-start(f32[1024,256]{1,0:T(8,128)S(1)} %fusion.refs_2_), channel_id=1, source_target_pairs={{0,1},{1,0},{2,3},{3,2},{4,5},{5,4},{6,7},{7,6},{8,9},{9,8},{10,11... | collective-permute-start | bytes 3145736 | tf_op jit(solution)/shard_map/ppermute | solution.py:299
  3.9 2.2 %copy-start.9 = (bf16[2048,1024]{1,0:T(8,128)(2,1)S(1)}, bf16[2048,1024]{1,0:T(8,128)(2,1)}, u32[]{:S(2)}) copy-start(bf16[2048,1024]{1,0:T(8,128)(2,1)} %refs_0_.5) | copy-start | bytes 12582916
  3.9 2.3 %copy-start.10 = (bf16[1024,256]{1,0:T(8,128)(2,1)S(1)}, bf16[1024,256]{1,0:T(8,128)(2,1)}, u32[]{:S(2)}) copy-start(bf16[1024,256]{1,0:T(8,128)(2,1)} %refs_1_.3) | copy-start | bytes 1572868
  3.9 3.0 %collective-permute-start.1 = (f32[1024,128]{1,0:T(8,128)S(1)}, f32[1024,128]{1,0:T(8,128)S(1)}, u32[]{:S(2)}, u32[]{:S(2)}) collective-permute-start(f32[1024,128]{1,0:T(8,128)S(1)} %select_convert_fusion), channel_id=1, source_target_pairs={{0,1},{1,0},{2,3},{3,2},{4,5},{5,4},{6,7},{7,6},{8,9},{9,8},{10,11... | collective-permute-start | bytes 1572872 | tf_op jit(solution)/shard_map/ppermute | solution.py:324
  6.2 2.2 %copy-start.1 = (bf16[2048,1024]{1,0:T(8,128)(2,1)S(1)}, bf16[2048,1024]{1,0:T(8,128)(2,1)}, u32[]{:S(2)}) copy-start(bf16[2048,1024]{1,0:T(8,128)(2,1)} %refs_2_.4) | copy-start | bytes 12582916
  10.3 2.7 %collective-permute-start.2 = (f32[2048,128]{1,0:T(8,128)S(1)}, f32[2048,128]{1,0:T(8,128)S(1)}, u32[]{:S(2)}, u32[]{:S(2)}) collective-permute-start(f32[2048,128]{1,0:T(8,128)S(1)} %get-tuple-element.29), channel_id=1, source_target_pairs={{0,1},{1,0},{2,3},{3,2},{4,5},{5,4},{6,7},{7,6},{8,9},{9,8},{10,11... | collective-permute-start | bytes 3145736 | tf_op jit(solution)/shard_map/ppermute | solution.py:340
  10.4 2.5 %collective-permute-start.3 = (s32[1,128]{1,0:T(1,128)S(1)}, s32[1,128]{1,0:T(1,128)S(1)}, u32[]{:S(2)}, u32[]{:S(2)}) collective-permute-start(s32[1,128]{1,0:T(1,128)S(1)} %shard_map.104.refs_2_.refs_3_.refs_4_.refs_5_), channel_id=1, source_target_pairs={{0,8},{8,0},{16,24},{24,16},{1,9},{9,1},{17,25},{25,17},{2,10},{10... | collective-permute-start | bytes 1544 | tf_op jit(solution)/shard_map/ppermute | solution.py:319
  12.8 28.6 %copy-start.4 = (s32[1,128]{1,0:T(1,128)}, s32[1,128]{1,0:T(1,128)S(1)}, u32[]{:S(2)}) copy-start(s32[1,128]{1,0:T(1,128)S(1)} %collective-permute-done.3.refs_3_.refs_1_.refs_2_.refs_4_.refs_5_) | copy-start | bytes 1540
  14.1 27.4 %collective-permute-start.9 = (f32[1664,128]{1,0:T(8,128)S(1)}, f32[1664,128]{1,0:T(8,128)S(1)}, u32[]{:S(2)}, u32[]{:S(2)}) collective-permute-start(f32[1664,128]{1,0:T(8,128)S(1)} %get-tuple-element.33.refs_8_.refs_2_.refs_4_.refs_6_), channel_id=1, source_target_pairs={{24,16},{25,17},{26,18},{27,19},{28,20},{29,21},{30,22},{31,23}} | collective-permute-start | bytes 2555912 | tf_op jit(solution)/shard_map/ppermute | solution.py:421
  15.4 11.3 %collective-permute-start.4 = (f32[640,128]{1,0:T(8,128)S(1)}, f32[640,128]{1,0:T(8,128)S(1)}, u32[]{:S(2)}, u32[]{:S(2)}) collective-permute-start(f32[640,128]{1,0:T(8,128)S(1)} %get-tuple-element.30.refs_0_), channel_id=1, source_target_pairs={{0,8},{16,24},{1,9},{17,25},{2,10},{18,26},{3,11},{19,27},{4,12},{... | collective-permute-start | bytes 983048 | tf_op jit(solution)/shard_map/ppermute | solution.py:348
  19.4 10.9 %collective-permute-start.5 = (f32[512,128]{1,0:T(8,128)S(1)}, f32[512,128]{1,0:T(8,128)S(1)}, u32[]{:S(2)}, u32[]{:S(2)}) collective-permute-start(f32[512,128]{1,0:T(8,128)S(1)} %get-tuple-element.31.refs_1_), channel_id=1, source_target_pairs={{0,8},{16,24},{1,9},{17,25},{2,10},{18,26},{3,11},{19,27},{4,12},{... | collective-permute-start | bytes 786440 | tf_op jit(solution)/shard_map/ppermute | solution.py:348
  20.7 19.4 %collective-permute-start.6 = (f32[896,128]{1,0:T(8,128)S(1)}, f32[896,128]{1,0:T(8,128)S(1)}, u32[]{:S(2)}, u32[]{:S(2)}) collective-permute-start(f32[896,128]{1,0:T(8,128)S(1)} %get-tuple-element.32.refs_2_), channel_id=1, source_target_pairs={{0,8},{16,24},{1,9},{17,25},{2,10},{18,26},{3,11},{19,27},{4,12},{... | collective-permute-start | bytes 1376264 | tf_op jit(solution)/shard_map/ppermute | solution.py:348
  22.1 4.6 %collective-permute-start.7 = (s32[1,128]{1,0:T(1,128)S(1)}, s32[1,128]{1,0:T(1,128)S(1)}, u32[]{:S(2)}, u32[]{:S(2)}) collective-permute-start(s32[1,128]{1,0:T(1,128)S(1)} %shard_map.104.refs_2_.refs_3_.refs_4_.refs_5_), channel_id=1, source_target_pairs={{8,16},{9,17},{10,18},{11,19},{12,20},{13,21},{14,22},{15,23}} | collective-permute-start | bytes 1544 | tf_op jit(solution)/shard_map/ppermute | solution.py:321
  26.7 14.8 %copy-start.7 = (s32[1,128]{1,0:T(1,128)}, s32[1,128]{1,0:T(1,128)S(1)}, u32[]{:S(2)}) copy-start(s32[1,128]{1,0:T(1,128)S(1)} %collective-permute-done.7.refs_5_.refs_2_) | copy-start | bytes 1540
  27.3 12.9 %collective-permute-start.8 = (f32[640,128]{1,0:T(8,128)S(1)}, f32[640,128]{1,0:T(8,128)S(1)}, u32[]{:S(2)}, u32[]{:S(2)}) collective-permute-start(f32[640,128]{1,0:T(8,128)S(1)} %shard_map.110.refs_6_), channel_id=1, source_target_pairs={{8,16},{9,17},{10,18},{11,19},{12,20},{13,21},{14,22},{15,23}} | collective-permute-start | bytes 983048 | tf_op jit(solution)/shard_map/ppermute | solution.py:444
  31.0 16.5 %copy-start = (bf16[2048,1024]{1,0:T(8,128)(2,1)S(1)}, bf16[2048,1024]{1,0:T(8,128)(2,1)}, u32[]{:S(2)}) copy-start(bf16[2048,1024]{1,0:T(8,128)(2,1)} %refs_0_.7) | copy-start | bytes 12582916
  31.0 10.4 %collective-permute-start.11 = (f32[512,128]{1,0:T(8,128)S(1)}, f32[512,128]{1,0:T(8,128)S(1)}, u32[]{:S(2)}, u32[]{:S(2)}) collective-permute-start(f32[512,128]{1,0:T(8,128)S(1)} %shard_map.111.refs_8_), channel_id=1, source_target_pairs={{8,16},{9,17},{10,18},{11,19},{12,20},{13,21},{14,22},{15,23}} | collective-permute-start | bytes 786440 | tf_op jit(solution)/shard_map/ppermute | solution.py:444
  32.6 8.4 %collective-permute-start.10 = (f32[384,128]{1,0:T(8,128)S(1)}, f32[384,128]{1,0:T(8,128)S(1)}, u32[]{:S(2)}, u32[]{:S(2)}) collective-permute-start(f32[384,128]{1,0:T(8,128)S(1)} %get-tuple-element.35.refs_3_.refs_5_.refs_7_), channel_id=1, source_target_pairs={{24,16},{25,17},{26,18},{27,19},{28,20},{29,21},{30,22},{31,23}} | collective-permute-start | bytes 589832 | tf_op jit(solution)/shard_map/ppermute | solution.py:421
  42.3 5.1 %collective-permute-start.12 = (f32[1024,128]{1,0:T(8,128)S(1)}, f32[1024,128]{1,0:T(8,128)S(1)}, u32[]{:S(2)}, u32[]{:S(2)}) collective-permute-start(f32[1024,128]{1,0:T(8,128)S(1)} %get-tuple-element.38), channel_id=1, source_target_pairs={{0,1},{1,0},{2,3},{3,2},{4,5},{5,4},{6,7},{7,6},{8,9},{9,8},{10,11... | collective-permute-start | bytes 1572872 | tf_op jit(solution)/shard_map/ppermute | solution.py:384
  45.9 14.0 %collective-permute-start.23 = (f32[896,128]{1,0:T(8,128)S(1)}, f32[896,128]{1,0:T(8,128)S(1)}, u32[]{:S(2)}, u32[]{:S(2)}) collective-permute-start(f32[896,128]{1,0:T(8,128)S(1)} %shard_map.112.refs_7_), channel_id=1, source_target_pairs={{8,16},{9,17},{10,18},{11,19},{12,20},{13,21},{14,22},{15,23}} | collective-permute-start | bytes 1376264 | tf_op jit(solution)/shard_map/ppermute | solution.py:444
  48.2 2.8 %copy-start.3 = (bf16[1024,1024]{1,0:T(8,128)(2,1)S(1)}, bf16[1024,1024]{1,0:T(8,128)(2,1)}, u32[]{:S(2)}) copy-start(bf16[1024,1024]{1,0:T(8,128)(2,1)} %refs_6_.3) | copy-start | bytes 6291460
  48.2 2.7 %copy-start.6 = (s32[4]{0:T(128)S(1)}, s32[4]{0:T(128)}, u32[]{:S(2)}) copy-start(s32[4]{0:T(128)} %refs_2_.7) | copy-start | bytes 52
  48.2 1.6 %collective-permute-start.13 = (f32[256,256]{1,0:T(8,128)S(1)}, f32[256,256]{1,0:T(8,128)S(1)}, u32[]{:S(2)}, u32[]{:S(2)}) collective-permute-start(f32[256,256]{1,0:T(8,128)S(1)} %get-tuple-element.40), channel_id=1, source_target_pairs={{0,1},{1,0},{2,3},{3,2},{4,5},{5,4},{6,7},{7,6},{8,9},{9,8},{10,11... | collective-permute-start | bytes 786440 | tf_op jit(solution)/shard_map/ppermute | solution.py:389
  48.7 1.5 %collective-permute-start.14 = (f32[256,256]{1,0:T(8,128)S(1)}, f32[256,256]{1,0:T(8,128)S(1)}, u32[]{:S(2)}, u32[]{:S(2)}) collective-permute-start(f32[256,256]{1,0:T(8,128)S(1)} %get-tuple-element.41), channel_id=1, source_target_pairs={{0,1},{1,0},{2,3},{3,2},{4,5},{5,4},{6,7},{7,6},{8,9},{9,8},{10,11... | collective-permute-start | bytes 786440 | tf_op jit(solution)/shard_map/ppermute | solution.py:389
  48.8 1.8 %collective-permute-start.15 = (f32[256,256]{1,0:T(8,128)S(1)}, f32[256,256]{1,0:T(8,128)S(1)}, u32[]{:S(2)}, u32[]{:S(2)}) collective-permute-start(f32[256,256]{1,0:T(8,128)S(1)} %get-tuple-element.42), channel_id=1, source_target_pairs={{0,1},{1,0},{2,3},{3,2},{4,5},{5,4},{6,7},{7,6},{8,9},{9,8},{10,11... | collective-permute-start | bytes 786440 | tf_op jit(solution)/shard_map/ppermute | solution.py:389
  49.2 1.8 %collective-permute-start.16 = (f32[256,256]{1,0:T(8,128)S(1)}, f32[256,256]{1,0:T(8,128)S(1)}, u32[]{:S(2)}, u32[]{:S(2)}) collective-permute-start(f32[256,256]{1,0:T(8,128)S(1)} %get-tuple-element.43), channel_id=1, source_target_pairs={{0,1},{1,0},{2,3},{3,2},{4,5},{5,4},{6,7},{7,6},{8,9},{9,8},{10,11... | collective-permute-start | bytes 786440 | tf_op jit(solution)/shard_map/ppermute | solution.py:389
  52.3 1.4 %collective-permute-start.17 = (f32[256,128]{1,0:T(8,128)S(1)}, f32[256,128]{1,0:T(8,128)S(1)}, u32[]{:S(2)}, u32[]{:S(2)}) collective-permute-start(f32[256,128]{1,0:T(8,128)S(1)} %get-tuple-element.45), channel_id=1, source_target_pairs={{0,1},{1,0},{2,3},{3,2},{4,5},{5,4},{6,7},{7,6},{8,9},{9,8},{10,11... | collective-permute-start | bytes 393224 | tf_op jit(solution)/shard_map/ppermute | solution.py:414
  52.7 1.3 %collective-permute-start.18 = (f32[256,128]{1,0:T(8,128)S(1)}, f32[256,128]{1,0:T(8,128)S(1)}, u32[]{:S(2)}, u32[]{:S(2)}) collective-permute-start(f32[256,128]{1,0:T(8,128)S(1)} %get-tuple-element.46), channel_id=1, source_target_pairs={{0,1},{1,0},{2,3},{3,2},{4,5},{5,4},{6,7},{7,6},{8,9},{9,8},{10,11... | collective-permute-start | bytes 393224 | tf_op jit(solution)/shard_map/ppermute | solution.py:414
  52.8 1.4 %collective-permute-start.19 = (f32[256,128]{1,0:T(8,128)S(1)}, f32[256,128]{1,0:T(8,128)S(1)}, u32[]{:S(2)}, u32[]{:S(2)}) collective-permute-start(f32[256,128]{1,0:T(8,128)S(1)} %get-tuple-element.47), channel_id=1, source_target_pairs={{0,1},{1,0},{2,3},{3,2},{4,5},{5,4},{6,7},{7,6},{8,9},{9,8},{10,11... | collective-permute-start | bytes 393224 | tf_op jit(solution)/shard_map/ppermute | solution.py:414
  53.2 1.3 %collective-permute-start.20 = (f32[256,128]{1,0:T(8,128)S(1)}, f32[256,128]{1,0:T(8,128)S(1)}, u32[]{:S(2)}, u32[]{:S(2)}) collective-permute-start(f32[256,128]{1,0:T(8,128)S(1)} %get-tuple-element.48), channel_id=1, source_target_pairs={{0,1},{1,0},{2,3},{3,2},{4,5},{5,4},{6,7},{7,6},{8,9},{9,8},{10,11... | collective-permute-start | bytes 393224 | tf_op jit(solution)/shard_map/ppermute | solution.py:414
  55.4 15.8 %collective-permute-start.21 = (f32[1024,128]{1,0:T(8,128)}, f32[1024,128]{1,0:T(8,128)}, u32[]{:S(2)}, u32[]{:S(2)}) collective-permute-start(f32[1024,128]{1,0:T(8,128)} %shard_map.117.refs_13_), channel_id=1, source_target_pairs={{8,16},{9,17},{10,18},{11,19},{12,20},{13,21},{14,22},{15,23}} | collective-permute-start | bytes 1572872 | tf_op jit(solution)/shard_map/ppermute | solution.py:468
  56.7 15.6 %collective-permute-start.22 = (f32[1024,128]{1,0:T(8,128)}, f32[1024,128]{1,0:T(8,128)}, u32[]{:S(2)}, u32[]{:S(2)}) collective-permute-start(f32[1024,128]{1,0:T(8,128)} %shard_map.117.refs_13_), channel_id=1, source_target_pairs={{24,16},{25,17},{26,18},{27,19},{28,20},{29,21},{30,22},{31,23}} | collective-permute-start | bytes 1572872 | tf_op jit(solution)/shard_map/ppermute | solution.py:468
  59.9 12.3 %copy-start.5 = (s32[1,128]{1,0:T(1,128)S(1)}, s32[1,128]{1,0:T(1,128)}, u32[]{:S(2)}) copy-start(s32[1,128]{1,0:T(1,128)} %copy-done.4) | copy-start | bytes 1540
  59.9 12.3 %copy-start.8 = (s32[1,128]{1,0:T(1,128)S(1)}, s32[1,128]{1,0:T(1,128)}, u32[]{:S(2)}) copy-start(s32[1,128]{1,0:T(1,128)} %copy-done.7) | copy-start | bytes 1540
  73.8 2.6 %collective-permute-start.24 = (f32[1024,128]{1,0:T(8,128)S(1)}, f32[1024,128]{1,0:T(8,128)S(1)}, u32[]{:S(2)}, u32[]{:S(2)}) collective-permute-start(f32[1024,128]{1,0:T(8,128)S(1)} %get-tuple-element.50), channel_id=1, source_target_pairs={{0,1},{1,0},{2,3},{3,2},{4,5},{5,4},{6,7},{7,6},{8,9},{9,8},{10,11... | collective-permute-start | bytes 1572872 | tf_op jit(solution)/shard_map/ppermute | solution.py:384
  77.2 2.7 %collective-permute-start.25 = (f32[1024,256]{1,0:T(8,128)S(1)}, f32[1024,256]{1,0:T(8,128)S(1)}, u32[]{:S(2)}, u32[]{:S(2)}) collective-permute-start(f32[1024,256]{1,0:T(8,128)S(1)} %get-tuple-element.52), channel_id=1, source_target_pairs={{0,1},{1,0},{2,3},{3,2},{4,5},{5,4},{6,7},{7,6},{8,9},{9,8},{10,11... | collective-permute-start | bytes 3145736 | tf_op jit(solution)/shard_map/ppermute | solution.py:389

commit v3 on v2

--- a/solution.py
+++ b/solution.py
@@ -10,14 +10,15 @@
 PANEL = 128
 TILE = 256
 TAGS = 128
+COPIED = 32
+PAD = 8
 COST = 1000
 CUTS, PARTS = (0, 5, 9, 16), 16
 VMEM_MIB = 8
 LEAF_COST = 2 * 10**9
-OWN_PART = 13
 SPLIT = 4
-PINNED = 2
-BASE_COST = 10**12
+RELAY_COSTS = (10**9, 1000, 1000)
+BASE_COST = 53 * 10**8
 F32 = jnp.float32
 BF16 = jnp.bfloat16
 ANY = pl.BlockSpec(memory_space=pl.ANY)
@@ -105,6 +106,11 @@
     @pl.when(lax.axis_index("col") != 0)
     def _():
         product(piece)
+
+
+def copy_tags_kernel(tags, out):
+    for j in range(COPIED):
+        out[0, j] = tags[0, j]
 
 
 def leaf_sum(diag, other):
@@ -269,12 +275,16 @@
 
 
 def sum_parts_kernel(whole, *refs):
-    *parts, out = refs
+    *parts, out, again, token = refs
+    token[...] = whole[0:8]
     at = 0
     for part in parts:
         here = slice(at, at + part.shape[0])
-        out[here] = whole[here] + part[...]
+        total = whole[here] + part[...]
+        out[here] = total
+        again[here] = total
         at += part.shape[0]
+    out[at:] = jnp.zeros((out.shape[0] - at, out.shape[1]), F32)
 
 
 def sum_two(one, two):
@@ -318,7 +328,6 @@
 
     tags_swap = lax.ppermute(tags, "leaf", [(i, i ^ 1) for i in range(leaves)])
     up = [(a - 1, a) for a in range(2, leaves, 4)]
-    tags_up = lax.ppermute(tags, "leaf", up)
 
     rhs_out = jnp.where(col == 0, sep_rhs[:, half:], sep_rhs[:, :half]).astype(F32)
     rhs_theirs = lax.ppermute(rhs_out, "col", swap)
@@ -334,20 +343,19 @@
         (VMEM,) * 2,
         after=[rhs_theirs],
     )
-    own_rows = sep_panels * OWN_PART // PARTS * PANEL
     got = call(
         functools.partial(gather_kernel, counts),
         (keep, lax.ppermute(send, "col", swap), tags),
         [VMEM] * 2 + [SMEM],
-        (*(shape(count * PANEL, half) for first, count in counts), shape(own_rows, half), shape(sep_cols - own_rows, half)),
-        (VMEM,) * (chunks + 2),
+        (*(shape(count * PANEL, half) for first, count in counts), shape(sep_cols + PAD, half)),
+        (VMEM,) * (chunks + 1),
         after=[tags_swap],
     )
     mine, own = list(got[:chunks]), list(got[chunks:])
 
     theirs = [lax.ppermute(one, "leaf", [(i, i + 1) for i in range(0, leaves, 2)]) for one in mine]
 
-    def scatter(rows, base, arrays, tag_list, firsts, dense, start, after):
+    def scatter(rows, base, arrays, tag_list, firsts, dense, start, after, flops=COST):
         return call(
             functools.partial(scatter_kernel, base, firsts, start),
             (*arrays, *tag_list, *dense),
@@ -355,6 +363,7 @@
             shape(rows, half),
             VMEM,
             after=after,
+            flops=flops,
         )
 
     def right_side(base, arrays, tag_list, firsts, dense, after, flops=COST):
@@ -368,7 +377,7 @@
             flops=flops,
         )
 
-    def solve(level, arrays, tag_list, firsts, base, right, before, after, after_late=(), split=1):
+    def solve(level, arrays, tag_list, firsts, base, right, before, after, after_across=(), split=1):
         update = level < levels
         keep, send = call(
             functools.partial(residual_kernel, base, firsts),
@@ -385,6 +394,7 @@
             [VMEM] * 3,
             (shape(sep_piece, width_rhs, BF16), *(shape(sep_piece // split, width_rhs),) * split),
             (VMEM,) * (1 + split),
+            after=after_across,
         )
         other = [lax.ppermute(one, "col", swap) for one in across]
         diag = call(
@@ -410,26 +420,22 @@
             (VMEM,) * len(outs),
         )
         if not update:
-            return got[0], None
+            return got[0], (None, None)
         there = [lax.ppermute(one, "col", swap) for one in got[2:]]
-        total = call(
-            sum_parts_kernel, (got[1], *there), [VMEM] * (1 + split), shape(*got[1].shape), VMEM, after=after_late
-        )
-        return got[0], total
+        rows = got[1].shape[0]
+        *total, token = call(
+            sum_parts_kernel,
+            (got[1], *there),
+            [VMEM] * (1 + split),
+            (shape(rows + PAD, half), shape(rows, half), shape(8, half)),
+            (VMEM,) * 3,
+        )
+        return got[0], (total, token)
 
     down = [(i + 1, i) for i in range(2, leaves, 4)]
     own_right = [lax.ppermute(one, "leaf", down) for one in own]
-    right = right_side((levels - 1) * sep_panels, mine, [tags] * chunks, counts, [], own[:1])
-    leaf_solution, last = call(
-        sum_kernel,
-        (diag, other),
-        [VMEM] * 2,
-        (shape(piece, width_rhs, BF16), shape(8, 128)),
-        (VMEM, VMEM),
-        after=[right],
-    )
-
     came = []
+    last = own[0]
     for n in range(chunks):
         one = scatter(
             counts[n][1] * PANEL,
@@ -439,13 +445,24 @@
             counts[: n + 1],
             own,
             starts[n] * PANEL,
-            [last, tags_up] if n == 0 else [last, *came[: n - 1]],
+            [last, *came[: max(n - 1, 0)]],
+            RELAY_COSTS[n],
         )
         came.append(lax.ppermute(one, "leaf", up))
         last = one
-    pinned = [last, *own_right[:PINNED], *came[:-1]]
-    held, update = solve(
-        1, theirs, [tags_swap] * chunks, counts, (levels - 1) * sep_panels, right, None, pinned, [], SPLIT
+        if n == 0:
+            right = right_side((levels - 1) * sep_panels, mine, [tags] * chunks, counts, [], own[:1])
+            leaf_solution, last = call(
+                sum_kernel,
+                (diag, other),
+                [VMEM] * 2,
+                (shape(piece, width_rhs, BF16), shape(8, 128)),
+                (VMEM, VMEM),
+                after=[right],
+            )
+    pinned = [last, *came[:-1]]
+    held, (update, token) = solve(
+        1, theirs, [tags_swap] * chunks, counts, (levels - 1) * sep_panels, right, None, pinned, own_right, SPLIT
     )
     above_left = above_right = None
     if levels > 2:
@@ -459,15 +476,18 @@
         pairs = [[(a - step, a) for a in owners], [(a + step, a) for a in owners]]
         base = (level - 2) * sep_panels
         if level == 2:
-            dense, tag_pair = [*came, *own_right], [tags_up, tags_swap]
+            dense, tag_pair = [*came, *own_right], [None, tags_swap]
             own_rows, own_tags, own_counts = mine, [tags] * chunks, counts
         else:
             dense = [lax.ppermute(dense_now, "leaf", one) for one in pairs]
             tag_pair = [lax.ppermute(tags, "leaf", one) for one in pairs]
             own_rows, own_tags, own_counts = [], [], []
-        came_update = [lax.ppermute(update, "leaf", one) for one in pairs]
+        came_update = [lax.ppermute(rows, "leaf", one) for rows, one in zip(update, pairs)]
         firsts = [(n_leaf, n_sep)] * 2
-        right = right_side(base, own_rows, own_tags, own_counts, dense, [update], BASE_COST)
+        right = right_side(base, own_rows, own_tags, own_counts, dense, [token], BASE_COST)
+        if level == 2:
+            late = call(copy_tags_kernel, (tags,), [SMEM], shape(1, TAGS, jnp.int32), SMEM, after=[right])
+            tag_pair[0] = lax.ppermute(late, "leaf", up)
         if level < levels:
             parts = (above_left, above_right) if level == 2 else (above_now, above_now)
             parts = [lax.ppermute(part, "leaf", one) for part, one in zip(parts, pairs)]
@@ -483,7 +503,7 @@
                 [],
             )
             dense_now, above_now = total[:sep_cols], total[sep_cols:]
-        held, update = solve(level, came_update, tag_pair, firsts, base, right, held, [])
+        held, (update, token) = solve(level, came_update, tag_pair, firsts, base, right, held, [])
     return leaf_solution, held
 
 

time: 81.7 us -> 77.2 us (0.945)
  waiting for transfers between devices: 30.6 us -> 27 us
    ppermute x3, waiting for transfers between devices: 12.8 us -> 7.77 us  [the longest x1 7.76 us: on_device(): tag_pair[0] = lax.ppermute(late, 'leaf', up)]
    ppermute x3, starting transfers between devices: 6.68 us -> 8.6 us  [on_device(): lax.ppermute(one, 'leaf', [(i, i + 1) for i in range(0, leaves, 2)])]
    ppermute x2 -> x1, starting transfers between devices: 2.58 us -> 1.29 us  [on_device(): own_right = [lax.ppermute(one, 'leaf', down) for one in own]]
    ppermute x2, starting transfers between devices: 4.63 us -> 3.57 us  [solve(): lax.ppermute(send, 'col', swap)]
    ppermute x3, waiting for transfers between devices: 8.07 us -> 9.01 us  [on_device(): lax.ppermute(one, 'leaf', [(i, i + 1) for i in range(0, leaves, 2)])]
    pallas_call x19 -> x20, Pallas kernels: 18.5 us -> 18.2 us  [call(): pl.pallas_call(trimmed, out_shape=outs, in_specs=list(specs) + [ANY] * ex...]
    unnamed x26 -> x18, local copies, waits for them, and re-layouts: 2.08 us -> 2.06 us
  transfers between devices with their start and end apart: 26 -> 25, of which waited for: 20 -> 18; matrix products, arithmetic and copies ran while one was open for 0% -> 0% of each run, Pallas kernels for 13% -> 16%
where the time goes in v3:
time: 77.2 us; the launch traced here: 76.9 us
  waiting for transfers between devices  27 us (35%)
  starting transfers between devices  26.1 us (34%)
  Pallas kernels  18.2 us (24%)
  matrix products  2.44 us (3%)
  local copies, waits for them, and re-layouts  2.06 us (3%)
  between operations  0.95 us (1%)
    pallas_call x20, Pallas kernels, call(): pl.pallas_call(trimmed, out_shape=outs, in_specs=list(specs) + [ANY] * ex...  18.2 us
    ppermute x3, waiting for transfers between devices, on_device(): lax.ppermute(one, 'leaf', [(i, i + 1) for i in range(0, leaves, 2)])  9.01 us
    ppermute x3, starting transfers between devices, on_device(): lax.ppermute(one, 'leaf', [(i, i + 1) for i in range(0, leaves, 2)])  8.6 us
    ppermute x1, waiting for transfers between devices, on_device(): tag_pair[0] = lax.ppermute(late, 'leaf', up)  7.76 us
    ppermute x3, starting transfers between devices, on_device(): came.append(lax.ppermute(one, 'leaf', up))  3.86 us
    ppermute x2, starting transfers between devices, solve(): lax.ppermute(send, 'col', swap)  3.57 us
    ppermute x3, waiting for transfers between devices, on_device(): came.append(lax.ppermute(one, 'leaf', up))  3.03 us
    ppermute x5, waiting for transfers between devices, solve(): other = [lax.ppermute(one, 'col', swap) for one in across]  2.81 us
  transfers between devices with their start and end apart: 25, of which 18 were waited for; matrix products, arithmetic and copies ran while one was open for 0% of the time, Pallas kernels for 16%

profile of v3, /device:TPU:21, one launch (start us, length us, event | category | flops | bytes accessed | tf_op | source)
XLA Modules:
  0.0 76.9 jit_solution(12027784015261127279)
XLA Ops:
  0.7 2.4 %fusion.refs_2_ = f32[1024,256]{1,0:T(8,128)S(1)} fusion(bf16[1024,256]{1,0:T(8,128)(2,1)} %refs_1_.3, bf16[2048,1024]{1,0:T(8,128)(2,1)} %refs_0_.5), kind=kOutput, calls=%fused_computation | convolution fusion | flops 536870912 | bytes 3670016 | tf_op jit(solution)/shard_map/dot_general | solution.py:31
  3.1 0.7 collective-permute-start
  4.0 1.5 %shard_map.104.refs_2_.refs_3_.refs_4_.refs_5_.refs_0_ = s32[1,128]{1,0:T(1,128)S(1)} custom-call(s32[1,16]{1,0:T(1,128)S(1)} %copy-done.7, s32[1,8]{1,0:T(1,128)S(1)} %copy-done.8, f32[1024,256]{1,0:T(8,128)S(1)} %fusion.refs_2_), custom_call_target="tpu_custom_call" | custom-call | flops 2000000000 | bytes 1 | tf_op jit(solution)/shard_map/pallas_call | solution.py:40
  5.6 0.5 copy-done.5
  6.2 0.6 shard_map.105.refs_0_
  6.9 1.5 %copy-done.1 = bf16[2048,1024]{1,0:T(8,128)(2,1)S(1)} copy-done((bf16[2048,1024]{1,0:T(8,128)(2,1)S(1)}, bf16[2048,1024]{1,0:T(8,128)(2,1)}, u32[]{:S(2)}) %copy-start.1) | copy-done | bytes 4194328
  8.3 1.9 %shard_map.106 = (f32[2048,128]{1,0:T(8,128)S(1)}, f32[2048,128]{1,0:T(8,128)S(1)}) custom-call(f32[1024,256]{1,0:T(8,128)S(1)} %shard_map.105.refs_0_, f32[1024,256]{1,0:T(8,128)S(1)} %collective-permute-done.refs_1_, bf16[2048,1024]{1,0:T(8,128)(2,1)S(1)} %copy-done.1, s32[1,128]{1,0:T(1,128)S(1)} %shard_map.104.refs_2_.refs_3_.refs_4_.refs_5_.refs_0_, ...), custom_call_target="tpu_custom_call" | custom-call | flops 1000 | bytes 1 | tf_op jit(solution)/shard_map/pallas_call | solution.py:40
  10.4 1.4 %collective-permute-start.3 = (s32[1,128]{1,0:T(1,128)S(1)}, s32[1,128]{1,0:T(1,128)S(1)}, u32[]{:S(2)}, u32[]{:S(2)}) collective-permute-start(s32[1,128]{1,0:T(1,128)S(1)} %shard_map.104.refs_2_.refs_3_.refs_4_.refs_5_.refs_0_), channel_id=1, source_target_pairs={{0,8},{8,0},{16,24},{24,16},{1,9},{9,1},{17,25},{25,17},{2,10},{10... | collective-permute-start | bytes 1544 | tf_op jit(solution)/shard_map/ppermute | solution.py:329
  11.7 1.1 %collective-permute-done.3.refs_3_.refs_2_.refs_1_.refs_4_.refs_5_ = s32[1,128]{1,0:T(1,128)S(1)} collective-permute-done((s32[1,128]{1,0:T(1,128)S(1)}, s32[1,128]{1,0:T(1,128)S(1)}, u32[]{:S(2)}, u32[]{:S(2)}) %collective-permute-start.3) | collective-permute-done | bytes 544 | tf_op jit(solution)/shard_map/ppermute | solution.py:329
  13.0 0.9 %shard_map.107 = (f32[640,128]{1,0:T(8,128)S(1)}, f32[512,128]{1,0:T(8,128)S(1)}, f32[896,128]{1,0:T(8,128)S(1)}, f32[2056,128]{1,0:T(8,128)S(1)}) custom-call(f32[2048,128]{1,0:T(8,128)S(1)} %get-tuple-element.30.refs_0_, f32[2048,128]{1,0:T(8,128)S(1)} %collective-permute-done.2.refs_1_, s32[1,128]{1,0:T(1,128)S(1)} %shard_map.104.refs_2_.refs_3_.refs_4_.refs_5_.refs_0_, ...), custom_call_target="tpu_custom_call" | custom-call | flops 1000 | bytes 1 | tf_op jit(solution)/shard_map/pallas_call | solution.py:40
  13.9 3.2 %collective-permute-start.4 = (f32[640,128]{1,0:T(8,128)S(1)}, f32[640,128]{1,0:T(8,128)S(1)}, u32[]{:S(2)}, u32[]{:S(2)}) collective-permute-start(f32[640,128]{1,0:T(8,128)S(1)} %get-tuple-element.32.refs_0_), channel_id=1, source_target_pairs={{0,8},{16,24},{1,9},{17,25},{2,10},{18,26},{3,11},{19,27},{4,12},{... | collective-permute-start | bytes 983048 | tf_op jit(solution)/shard_map/ppermute | solution.py:356
  17.2 1.3 %collective-permute-start.10 = (f32[2056,128]{1,0:T(8,128)S(1)}, f32[2056,128]{1,0:T(8,128)S(1)}, u32[]{:S(2)}, u32[]{:S(2)}) collective-permute-start(f32[2056,128]{1,0:T(8,128)S(1)} %get-tuple-element.35.refs_8_.refs_4_.refs_2_.refs_3_.refs_6_), channel_id=1, source_target_pairs={{24,16},{25,17},{26,18},{27,19},{28,20},{29,21},{30,22},{31,23}} | collective-permute-start | bytes 3158024 | tf_op jit(solution)/shard_map/ppermute | solution.py:436
  18.5 4.1 %collective-permute-start.5 = (f32[512,128]{1,0:T(8,128)S(1)}, f32[512,128]{1,0:T(8,128)S(1)}, u32[]{:S(2)}, u32[]{:S(2)}) collective-permute-start(f32[512,128]{1,0:T(8,128)S(1)} %get-tuple-element.33.refs_1_), channel_id=1, source_target_pairs={{0,8},{16,24},{1,9},{17,25},{2,10},{18,26},{3,11},{19,27},{4,12},{... | collective-permute-start | bytes 786440 | tf_op jit(solution)/shard_map/ppermute | solution.py:356
  22.5 1.3 %collective-permute-start.6 = (f32[896,128]{1,0:T(8,128)S(1)}, f32[896,128]{1,0:T(8,128)S(1)}, u32[]{:S(2)}, u32[]{:S(2)}) collective-permute-start(f32[896,128]{1,0:T(8,128)S(1)} %get-tuple-element.34.refs_2_), channel_id=1, source_target_pairs={{0,8},{16,24},{1,9},{17,25},{2,10},{18,26},{3,11},{19,27},{4,12},{... | collective-permute-start | bytes 1376264 | tf_op jit(solution)/shard_map/ppermute | solution.py:356
  23.9 0.6 shard_map.111
  24.5 1.3 %collective-permute-start.7 = (f32[640,128]{1,0:T(8,128)S(1)}, f32[640,128]{1,0:T(8,128)S(1)}, u32[]{:S(2)}, u32[]{:S(2)}) collective-permute-start(f32[640,128]{1,0:T(8,128)S(1)} %shard_map.111), channel_id=1, source_target_pairs={{8,16},{9,17},{10,18},{11,19},{12,20},{13,21},{14,22},{15,23}} | collective-permute-start | bytes 983048 | tf_op jit(solution)/shard_map/ppermute | solution.py:451
  25.8 0.8 %shard_map.108.refs_2_.refs_6_ = f32[2048,128]{1,0:T(8,128)S(1)} custom-call(f32[640,128]{1,0:T(8,128)S(1)} %get-tuple-element.32.refs_0_, f32[512,128]{1,0:T(8,128)S(1)} %get-tuple-element.33.refs_1_, f32[896,128]{1,0:T(8,128)S(1)} %get-tuple-element.34.refs_2_, s32[1,128]{1,0:T(1,128)S(1)} %shard_map.104.refs_2_.refs_3_.refs_4_.refs_5_.refs_0_, ...), custom_call_target="tpu_custom_call" | custom-call | flops 1000 | bytes 1 | tf_op jit(solution)/shard_map/pallas_call | solution.py:40
  26.6 0.9 %shard_map.109 = (bf16[1024,256]{1,0:T(8,128)(2,1)}, f32[8,128]{1,0:T(8,128)S(1)}) custom-call(f32[1024,256]{1,0:T(8,128)S(1)} %shard_map.105.refs_0_, f32[1024,256]{1,0:T(8,128)S(1)} %collective-permute-done.refs_1_, f32[2048,128]{1,0:T(8,128)S(1)} %shard_map.108.refs_2_.refs_6_), custom_call_target="tpu_custom_call" | custom-call | flops 1000 | bytes 1 | tf_op jit(solution)/shard_map/pallas_call | solution.py:40
  27.6 1.1 %collective-permute-done.5.refs_1_ = f32[512,128]{1,0:T(8,128)S(1)} collective-permute-done((f32[512,128]{1,0:T(8,128)S(1)}, f32[512,128]{1,0:T(8,128)S(1)}, u32[]{:S(2)}, u32[]{:S(2)}) %collective-permute-start.5) | collective-permute-done | bytes 262176 | tf_op jit(solution)/shard_map/ppermute | solution.py:356
  28.7 0.6 shard_map.110.refs_7_
  29.4 1.3 %collective-permute-start.8 = (f32[512,128]{1,0:T(8,128)S(1)}, f32[512,128]{1,0:T(8,128)S(1)}, u32[]{:S(2)}, u32[]{:S(2)}) collective-permute-start(f32[512,128]{1,0:T(8,128)S(1)} %shard_map.110.refs_7_), channel_id=1, source_target_pairs={{8,16},{9,17},{10,18},{11,19},{12,20},{13,21},{14,22},{15,23}} | collective-permute-start | bytes 786440 | tf_op jit(solution)/shard_map/ppermute | solution.py:451
  30.7 7.9 %collective-permute-done.6.refs_2_ = f32[896,128]{1,0:T(8,128)S(1)} collective-permute-done((f32[896,128]{1,0:T(8,128)S(1)}, f32[896,128]{1,0:T(8,128)S(1)}, u32[]{:S(2)}, u32[]{:S(2)}) %collective-permute-start.6) | collective-permute-done | bytes 458784 | tf_op jit(solution)/shard_map/ppermute | solution.py:356
  38.5 0.7 shard_map.112.refs_7_
  39.6 0.9 %shard_map.113 = (f32[1024,128]{1,0:T(8,128)S(1)}, f32[1024,128]{1,0:T(8,128)S(1)}) custom-call(f32[640,128]{1,0:T(8,128)S(1)} %collective-permute-done.4.refs_0_, f32[512,128]{1,0:T(8,128)S(1)} %collective-permute-done.5.refs_1_, f32[896,128]{1,0:T(8,128)S(1)} %collective-permute-done.6.refs_2_, ...), custom_call_target="tpu_custom_call" | custom-call | flops 1000 | bytes 1 | tf_op jit(solution)/shard_map/pallas_call | solution.py:40
  40.5 2.6 %collective-permute-start.9 = (f32[1024,128]{1,0:T(8,128)S(1)}, f32[1024,128]{1,0:T(8,128)S(1)}, u32[]{:S(2)}, u32[]{:S(2)}) collective-permute-start(f32[1024,128]{1,0:T(8,128)S(1)} %get-tuple-element.39), channel_id=1, source_target_pairs={{0,1},{1,0},{2,3},{3,2},{4,5},{5,4},{6,7},{7,6},{8,9},{9,8},{10,11... | collective-permute-start | bytes 1572872 | tf_op jit(solution)/shard_map/ppermute | solution.py:393
  43.1 1.3 %collective-permute-start.21 = (f32[896,128]{1,0:T(8,128)S(1)}, f32[896,128]{1,0:T(8,128)S(1)}, u32[]{:S(2)}, u32[]{:S(2)}) collective-permute-start(f32[896,128]{1,0:T(8,128)S(1)} %shard_map.112.refs_7_), channel_id=1, source_target_pairs={{8,16},{9,17},{10,18},{11,19},{12,20},{13,21},{14,22},{15,23}} | collective-permute-start | bytes 1376264 | tf_op jit(solution)/shard_map/ppermute | solution.py:451
  44.6 0.7 shard_map.114
  45.4 0.5 collective-permute-start.11
  46.0 0.4 collective-permute-start.13
  46.5 0.6 shard_map.115.refs_0_
  47.4 0.4 collective-permute-done.13.refs_3_
  48.1 1.3 %shard_map.116 = (bf16[1024,256]{1,0:T(8,128)(2,1)S(1)}, f32[1024,128]{1,0:T(8,128)S(1)}, f32[256,128]{1,0:T(8,128)S(1)}, f32[256,128]{1,0:T(8,128)S(1)}, f32[25...) custom-call(f32[1024,256]{1,0:T(8,128)S(1)} %shard_map.115.refs_0_, f32[256,256]{1,0:T(8,128)S(1)} %collective-permute-done.11.refs_1_, ...), custom_call_target="tpu_custom_call" | custom-call | flops 1000 | bytes 1 | tf_op jit(solution)/shard_map/pallas_call | solution.py:40
  49.5 0.4 collective-permute-start.15
  51.8 1.3 %collective-permute-start.19 = (f32[1032,128]{1,0:T(8,128)S(1)}, f32[1032,128]{1,0:T(8,128)S(1)}, u32[]{:S(2)}, u32[]{:S(2)}) collective-permute-start(f32[1032,128]{1,0:T(8,128)S(1)} %get-tuple-element.50), channel_id=1, source_target_pairs={{8,16},{9,17},{10,18},{11,19},{12,20},{13,21},{14,22},{15,23}} | collective-permute-start | bytes 1585160 | tf_op jit(solution)/shard_map/ppermute | solution.py:485
  53.1 1.3 %collective-permute-start.20 = (f32[1024,128]{1,0:T(8,128)S(1)}, f32[1024,128]{1,0:T(8,128)S(1)}, u32[]{:S(2)}, u32[]{:S(2)}) collective-permute-start(f32[1024,128]{1,0:T(8,128)S(1)} %get-tuple-element.51), channel_id=1, source_target_pairs={{24,16},{25,17},{26,18},{27,19},{28,20},{29,21},{30,22},{31,23}} | collective-permute-start | bytes 1572872 | tf_op jit(solution)/shard_map/ppermute | solution.py:485
  54.4 2.7 %collective-permute-done.21.refs_8_ = f32[896,128]{1,0:T(8,128)S(1)} collective-permute-done((f32[896,128]{1,0:T(8,128)S(1)}, f32[896,128]{1,0:T(8,128)S(1)}, u32[]{:S(2)}, u32[]{:S(2)}) %collective-permute-start.21) | collective-permute-done | bytes 458784 | tf_op jit(solution)/shard_map/ppermute | solution.py:451
  57.1 1.1 %shard_map.118.refs_1_.refs_4_ = f32[2048,128]{1,0:T(8,128)S(1)} custom-call(f32[640,128]{1,0:T(8,128)S(1)} %get-tuple-element.32.refs_0_, f32[512,128]{1,0:T(8,128)S(1)} %get-tuple-element.33.refs_1_, f32[896,128]{1,0:T(8,128)S(1)} %get-tuple-element.34.refs_2_, s32[1,128]{1,0:T(1,128)S(1)} %shard_map.104.refs_2_.refs_3_.refs_4_.refs_5_.refs_0_, ...), custom_call_target="tpu_custom_call" | custom-call | flops 5299999744 | bytes 1 | tf_op jit(solution)/shard_map/pallas_call | solution.py:40
  58.2 1.2 %shard_map.119 = s32[1,128]{1,0:T(1,128)S(1)} custom-call(s32[1,128]{1,0:T(1,128)S(1)} %shard_map.104.refs_2_.refs_3_.refs_4_.refs_5_.refs_0_, f32[2048,128]{1,0:T(8,128)S(1)} %shard_map.118.refs_1_.refs_4_), custom_call_target="tpu_custom_call" | custom-call | flops 1000 | bytes 1 | tf_op jit(solution)/shard_map/pallas_call | solution.py:40
  59.4 1.3 %collective-permute-start.22 = (s32[1,128]{1,0:T(1,128)S(1)}, s32[1,128]{1,0:T(1,128)S(1)}, u32[]{:S(2)}, u32[]{:S(2)}) collective-permute-start(s32[1,128]{1,0:T(1,128)S(1)} %shard_map.119), channel_id=1, source_target_pairs={{8,16},{9,17},{10,18},{11,19},{12,20},{13,21},{14,22},{15,23}} | collective-permute-start | bytes 1544 | tf_op jit(solution)/shard_map/ppermute | solution.py:490
  60.7 7.8 %collective-permute-done.22.refs_2_ = s32[1,128]{1,0:T(1,128)S(1)} collective-permute-done((s32[1,128]{1,0:T(1,128)S(1)}, s32[1,128]{1,0:T(1,128)S(1)}, u32[]{:S(2)}, u32[]{:S(2)}) %collective-permute-start.22) | collective-permute-done | bytes 544 | tf_op jit(solution)/shard_map/ppermute | solution.py:490
  68.4 0.9 %shard_map.120 = (f32[1024,128]{1,0:T(8,128)S(1)}, f32[1024,128]{1,0:T(8,128)S(1)}) custom-call(f32[1032,128]{1,0:T(8,128)S(1)} %collective-permute-done.19.refs_0_, f32[1024,128]{1,0:T(8,128)S(1)} %collective-permute-done.20.refs_1_, s32[1,128]{1,0:T(1,128)S(1)} %collective-permute-done.22.refs_2_, ...), custom_call_target="tpu_custom_call" | custom-call | flops 1000 | bytes 1 | tf_op jit(solution)/shard_map/pallas_call | solution.py:40
  69.3 1.0 %collective-permute-start.23 = (f32[1024,128]{1,0:T(8,128)S(1)}, f32[1024,128]{1,0:T(8,128)S(1)}, u32[]{:S(2)}, u32[]{:S(2)}) collective-permute-start(f32[1024,128]{1,0:T(8,128)S(1)} %get-tuple-element.54), channel_id=1, source_target_pairs={{0,1},{1,0},{2,3},{3,2},{4,5},{5,4},{6,7},{7,6},{8,9},{9,8},{10,11... | collective-permute-start | bytes 1572872 | tf_op jit(solution)/shard_map/ppermute | solution.py:393
  70.3 1.5 %collective-permute-done.23.refs_1_ = f32[1024,128]{1,0:T(8,128)S(1)} collective-permute-done((f32[1024,128]{1,0:T(8,128)S(1)}, f32[1024,128]{1,0:T(8,128)S(1)}, u32[]{:S(2)}, u32[]{:S(2)}) %collective-permute-start.23) | collective-permute-done | bytes 524320 | tf_op jit(solution)/shard_map/ppermute | solution.py:393
  71.9 0.8 %shard_map.121 = (bf16[1024,256]{1,0:T(8,128)(2,1)S(1)}, f32[1024,256]{1,0:T(8,128)S(1)}) custom-call(f32[1024,128]{1,0:T(8,128)S(1)} %get-tuple-element.53.refs_0_, f32[1024,128]{1,0:T(8,128)S(1)} %collective-permute-done.23.refs_1_, bf16[2048,1024]{1,0:T(8,128)(2,1)S(1)} %copy-done), custom_call_target="tpu_custom_call" | custom-call | flops 1000 | bytes 1 | tf_op jit(solution)/shard_map/pallas_call | solution.py:40
  72.7 0.4 collective-permute-start.24
  73.1 0.6 shard_map.122.refs_0_
  73.6 1.7 %collective-permute-done.24.refs_1_ = f32[1024,256]{1,0:T(8,128)S(1)} collective-permute-done((f32[1024,256]{1,0:T(8,128)S(1)}, f32[1024,256]{1,0:T(8,128)S(1)}, u32[]{:S(2)}, u32[]{:S(2)}) %collective-permute-start.24) | collective-permute-done | bytes 1048608 | tf_op jit(solution)/shard_map/ppermute | solution.py:399
  75.4 1.5 %shard_map.123 = bf16[1024,256]{1,0:T(8,128)(2,1)} custom-call(f32[1024,256]{1,0:T(8,128)S(1)} %shard_map.122.refs_0_, f32[1024,256]{1,0:T(8,128)S(1)} %collective-permute-done.24.refs_1_, s32[4]{0:T(128)S(1)} %copy-done.4, bf16[1024,256]{1,0:T(8,128)(2,1)S(1)} %get-tuple-element.57.refs_3_), custom_call_target="tpu_custom_call" | custom-call | flops 1000 | bytes 1 | tf_op jit(solution)/shard_map/pallas_call | solution.py:40
  (42 shorter events, 4.2 us)
Async XLA Ops:
  0.6 3.2 %copy-start.3 = (bf16[1024,256]{1,0:T(8,128)(2,1)S(1)}, bf16[1024,256]{1,0:T(8,128)(2,1)}, u32[]{:S(2)}) copy-start(bf16[1024,256]{1,0:T(8,128)(2,1)} %refs_10_.1) | copy-start | bytes 1572868
  0.6 3.4 %copy-start.8 = (s32[1,8]{1,0:T(1,128)S(1)}, s32[1,8]{1,0:T(1,128)}, u32[]{:S(2)}) copy-start(s32[1,8]{1,0:T(1,128)} %refs_1_.2) | copy-start | bytes 100
  0.7 3.4 %copy-start.7 = (s32[1,16]{1,0:T(1,128)S(1)}, s32[1,16]{1,0:T(1,128)}, u32[]{:S(2)}) copy-start(s32[1,16]{1,0:T(1,128)} %refs_0_.4) | copy-start | bytes 196
  3.1 3.8 %collective-permute-start = (f32[1024,256]{1,0:T(8,128)S(1)}, f32[1024,256]{1,0:T(8,128)S(1)}, u32[]{:S(2)}, u32[]{:S(2)}) collective-permute-start(f32[1024,256]{1,0:T(8,128)S(1)} %fusion.refs_2_), channel_id=1, source_target_pairs={{0,1},{1,0},{2,3},{3,2},{4,5},{5,4},{6,7},{7,6},{8,9},{9,8},{10,11... | collective-permute-start | bytes 3145736 | tf_op jit(solution)/shard_map/ppermute | solution.py:309
  3.9 2.2 %copy-start.5 = (bf16[2048,1024]{1,0:T(8,128)(2,1)S(1)}, bf16[2048,1024]{1,0:T(8,128)(2,1)}, u32[]{:S(2)}) copy-start(bf16[2048,1024]{1,0:T(8,128)(2,1)} %refs_0_.5) | copy-start | bytes 12582916
  3.9 2.3 %copy-start.6 = (bf16[1024,256]{1,0:T(8,128)(2,1)S(1)}, bf16[1024,256]{1,0:T(8,128)(2,1)}, u32[]{:S(2)}) copy-start(bf16[1024,256]{1,0:T(8,128)(2,1)} %refs_1_.3) | copy-start | bytes 1572868
  3.9 3.0 %collective-permute-start.1 = (f32[1024,128]{1,0:T(8,128)S(1)}, f32[1024,128]{1,0:T(8,128)S(1)}, u32[]{:S(2)}, u32[]{:S(2)}) collective-permute-start(f32[1024,128]{1,0:T(8,128)S(1)} %select_convert_fusion), channel_id=1, source_target_pairs={{0,1},{1,0},{2,3},{3,2},{4,5},{5,4},{6,7},{7,6},{8,9},{9,8},{10,11... | collective-permute-start | bytes 1572872 | tf_op jit(solution)/shard_map/ppermute | solution.py:333
  6.2 2.2 %copy-start.1 = (bf16[2048,1024]{1,0:T(8,128)(2,1)S(1)}, bf16[2048,1024]{1,0:T(8,128)(2,1)}, u32[]{:S(2)}) copy-start(bf16[2048,1024]{1,0:T(8,128)(2,1)} %refs_2_.4) | copy-start | bytes 12582916
  10.3 2.7 %collective-permute-start.2 = (f32[2048,128]{1,0:T(8,128)S(1)}, f32[2048,128]{1,0:T(8,128)S(1)}, u32[]{:S(2)}, u32[]{:S(2)}) collective-permute-start(f32[2048,128]{1,0:T(8,128)S(1)} %get-tuple-element.31), channel_id=1, source_target_pairs={{0,1},{1,0},{2,3},{3,2},{4,5},{5,4},{6,7},{7,6},{8,9},{9,8},{10,11... | collective-permute-start | bytes 3145736 | tf_op jit(solution)/shard_map/ppermute | solution.py:348
  10.4 2.5 %collective-permute-start.3 = (s32[1,128]{1,0:T(1,128)S(1)}, s32[1,128]{1,0:T(1,128)S(1)}, u32[]{:S(2)}, u32[]{:S(2)}) collective-permute-start(s32[1,128]{1,0:T(1,128)S(1)} %shard_map.104.refs_2_.refs_3_.refs_4_.refs_5_.refs_0_), channel_id=1, source_target_pairs={{0,8},{8,0},{16,24},{24,16},{1,9},{9,1},{17,25},{25,17},{2,10},{10... | collective-permute-start | bytes 1544 | tf_op jit(solution)/shard_map/ppermute | solution.py:329
  13.9 9.9 %collective-permute-start.4 = (f32[640,128]{1,0:T(8,128)S(1)}, f32[640,128]{1,0:T(8,128)S(1)}, u32[]{:S(2)}, u32[]{:S(2)}) collective-permute-start(f32[640,128]{1,0:T(8,128)S(1)} %get-tuple-element.32.refs_0_), channel_id=1, source_target_pairs={{0,8},{16,24},{1,9},{17,25},{2,10},{18,26},{3,11},{19,27},{4,12},{... | collective-permute-start | bytes 983048 | tf_op jit(solution)/shard_map/ppermute | solution.py:356
  17.2 27.2 %collective-permute-start.10 = (f32[2056,128]{1,0:T(8,128)S(1)}, f32[2056,128]{1,0:T(8,128)S(1)}, u32[]{:S(2)}, u32[]{:S(2)}) collective-permute-start(f32[2056,128]{1,0:T(8,128)S(1)} %get-tuple-element.35.refs_8_.refs_4_.refs_2_.refs_3_.refs_6_), channel_id=1, source_target_pairs={{24,16},{25,17},{26,18},{27,19},{28,20},{29,21},{30,22},{31,23}} | collective-permute-start | bytes 3158024 | tf_op jit(solution)/shard_map/ppermute | solution.py:436
  18.5 10.2 %collective-permute-start.5 = (f32[512,128]{1,0:T(8,128)S(1)}, f32[512,128]{1,0:T(8,128)S(1)}, u32[]{:S(2)}, u32[]{:S(2)}) collective-permute-start(f32[512,128]{1,0:T(8,128)S(1)} %get-tuple-element.33.refs_1_), channel_id=1, source_target_pairs={{0,8},{16,24},{1,9},{17,25},{2,10},{18,26},{3,11},{19,27},{4,12},{... | collective-permute-start | bytes 786440 | tf_op jit(solution)/shard_map/ppermute | solution.py:356
  22.5 16.0 %collective-permute-start.6 = (f32[896,128]{1,0:T(8,128)S(1)}, f32[896,128]{1,0:T(8,128)S(1)}, u32[]{:S(2)}, u32[]{:S(2)}) collective-permute-start(f32[896,128]{1,0:T(8,128)S(1)} %get-tuple-element.34.refs_2_), channel_id=1, source_target_pairs={{0,8},{16,24},{1,9},{17,25},{2,10},{18,26},{3,11},{19,27},{4,12},{... | collective-permute-start | bytes 1376264 | tf_op jit(solution)/shard_map/ppermute | solution.py:356
  24.5 14.0 %collective-permute-start.7 = (f32[640,128]{1,0:T(8,128)S(1)}, f32[640,128]{1,0:T(8,128)S(1)}, u32[]{:S(2)}, u32[]{:S(2)}) collective-permute-start(f32[640,128]{1,0:T(8,128)S(1)} %shard_map.111), channel_id=1, source_target_pairs={{8,16},{9,17},{10,18},{11,19},{12,20},{13,21},{14,22},{15,23}} | collective-permute-start | bytes 983048 | tf_op jit(solution)/shard_map/ppermute | solution.py:451
  27.6 17.1 %copy-start = (bf16[2048,1024]{1,0:T(8,128)(2,1)S(1)}, bf16[2048,1024]{1,0:T(8,128)(2,1)}, u32[]{:S(2)}) copy-start(bf16[2048,1024]{1,0:T(8,128)(2,1)} %refs_0_.7) | copy-start | bytes 12582916
  29.4 10.3 %collective-permute-start.8 = (f32[512,128]{1,0:T(8,128)S(1)}, f32[512,128]{1,0:T(8,128)S(1)}, u32[]{:S(2)}, u32[]{:S(2)}) collective-permute-start(f32[512,128]{1,0:T(8,128)S(1)} %shard_map.110.refs_7_), channel_id=1, source_target_pairs={{8,16},{9,17},{10,18},{11,19},{12,20},{13,21},{14,22},{15,23}} | collective-permute-start | bytes 786440 | tf_op jit(solution)/shard_map/ppermute | solution.py:451
  40.5 4.1 %collective-permute-start.9 = (f32[1024,128]{1,0:T(8,128)S(1)}, f32[1024,128]{1,0:T(8,128)S(1)}, u32[]{:S(2)}, u32[]{:S(2)}) collective-permute-start(f32[1024,128]{1,0:T(8,128)S(1)} %get-tuple-element.39), channel_id=1, source_target_pairs={{0,1},{1,0},{2,3},{3,2},{4,5},{5,4},{6,7},{7,6},{8,9},{9,8},{10,11... | collective-permute-start | bytes 1572872 | tf_op jit(solution)/shard_map/ppermute | solution.py:393
  43.1 14.0 %collective-permute-start.21 = (f32[896,128]{1,0:T(8,128)S(1)}, f32[896,128]{1,0:T(8,128)S(1)}, u32[]{:S(2)}, u32[]{:S(2)}) collective-permute-start(f32[896,128]{1,0:T(8,128)S(1)} %shard_map.112.refs_7_), channel_id=1, source_target_pairs={{8,16},{9,17},{10,18},{11,19},{12,20},{13,21},{14,22},{15,23}} | collective-permute-start | bytes 1376264 | tf_op jit(solution)/shard_map/ppermute | solution.py:451
  45.4 2.8 %copy-start.2 = (bf16[1024,1024]{1,0:T(8,128)(2,1)S(1)}, bf16[1024,1024]{1,0:T(8,128)(2,1)}, u32[]{:S(2)}) copy-start(bf16[1024,1024]{1,0:T(8,128)(2,1)} %refs_6_.3) | copy-start | bytes 6291460
  45.4 2.8 %copy-start.4 = (s32[4]{0:T(128)S(1)}, s32[4]{0:T(128)}, u32[]{:S(2)}) copy-start(s32[4]{0:T(128)} %refs_2_.7) | copy-start | bytes 52
  45.4 1.7 %collective-permute-start.11 = (f32[256,256]{1,0:T(8,128)S(1)}, f32[256,256]{1,0:T(8,128)S(1)}, u32[]{:S(2)}, u32[]{:S(2)}) collective-permute-start(f32[256,256]{1,0:T(8,128)S(1)} %get-tuple-element.41), channel_id=1, source_target_pairs={{0,1},{1,0},{2,3},{3,2},{4,5},{5,4},{6,7},{7,6},{8,9},{9,8},{10,11... | collective-permute-start | bytes 786440 | tf_op jit(solution)/shard_map/ppermute | solution.py:399
  45.8 1.5 %collective-permute-start.12 = (f32[256,256]{1,0:T(8,128)S(1)}, f32[256,256]{1,0:T(8,128)S(1)}, u32[]{:S(2)}, u32[]{:S(2)}) collective-permute-start(f32[256,256]{1,0:T(8,128)S(1)} %get-tuple-element.42), channel_id=1, source_target_pairs={{0,1},{1,0},{2,3},{3,2},{4,5},{5,4},{6,7},{7,6},{8,9},{9,8},{10,11... | collective-permute-start | bytes 786440 | tf_op jit(solution)/shard_map/ppermute | solution.py:399
  46.0 1.8 %collective-permute-start.13 = (f32[256,256]{1,0:T(8,128)S(1)}, f32[256,256]{1,0:T(8,128)S(1)}, u32[]{:S(2)}, u32[]{:S(2)}) collective-permute-start(f32[256,256]{1,0:T(8,128)S(1)} %get-tuple-element.43), channel_id=1, source_target_pairs={{0,1},{1,0},{2,3},{3,2},{4,5},{5,4},{6,7},{7,6},{8,9},{9,8},{10,11... | collective-permute-start | bytes 786440 | tf_op jit(solution)/shard_map/ppermute | solution.py:399
  46.4 1.8 %collective-permute-start.14 = (f32[256,256]{1,0:T(8,128)S(1)}, f32[256,256]{1,0:T(8,128)S(1)}, u32[]{:S(2)}, u32[]{:S(2)}) collective-permute-start(f32[256,256]{1,0:T(8,128)S(1)} %get-tuple-element.44), channel_id=1, source_target_pairs={{0,1},{1,0},{2,3},{3,2},{4,5},{5,4},{6,7},{7,6},{8,9},{9,8},{10,11... | collective-permute-start | bytes 786440 | tf_op jit(solution)/shard_map/ppermute | solution.py:399
  49.5 1.4 %collective-permute-start.15 = (f32[256,128]{1,0:T(8,128)S(1)}, f32[256,128]{1,0:T(8,128)S(1)}, u32[]{:S(2)}, u32[]{:S(2)}) collective-permute-start(f32[256,128]{1,0:T(8,128)S(1)} %get-tuple-element.46), channel_id=1, source_target_pairs={{0,1},{1,0},{2,3},{3,2},{4,5},{5,4},{6,7},{7,6},{8,9},{9,8},{10,11... | collective-permute-start | bytes 393224 | tf_op jit(solution)/shard_map/ppermute | solution.py:424
  49.9 1.3 %collective-permute-start.16 = (f32[256,128]{1,0:T(8,128)S(1)}, f32[256,128]{1,0:T(8,128)S(1)}, u32[]{:S(2)}, u32[]{:S(2)}) collective-permute-start(f32[256,128]{1,0:T(8,128)S(1)} %get-tuple-element.47), channel_id=1, source_target_pairs={{0,1},{1,0},{2,3},{3,2},{4,5},{5,4},{6,7},{7,6},{8,9},{9,8},{10,11... | collective-permute-start | bytes 393224 | tf_op jit(solution)/shard_map/ppermute | solution.py:424
  50.0 1.4 %collective-permute-start.17 = (f32[256,128]{1,0:T(8,128)S(1)}, f32[256,128]{1,0:T(8,128)S(1)}, u32[]{:S(2)}, u32[]{:S(2)}) collective-permute-start(f32[256,128]{1,0:T(8,128)S(1)} %get-tuple-element.48), channel_id=1, source_target_pairs={{0,1},{1,0},{2,3},{3,2},{4,5},{5,4},{6,7},{7,6},{8,9},{9,8},{10,11... | collective-permute-start | bytes 393224 | tf_op jit(solution)/shard_map/ppermute | solution.py:424
  50.4 1.3 %collective-permute-start.18 = (f32[256,128]{1,0:T(8,128)S(1)}, f32[256,128]{1,0:T(8,128)S(1)}, u32[]{:S(2)}, u32[]{:S(2)}) collective-permute-start(f32[256,128]{1,0:T(8,128)S(1)} %get-tuple-element.49), channel_id=1, source_target_pairs={{0,1},{1,0},{2,3},{3,2},{4,5},{5,4},{6,7},{7,6},{8,9},{9,8},{10,11... | collective-permute-start | bytes 393224 | tf_op jit(solution)/shard_map/ppermute | solution.py:424
  51.8 16.6 %collective-permute-start.19 = (f32[1032,128]{1,0:T(8,128)S(1)}, f32[1032,128]{1,0:T(8,128)S(1)}, u32[]{:S(2)}, u32[]{:S(2)}) collective-permute-start(f32[1032,128]{1,0:T(8,128)S(1)} %get-tuple-element.50), channel_id=1, source_target_pairs={{8,16},{9,17},{10,18},{11,19},{12,20},{13,21},{14,22},{15,23}} | collective-permute-start | bytes 1585160 | tf_op jit(solution)/shard_map/ppermute | solution.py:485
  53.1 15.3 %collective-permute-start.20 = (f32[1024,128]{1,0:T(8,128)S(1)}, f32[1024,128]{1,0:T(8,128)S(1)}, u32[]{:S(2)}, u32[]{:S(2)}) collective-permute-start(f32[1024,128]{1,0:T(8,128)S(1)} %get-tuple-element.51), channel_id=1, source_target_pairs={{24,16},{25,17},{26,18},{27,19},{28,20},{29,21},{30,22},{31,23}} | collective-permute-start | bytes 1572872 | tf_op jit(solution)/shard_map/ppermute | solution.py:485
  59.4 9.1 %collective-permute-start.22 = (s32[1,128]{1,0:T(1,128)S(1)}, s32[1,128]{1,0:T(1,128)S(1)}, u32[]{:S(2)}, u32[]{:S(2)}) collective-permute-start(s32[1,128]{1,0:T(1,128)S(1)} %shard_map.119), channel_id=1, source_target_pairs={{8,16},{9,17},{10,18},{11,19},{12,20},{13,21},{14,22},{15,23}} | collective-permute-start | bytes 1544 | tf_op jit(solution)/shard_map/ppermute | solution.py:490
  69.3 2.5 %collective-permute-start.23 = (f32[1024,128]{1,0:T(8,128)S(1)}, f32[1024,128]{1,0:T(8,128)S(1)}, u32[]{:S(2)}, u32[]{:S(2)}) collective-permute-start(f32[1024,128]{1,0:T(8,128)S(1)} %get-tuple-element.54), channel_id=1, source_target_pairs={{0,1},{1,0},{2,3},{3,2},{4,5},{5,4},{6,7},{7,6},{8,9},{9,8},{10,11... | collective-permute-start | bytes 1572872 | tf_op jit(solution)/shard_map/ppermute | solution.py:393
  72.7 2.7 %collective-permute-start.24 = (f32[1024,256]{1,0:T(8,128)S(1)}, f32[1024,256]{1,0:T(8,128)S(1)}, u32[]{:S(2)}, u32[]{:S(2)}) collective-permute-start(f32[1024,256]{1,0:T(8,128)S(1)} %get-tuple-element.56), channel_id=1, source_target_pairs={{0,1},{1,0},{2,3},{3,2},{4,5},{5,4},{6,7},{7,6},{8,9},{9,8},{10,11... | collective-permute-start | bytes 3145736 | tf_op jit(solution)/shard_map/ppermute | solution.py:399

commit v4 on v3

--- a/solution.py
+++ b/solution.py
@@ -15,7 +15,7 @@
 COST = 1000
 CUTS, PARTS = (0, 5, 9, 16), 16
 VMEM_MIB = 8
-LEAF_COST = 2 * 10**9
+LEAF_COST = 10**9
 SPLIT = 4
 RELAY_COSTS = (10**9, 1000, 1000)
 BASE_COST = 53 * 10**8

time: 77.2 us -> 76.2 us (0.987)
  local copies, waits for them, and re-layouts: 2.06 us -> 1 us
    unnamed x18, local copies, waits for them, and re-layouts: 2.06 us -> 1 us
where the time goes in v4:
time: 76.2 us; the launch traced here: 75.9 us
  waiting for transfers between devices  27.1 us (36%)
  starting transfers between devices  26.1 us (34%)
  Pallas kernels  18.2 us (24%)
  matrix products  2.44 us (3%)
  local copies, waits for them, and re-layouts  1 us (1%)
  between operations  0.97 us (1%)
    pallas_call x20, Pallas kernels, call(): pl.pallas_call(trimmed, out_shape=outs, in_specs=list(specs) + [ANY] * ex...  18.2 us
    ppermute x3, waiting for transfers between devices, on_device(): lax.ppermute(one, 'leaf', [(i, i + 1) for i in range(0, leaves, 2)])  9.01 us
    ppermute x3, starting transfers between devices, on_device(): lax.ppermute(one, 'leaf', [(i, i + 1) for i in range(0, leaves, 2)])  8.61 us
    ppermute x1, waiting for transfers between devices, on_device(): tag_pair[0] = lax.ppermute(late, 'leaf', up)  7.78 us
    ppermute x3, starting transfers between devices, on_device(): came.append(lax.ppermute(one, 'leaf', up))  3.86 us
    ppermute x2, starting transfers between devices, solve(): lax.ppermute(send, 'col', swap)  3.58 us
    ppermute x3, waiting for transfers between devices, on_device(): came.append(lax.ppermute(one, 'leaf', up))  3.01 us
    ppermute x5, waiting for transfers between devices, solve(): other = [lax.ppermute(one, 'col', swap) for one in across]  2.81 us
  transfers between devices with their start and end apart: 25, of which 18 were waited for; matrix products, arithmetic and copies ran while one was open for 0% of the time, Pallas kernels for 16%

profile of v4, /device:TPU:21, one launch (start us, length us, event | category | flops | bytes accessed | tf_op | source)
XLA Modules:
  0.0 75.9 jit_solution(1738441062508124648)
XLA Ops:
  0.7 2.4 %fusion.refs_2_ = f32[1024,256]{1,0:T(8,128)S(1)} fusion(bf16[1024,256]{1,0:T(8,128)(2,1)} %refs_1_.3, bf16[2048,1024]{1,0:T(8,128)(2,1)} %refs_0_.5), kind=kOutput, calls=%fused_computation | convolution fusion | flops 536870912 | bytes 3670016 | tf_op jit(solution)/shard_map/dot_general | solution.py:31
  3.1 0.7 collective-permute-start
  4.0 1.5 %shard_map.104.refs_2_.refs_3_.refs_4_.refs_5_.refs_0_ = s32[1,128]{1,0:T(1,128)S(1)} custom-call(s32[1,16]{1,0:T(1,128)S(1)} %copy-done.7, s32[1,8]{1,0:T(1,128)S(1)} %copy-done.8, f32[1024,256]{1,0:T(8,128)S(1)} %fusion.refs_2_), custom_call_target="tpu_custom_call" | custom-call | flops 1000000000 | bytes 1 | tf_op jit(solution)/shard_map/pallas_call | solution.py:40
  5.6 0.5 copy-done.1
  6.1 0.6 shard_map.105.refs_0_
  6.9 0.5 copy-done.2
  7.4 1.9 %shard_map.106 = (f32[2048,128]{1,0:T(8,128)S(1)}, f32[2048,128]{1,0:T(8,128)S(1)}) custom-call(f32[1024,256]{1,0:T(8,128)S(1)} %shard_map.105.refs_0_, f32[1024,256]{1,0:T(8,128)S(1)} %collective-permute-done.refs_1_, bf16[2048,1024]{1,0:T(8,128)(2,1)S(1)} %copy-done.2, s32[1,128]{1,0:T(1,128)S(1)} %shard_map.104.refs_2_.refs_3_.refs_4_.refs_5_.refs_0_, ...), custom_call_target="tpu_custom_call" | custom-call | flops 1000 | bytes 1 | tf_op jit(solution)/shard_map/pallas_call | solution.py:40
  9.4 1.3 %collective-permute-start.3 = (s32[1,128]{1,0:T(1,128)S(1)}, s32[1,128]{1,0:T(1,128)S(1)}, u32[]{:S(2)}, u32[]{:S(2)}) collective-permute-start(s32[1,128]{1,0:T(1,128)S(1)} %shard_map.104.refs_2_.refs_3_.refs_4_.refs_5_.refs_0_), channel_id=1, source_target_pairs={{0,8},{8,0},{16,24},{24,16},{1,9},{9,1},{17,25},{25,17},{2,10},{10... | collective-permute-start | bytes 1544 | tf_op jit(solution)/shard_map/ppermute | solution.py:329
  10.8 1.1 %collective-permute-done.3.refs_3_.refs_2_.refs_1_.refs_4_.refs_5_ = s32[1,128]{1,0:T(1,128)S(1)} collective-permute-done((s32[1,128]{1,0:T(1,128)S(1)}, s32[1,128]{1,0:T(1,128)S(1)}, u32[]{:S(2)}, u32[]{:S(2)}) %collective-permute-start.3) | collective-permute-done | bytes 544 | tf_op jit(solution)/shard_map/ppermute | solution.py:329
  12.1 0.9 %shard_map.107 = (f32[640,128]{1,0:T(8,128)S(1)}, f32[512,128]{1,0:T(8,128)S(1)}, f32[896,128]{1,0:T(8,128)S(1)}, f32[2056,128]{1,0:T(8,128)S(1)}) custom-call(f32[2048,128]{1,0:T(8,128)S(1)} %get-tuple-element.30.refs_0_, f32[2048,128]{1,0:T(8,128)S(1)} %collective-permute-done.2.refs_1_, s32[1,128]{1,0:T(1,128)S(1)} %shard_map.104.refs_2_.refs_3_.refs_4_.refs_5_.refs_0_, ...), custom_call_target="tpu_custom_call" | custom-call | flops 1000 | bytes 1 | tf_op jit(solution)/shard_map/pallas_call | solution.py:40
  13.0 3.2 %collective-permute-start.4 = (f32[640,128]{1,0:T(8,128)S(1)}, f32[640,128]{1,0:T(8,128)S(1)}, u32[]{:S(2)}, u32[]{:S(2)}) collective-permute-start(f32[640,128]{1,0:T(8,128)S(1)} %get-tuple-element.32.refs_0_), channel_id=1, source_target_pairs={{0,8},{16,24},{1,9},{17,25},{2,10},{18,26},{3,11},{19,27},{4,12},{... | collective-permute-start | bytes 983048 | tf_op jit(solution)/shard_map/ppermute | solution.py:356
  16.2 1.3 %collective-permute-start.10 = (f32[2056,128]{1,0:T(8,128)S(1)}, f32[2056,128]{1,0:T(8,128)S(1)}, u32[]{:S(2)}, u32[]{:S(2)}) collective-permute-start(f32[2056,128]{1,0:T(8,128)S(1)} %get-tuple-element.35.refs_8_.refs_4_.refs_2_.refs_3_.refs_6_), channel_id=1, source_target_pairs={{24,16},{25,17},{26,18},{27,19},{28,20},{29,21},{30,22},{31,23}} | collective-permute-start | bytes 3158024 | tf_op jit(solution)/shard_map/ppermute | solution.py:436
  17.5 4.1 %collective-permute-start.5 = (f32[512,128]{1,0:T(8,128)S(1)}, f32[512,128]{1,0:T(8,128)S(1)}, u32[]{:S(2)}, u32[]{:S(2)}) collective-permute-start(f32[512,128]{1,0:T(8,128)S(1)} %get-tuple-element.33.refs_1_), channel_id=1, source_target_pairs={{0,8},{16,24},{1,9},{17,25},{2,10},{18,26},{3,11},{19,27},{4,12},{... | collective-permute-start | bytes 786440 | tf_op jit(solution)/shard_map/ppermute | solution.py:356
  21.6 1.3 %collective-permute-start.6 = (f32[896,128]{1,0:T(8,128)S(1)}, f32[896,128]{1,0:T(8,128)S(1)}, u32[]{:S(2)}, u32[]{:S(2)}) collective-permute-start(f32[896,128]{1,0:T(8,128)S(1)} %get-tuple-element.34.refs_2_), channel_id=1, source_target_pairs={{0,8},{16,24},{1,9},{17,25},{2,10},{18,26},{3,11},{19,27},{4,12},{... | collective-permute-start | bytes 1376264 | tf_op jit(solution)/shard_map/ppermute | solution.py:356
  22.9 0.6 shard_map.111
  23.5 1.3 %collective-permute-start.7 = (f32[640,128]{1,0:T(8,128)S(1)}, f32[640,128]{1,0:T(8,128)S(1)}, u32[]{:S(2)}, u32[]{:S(2)}) collective-permute-start(f32[640,128]{1,0:T(8,128)S(1)} %shard_map.111), channel_id=1, source_target_pairs={{8,16},{9,17},{10,18},{11,19},{12,20},{13,21},{14,22},{15,23}} | collective-permute-start | bytes 983048 | tf_op jit(solution)/shard_map/ppermute | solution.py:451
  24.8 0.8 %shard_map.108.refs_2_.refs_6_ = f32[2048,128]{1,0:T(8,128)S(1)} custom-call(f32[640,128]{1,0:T(8,128)S(1)} %get-tuple-element.32.refs_0_, f32[512,128]{1,0:T(8,128)S(1)} %get-tuple-element.33.refs_1_, f32[896,128]{1,0:T(8,128)S(1)} %get-tuple-element.34.refs_2_, s32[1,128]{1,0:T(1,128)S(1)} %shard_map.104.refs_2_.refs_3_.refs_4_.refs_5_.refs_0_, ...), custom_call_target="tpu_custom_call" | custom-call | flops 1000 | bytes 1 | tf_op jit(solution)/shard_map/pallas_call | solution.py:40
  25.7 0.9 %shard_map.109 = (bf16[1024,256]{1,0:T(8,128)(2,1)}, f32[8,128]{1,0:T(8,128)S(1)}) custom-call(f32[1024,256]{1,0:T(8,128)S(1)} %shard_map.105.refs_0_, f32[1024,256]{1,0:T(8,128)S(1)} %collective-permute-done.refs_1_, f32[2048,128]{1,0:T(8,128)S(1)} %shard_map.108.refs_2_.refs_6_), custom_call_target="tpu_custom_call" | custom-call | flops 1000 | bytes 1 | tf_op jit(solution)/shard_map/pallas_call | solution.py:40
  26.6 1.1 %collective-permute-done.5.refs_1_ = f32[512,128]{1,0:T(8,128)S(1)} collective-permute-done((f32[512,128]{1,0:T(8,128)S(1)}, f32[512,128]{1,0:T(8,128)S(1)}, u32[]{:S(2)}, u32[]{:S(2)}) %collective-permute-start.5) | collective-permute-done | bytes 262176 | tf_op jit(solution)/shard_map/ppermute | solution.py:356
  27.7 0.6 shard_map.110.refs_7_
  28.4 1.3 %collective-permute-start.8 = (f32[512,128]{1,0:T(8,128)S(1)}, f32[512,128]{1,0:T(8,128)S(1)}, u32[]{:S(2)}, u32[]{:S(2)}) collective-permute-start(f32[512,128]{1,0:T(8,128)S(1)} %shard_map.110.refs_7_), channel_id=1, source_target_pairs={{8,16},{9,17},{10,18},{11,19},{12,20},{13,21},{14,22},{15,23}} | collective-permute-start | bytes 786440 | tf_op jit(solution)/shard_map/ppermute | solution.py:451
  29.7 7.9 %collective-permute-done.6.refs_2_ = f32[896,128]{1,0:T(8,128)S(1)} collective-permute-done((f32[896,128]{1,0:T(8,128)S(1)}, f32[896,128]{1,0:T(8,128)S(1)}, u32[]{:S(2)}, u32[]{:S(2)}) %collective-permute-start.6) | collective-permute-done | bytes 458784 | tf_op jit(solution)/shard_map/ppermute | solution.py:356
  37.6 0.7 shard_map.112.refs_7_
  38.7 0.9 %shard_map.113 = (f32[1024,128]{1,0:T(8,128)S(1)}, f32[1024,128]{1,0:T(8,128)S(1)}) custom-call(f32[640,128]{1,0:T(8,128)S(1)} %collective-permute-done.4.refs_0_, f32[512,128]{1,0:T(8,128)S(1)} %collective-permute-done.5.refs_1_, f32[896,128]{1,0:T(8,128)S(1)} %collective-permute-done.6.refs_2_, ...), custom_call_target="tpu_custom_call" | custom-call | flops 1000 | bytes 1 | tf_op jit(solution)/shard_map/pallas_call | solution.py:40
  39.5 2.6 %collective-permute-start.9 = (f32[1024,128]{1,0:T(8,128)S(1)}, f32[1024,128]{1,0:T(8,128)S(1)}, u32[]{:S(2)}, u32[]{:S(2)}) collective-permute-start(f32[1024,128]{1,0:T(8,128)S(1)} %get-tuple-element.39), channel_id=1, source_target_pairs={{0,1},{1,0},{2,3},{3,2},{4,5},{5,4},{6,7},{7,6},{8,9},{9,8},{10,11... | collective-permute-start | bytes 1572872 | tf_op jit(solution)/shard_map/ppermute | solution.py:393
  42.1 1.3 %collective-permute-start.21 = (f32[896,128]{1,0:T(8,128)S(1)}, f32[896,128]{1,0:T(8,128)S(1)}, u32[]{:S(2)}, u32[]{:S(2)}) collective-permute-start(f32[896,128]{1,0:T(8,128)S(1)} %shard_map.112.refs_7_), channel_id=1, source_target_pairs={{8,16},{9,17},{10,18},{11,19},{12,20},{13,21},{14,22},{15,23}} | collective-permute-start | bytes 1376264 | tf_op jit(solution)/shard_map/ppermute | solution.py:451
  43.7 0.7 shard_map.114
  44.4 0.5 collective-permute-start.11
  45.0 0.4 collective-permute-start.13
  45.5 0.6 shard_map.115.refs_0_
  46.4 0.4 collective-permute-done.13.refs_3_
  47.2 1.3 %shard_map.116 = (bf16[1024,256]{1,0:T(8,128)(2,1)S(1)}, f32[1024,128]{1,0:T(8,128)S(1)}, f32[256,128]{1,0:T(8,128)S(1)}, f32[256,128]{1,0:T(8,128)S(1)}, f32[25...) custom-call(f32[1024,256]{1,0:T(8,128)S(1)} %shard_map.115.refs_0_, f32[256,256]{1,0:T(8,128)S(1)} %collective-permute-done.11.refs_1_, ...), custom_call_target="tpu_custom_call" | custom-call | flops 1000 | bytes 1 | tf_op jit(solution)/shard_map/pallas_call | solution.py:40
  48.5 0.4 collective-permute-start.15
  50.9 1.3 %collective-permute-start.19 = (f32[1032,128]{1,0:T(8,128)S(1)}, f32[1032,128]{1,0:T(8,128)S(1)}, u32[]{:S(2)}, u32[]{:S(2)}) collective-permute-start(f32[1032,128]{1,0:T(8,128)S(1)} %get-tuple-element.50), channel_id=1, source_target_pairs={{8,16},{9,17},{10,18},{11,19},{12,20},{13,21},{14,22},{15,23}} | collective-permute-start | bytes 1585160 | tf_op jit(solution)/shard_map/ppermute | solution.py:485
  52.2 1.3 %collective-permute-start.20 = (f32[1024,128]{1,0:T(8,128)S(1)}, f32[1024,128]{1,0:T(8,128)S(1)}, u32[]{:S(2)}, u32[]{:S(2)}) collective-permute-start(f32[1024,128]{1,0:T(8,128)S(1)} %get-tuple-element.51), channel_id=1, source_target_pairs={{24,16},{25,17},{26,18},{27,19},{28,20},{29,21},{30,22},{31,23}} | collective-permute-start | bytes 1572872 | tf_op jit(solution)/shard_map/ppermute | solution.py:485
  53.5 2.7 %collective-permute-done.21.refs_8_ = f32[896,128]{1,0:T(8,128)S(1)} collective-permute-done((f32[896,128]{1,0:T(8,128)S(1)}, f32[896,128]{1,0:T(8,128)S(1)}, u32[]{:S(2)}, u32[]{:S(2)}) %collective-permute-start.21) | collective-permute-done | bytes 458784 | tf_op jit(solution)/shard_map/ppermute | solution.py:451
  56.1 1.1 %shard_map.118.refs_1_.refs_4_ = f32[2048,128]{1,0:T(8,128)S(1)} custom-call(f32[640,128]{1,0:T(8,128)S(1)} %get-tuple-element.32.refs_0_, f32[512,128]{1,0:T(8,128)S(1)} %get-tuple-element.33.refs_1_, f32[896,128]{1,0:T(8,128)S(1)} %get-tuple-element.34.refs_2_, s32[1,128]{1,0:T(1,128)S(1)} %shard_map.104.refs_2_.refs_3_.refs_4_.refs_5_.refs_0_, ...), custom_call_target="tpu_custom_call" | custom-call | flops 5299999744 | bytes 1 | tf_op jit(solution)/shard_map/pallas_call | solution.py:40
  57.2 1.2 %shard_map.119 = s32[1,128]{1,0:T(1,128)S(1)} custom-call(s32[1,128]{1,0:T(1,128)S(1)} %shard_map.104.refs_2_.refs_3_.refs_4_.refs_5_.refs_0_, f32[2048,128]{1,0:T(8,128)S(1)} %shard_map.118.refs_1_.refs_4_), custom_call_target="tpu_custom_call" | custom-call | flops 1000 | bytes 1 | tf_op jit(solution)/shard_map/pallas_call | solution.py:40
  58.4 1.3 %collective-permute-start.22 = (s32[1,128]{1,0:T(1,128)S(1)}, s32[1,128]{1,0:T(1,128)S(1)}, u32[]{:S(2)}, u32[]{:S(2)}) collective-permute-start(s32[1,128]{1,0:T(1,128)S(1)} %shard_map.119), channel_id=1, source_target_pairs={{8,16},{9,17},{10,18},{11,19},{12,20},{13,21},{14,22},{15,23}} | collective-permute-start | bytes 1544 | tf_op jit(solution)/shard_map/ppermute | solution.py:490
  59.7 7.8 %collective-permute-done.22.refs_2_ = s32[1,128]{1,0:T(1,128)S(1)} collective-permute-done((s32[1,128]{1,0:T(1,128)S(1)}, s32[1,128]{1,0:T(1,128)S(1)}, u32[]{:S(2)}, u32[]{:S(2)}) %collective-permute-start.22) | collective-permute-done | bytes 544 | tf_op jit(solution)/shard_map/ppermute | solution.py:490
  67.5 0.9 %shard_map.120 = (f32[1024,128]{1,0:T(8,128)S(1)}, f32[1024,128]{1,0:T(8,128)S(1)}) custom-call(f32[1032,128]{1,0:T(8,128)S(1)} %collective-permute-done.19.refs_0_, f32[1024,128]{1,0:T(8,128)S(1)} %collective-permute-done.20.refs_1_, s32[1,128]{1,0:T(1,128)S(1)} %collective-permute-done.22.refs_2_, ...), custom_call_target="tpu_custom_call" | custom-call | flops 1000 | bytes 1 | tf_op jit(solution)/shard_map/pallas_call | solution.py:40
  68.4 1.0 %collective-permute-start.23 = (f32[1024,128]{1,0:T(8,128)S(1)}, f32[1024,128]{1,0:T(8,128)S(1)}, u32[]{:S(2)}, u32[]{:S(2)}) collective-permute-start(f32[1024,128]{1,0:T(8,128)S(1)} %get-tuple-element.54), channel_id=1, source_target_pairs={{0,1},{1,0},{2,3},{3,2},{4,5},{5,4},{6,7},{7,6},{8,9},{9,8},{10,11... | collective-permute-start | bytes 1572872 | tf_op jit(solution)/shard_map/ppermute | solution.py:393
  69.4 1.5 %collective-permute-done.23.refs_1_ = f32[1024,128]{1,0:T(8,128)S(1)} collective-permute-done((f32[1024,128]{1,0:T(8,128)S(1)}, f32[1024,128]{1,0:T(8,128)S(1)}, u32[]{:S(2)}, u32[]{:S(2)}) %collective-permute-start.23) | collective-permute-done | bytes 524320 | tf_op jit(solution)/shard_map/ppermute | solution.py:393
  70.9 0.8 %shard_map.121 = (bf16[1024,256]{1,0:T(8,128)(2,1)S(1)}, f32[1024,256]{1,0:T(8,128)S(1)}) custom-call(f32[1024,128]{1,0:T(8,128)S(1)} %get-tuple-element.53.refs_0_, f32[1024,128]{1,0:T(8,128)S(1)} %collective-permute-done.23.refs_1_, bf16[2048,1024]{1,0:T(8,128)(2,1)S(1)} %copy-done), custom_call_target="tpu_custom_call" | custom-call | flops 1000 | bytes 1 | tf_op jit(solution)/shard_map/pallas_call | solution.py:40
  71.7 0.4 collective-permute-start.24
  72.1 0.6 shard_map.122.refs_0_
  72.7 1.7 %collective-permute-done.24.refs_1_ = f32[1024,256]{1,0:T(8,128)S(1)} collective-permute-done((f32[1024,256]{1,0:T(8,128)S(1)}, f32[1024,256]{1,0:T(8,128)S(1)}, u32[]{:S(2)}, u32[]{:S(2)}) %collective-permute-start.24) | collective-permute-done | bytes 1048608 | tf_op jit(solution)/shard_map/ppermute | solution.py:399
  74.4 1.5 %shard_map.123 = bf16[1024,256]{1,0:T(8,128)(2,1)} custom-call(f32[1024,256]{1,0:T(8,128)S(1)} %shard_map.122.refs_0_, f32[1024,256]{1,0:T(8,128)S(1)} %collective-permute-done.24.refs_1_, s32[4]{0:T(128)S(1)} %copy-done.6, bf16[1024,256]{1,0:T(8,128)(2,1)S(1)} %get-tuple-element.57.refs_3_), custom_call_target="tpu_custom_call" | custom-call | flops 1000 | bytes 1 | tf_op jit(solution)/shard_map/pallas_call | solution.py:40
  (42 shorter events, 4.2 us)
Async XLA Ops:
  0.6 3.2 %copy-start.4 = (bf16[1024,256]{1,0:T(8,128)(2,1)S(1)}, bf16[1024,256]{1,0:T(8,128)(2,1)}, u32[]{:S(2)}) copy-start(bf16[1024,256]{1,0:T(8,128)(2,1)} %refs_10_.1) | copy-start | bytes 1572868
  0.6 3.4 %copy-start.8 = (s32[1,8]{1,0:T(1,128)S(1)}, s32[1,8]{1,0:T(1,128)}, u32[]{:S(2)}) copy-start(s32[1,8]{1,0:T(1,128)} %refs_1_.2) | copy-start | bytes 100
  0.7 3.4 %copy-start.7 = (s32[1,16]{1,0:T(1,128)S(1)}, s32[1,16]{1,0:T(1,128)}, u32[]{:S(2)}) copy-start(s32[1,16]{1,0:T(1,128)} %refs_0_.4) | copy-start | bytes 196
  3.1 2.5 %copy-start.5 = (bf16[1024,256]{1,0:T(8,128)(2,1)S(1)}, bf16[1024,256]{1,0:T(8,128)(2,1)}, u32[]{:S(2)}) copy-start(bf16[1024,256]{1,0:T(8,128)(2,1)} %refs_1_.3) | copy-start | bytes 1572868
  3.1 3.8 %collective-permute-start = (f32[1024,256]{1,0:T(8,128)S(1)}, f32[1024,256]{1,0:T(8,128)S(1)}, u32[]{:S(2)}, u32[]{:S(2)}) collective-permute-start(f32[1024,256]{1,0:T(8,128)S(1)} %fusion.refs_2_), channel_id=1, source_target_pairs={{0,1},{1,0},{2,3},{3,2},{4,5},{5,4},{6,7},{7,6},{8,9},{9,8},{10,11... | collective-permute-start | bytes 3145736 | tf_op jit(solution)/shard_map/ppermute | solution.py:309
  3.9 2.2 %copy-start.1 = (bf16[2048,1024]{1,0:T(8,128)(2,1)S(1)}, bf16[2048,1024]{1,0:T(8,128)(2,1)}, u32[]{:S(2)}) copy-start(bf16[2048,1024]{1,0:T(8,128)(2,1)} %refs_0_.5) | copy-start | bytes 12582916
  3.9 3.5 %copy-start.2 = (bf16[2048,1024]{1,0:T(8,128)(2,1)S(1)}, bf16[2048,1024]{1,0:T(8,128)(2,1)}, u32[]{:S(2)}) copy-start(bf16[2048,1024]{1,0:T(8,128)(2,1)} %refs_2_.4) | copy-start | bytes 12582916
  3.9 3.0 %collective-permute-start.1 = (f32[1024,128]{1,0:T(8,128)S(1)}, f32[1024,128]{1,0:T(8,128)S(1)}, u32[]{:S(2)}, u32[]{:S(2)}) collective-permute-start(f32[1024,128]{1,0:T(8,128)S(1)} %select_convert_fusion), channel_id=1, source_target_pairs={{0,1},{1,0},{2,3},{3,2},{4,5},{5,4},{6,7},{7,6},{8,9},{9,8},{10,11... | collective-permute-start | bytes 1572872 | tf_op jit(solution)/shard_map/ppermute | solution.py:333
  9.3 2.7 %collective-permute-start.2 = (f32[2048,128]{1,0:T(8,128)S(1)}, f32[2048,128]{1,0:T(8,128)S(1)}, u32[]{:S(2)}, u32[]{:S(2)}) collective-permute-start(f32[2048,128]{1,0:T(8,128)S(1)} %get-tuple-element.31), channel_id=1, source_target_pairs={{0,1},{1,0},{2,3},{3,2},{4,5},{5,4},{6,7},{7,6},{8,9},{9,8},{10,11... | collective-permute-start | bytes 3145736 | tf_op jit(solution)/shard_map/ppermute | solution.py:348
  9.4 2.4 %collective-permute-start.3 = (s32[1,128]{1,0:T(1,128)S(1)}, s32[1,128]{1,0:T(1,128)S(1)}, u32[]{:S(2)}, u32[]{:S(2)}) collective-permute-start(s32[1,128]{1,0:T(1,128)S(1)} %shard_map.104.refs_2_.refs_3_.refs_4_.refs_5_.refs_0_), channel_id=1, source_target_pairs={{0,8},{8,0},{16,24},{24,16},{1,9},{9,1},{17,25},{25,17},{2,10},{10... | collective-permute-start | bytes 1544 | tf_op jit(solution)/shard_map/ppermute | solution.py:329
  13.0 9.9 %collective-permute-start.4 = (f32[640,128]{1,0:T(8,128)S(1)}, f32[640,128]{1,0:T(8,128)S(1)}, u32[]{:S(2)}, u32[]{:S(2)}) collective-permute-start(f32[640,128]{1,0:T(8,128)S(1)} %get-tuple-element.32.refs_0_), channel_id=1, source_target_pairs={{0,8},{16,24},{1,9},{17,25},{2,10},{18,26},{3,11},{19,27},{4,12},{... | collective-permute-start | bytes 983048 | tf_op jit(solution)/shard_map/ppermute | solution.py:356
  16.2 27.2 %collective-permute-start.10 = (f32[2056,128]{1,0:T(8,128)S(1)}, f32[2056,128]{1,0:T(8,128)S(1)}, u32[]{:S(2)}, u32[]{:S(2)}) collective-permute-start(f32[2056,128]{1,0:T(8,128)S(1)} %get-tuple-element.35.refs_8_.refs_4_.refs_2_.refs_3_.refs_6_), channel_id=1, source_target_pairs={{24,16},{25,17},{26,18},{27,19},{28,20},{29,21},{30,22},{31,23}} | collective-permute-start | bytes 3158024 | tf_op jit(solution)/shard_map/ppermute | solution.py:436
  17.5 10.2 %collective-permute-start.5 = (f32[512,128]{1,0:T(8,128)S(1)}, f32[512,128]{1,0:T(8,128)S(1)}, u32[]{:S(2)}, u32[]{:S(2)}) collective-permute-start(f32[512,128]{1,0:T(8,128)S(1)} %get-tuple-element.33.refs_1_), channel_id=1, source_target_pairs={{0,8},{16,24},{1,9},{17,25},{2,10},{18,26},{3,11},{19,27},{4,12},{... | collective-permute-start | bytes 786440 | tf_op jit(solution)/shard_map/ppermute | solution.py:356
  21.6 16.0 %collective-permute-start.6 = (f32[896,128]{1,0:T(8,128)S(1)}, f32[896,128]{1,0:T(8,128)S(1)}, u32[]{:S(2)}, u32[]{:S(2)}) collective-permute-start(f32[896,128]{1,0:T(8,128)S(1)} %get-tuple-element.34.refs_2_), channel_id=1, source_target_pairs={{0,8},{16,24},{1,9},{17,25},{2,10},{18,26},{3,11},{19,27},{4,12},{... | collective-permute-start | bytes 1376264 | tf_op jit(solution)/shard_map/ppermute | solution.py:356
  23.5 14.0 %collective-permute-start.7 = (f32[640,128]{1,0:T(8,128)S(1)}, f32[640,128]{1,0:T(8,128)S(1)}, u32[]{:S(2)}, u32[]{:S(2)}) collective-permute-start(f32[640,128]{1,0:T(8,128)S(1)} %shard_map.111), channel_id=1, source_target_pairs={{8,16},{9,17},{10,18},{11,19},{12,20},{13,21},{14,22},{15,23}} | collective-permute-start | bytes 983048 | tf_op jit(solution)/shard_map/ppermute | solution.py:451
  26.6 17.0 %copy-start = (bf16[2048,1024]{1,0:T(8,128)(2,1)S(1)}, bf16[2048,1024]{1,0:T(8,128)(2,1)}, u32[]{:S(2)}) copy-start(bf16[2048,1024]{1,0:T(8,128)(2,1)} %refs_0_.7) | copy-start | bytes 12582916
  28.4 10.3 %collective-permute-start.8 = (f32[512,128]{1,0:T(8,128)S(1)}, f32[512,128]{1,0:T(8,128)S(1)}, u32[]{:S(2)}, u32[]{:S(2)}) collective-permute-start(f32[512,128]{1,0:T(8,128)S(1)} %shard_map.110.refs_7_), channel_id=1, source_target_pairs={{8,16},{9,17},{10,18},{11,19},{12,20},{13,21},{14,22},{15,23}} | collective-permute-start | bytes 786440 | tf_op jit(solution)/shard_map/ppermute | solution.py:451
  39.5 4.1 %collective-permute-start.9 = (f32[1024,128]{1,0:T(8,128)S(1)}, f32[1024,128]{1,0:T(8,128)S(1)}, u32[]{:S(2)}, u32[]{:S(2)}) collective-permute-start(f32[1024,128]{1,0:T(8,128)S(1)} %get-tuple-element.39), channel_id=1, source_target_pairs={{0,1},{1,0},{2,3},{3,2},{4,5},{5,4},{6,7},{7,6},{8,9},{9,8},{10,11... | collective-permute-start | bytes 1572872 | tf_op jit(solution)/shard_map/ppermute | solution.py:393
  42.1 14.0 %collective-permute-start.21 = (f32[896,128]{1,0:T(8,128)S(1)}, f32[896,128]{1,0:T(8,128)S(1)}, u32[]{:S(2)}, u32[]{:S(2)}) collective-permute-start(f32[896,128]{1,0:T(8,128)S(1)} %shard_map.112.refs_7_), channel_id=1, source_target_pairs={{8,16},{9,17},{10,18},{11,19},{12,20},{13,21},{14,22},{15,23}} | collective-permute-start | bytes 1376264 | tf_op jit(solution)/shard_map/ppermute | solution.py:451
  44.4 2.8 %copy-start.3 = (bf16[1024,1024]{1,0:T(8,128)(2,1)S(1)}, bf16[1024,1024]{1,0:T(8,128)(2,1)}, u32[]{:S(2)}) copy-start(bf16[1024,1024]{1,0:T(8,128)(2,1)} %refs_6_.3) | copy-start | bytes 6291460
  44.4 2.8 %copy-start.6 = (s32[4]{0:T(128)S(1)}, s32[4]{0:T(128)}, u32[]{:S(2)}) copy-start(s32[4]{0:T(128)} %refs_2_.7) | copy-start | bytes 52
  44.4 1.7 %collective-permute-start.11 = (f32[256,256]{1,0:T(8,128)S(1)}, f32[256,256]{1,0:T(8,128)S(1)}, u32[]{:S(2)}, u32[]{:S(2)}) collective-permute-start(f32[256,256]{1,0:T(8,128)S(1)} %get-tuple-element.41), channel_id=1, source_target_pairs={{0,1},{1,0},{2,3},{3,2},{4,5},{5,4},{6,7},{7,6},{8,9},{9,8},{10,11... | collective-permute-start | bytes 786440 | tf_op jit(solution)/shard_map/ppermute | solution.py:399
  44.9 1.5 %collective-permute-start.12 = (f32[256,256]{1,0:T(8,128)S(1)}, f32[256,256]{1,0:T(8,128)S(1)}, u32[]{:S(2)}, u32[]{:S(2)}) collective-permute-start(f32[256,256]{1,0:T(8,128)S(1)} %get-tuple-element.42), channel_id=1, source_target_pairs={{0,1},{1,0},{2,3},{3,2},{4,5},{5,4},{6,7},{7,6},{8,9},{9,8},{10,11... | collective-permute-start | bytes 786440 | tf_op jit(solution)/shard_map/ppermute | solution.py:399
  45.0 1.8 %collective-permute-start.13 = (f32[256,256]{1,0:T(8,128)S(1)}, f32[256,256]{1,0:T(8,128)S(1)}, u32[]{:S(2)}, u32[]{:S(2)}) collective-permute-start(f32[256,256]{1,0:T(8,128)S(1)} %get-tuple-element.43), channel_id=1, source_target_pairs={{0,1},{1,0},{2,3},{3,2},{4,5},{5,4},{6,7},{7,6},{8,9},{9,8},{10,11... | collective-permute-start | bytes 786440 | tf_op jit(solution)/shard_map/ppermute | solution.py:399
  45.4 1.8 %collective-permute-start.14 = (f32[256,256]{1,0:T(8,128)S(1)}, f32[256,256]{1,0:T(8,128)S(1)}, u32[]{:S(2)}, u32[]{:S(2)}) collective-permute-start(f32[256,256]{1,0:T(8,128)S(1)} %get-tuple-element.44), channel_id=1, source_target_pairs={{0,1},{1,0},{2,3},{3,2},{4,5},{5,4},{6,7},{7,6},{8,9},{9,8},{10,11... | collective-permute-start | bytes 786440 | tf_op jit(solution)/shard_map/ppermute | solution.py:399
  48.5 1.4 %collective-permute-start.15 = (f32[256,128]{1,0:T(8,128)S(1)}, f32[256,128]{1,0:T(8,128)S(1)}, u32[]{:S(2)}, u32[]{:S(2)}) collective-permute-start(f32[256,128]{1,0:T(8,128)S(1)} %get-tuple-element.46), channel_id=1, source_target_pairs={{0,1},{1,0},{2,3},{3,2},{4,5},{5,4},{6,7},{7,6},{8,9},{9,8},{10,11... | collective-permute-start | bytes 393224 | tf_op jit(solution)/shard_map/ppermute | solution.py:424
  48.9 1.3 %collective-permute-start.16 = (f32[256,128]{1,0:T(8,128)S(1)}, f32[256,128]{1,0:T(8,128)S(1)}, u32[]{:S(2)}, u32[]{:S(2)}) collective-permute-start(f32[256,128]{1,0:T(8,128)S(1)} %get-tuple-element.47), channel_id=1, source_target_pairs={{0,1},{1,0},{2,3},{3,2},{4,5},{5,4},{6,7},{7,6},{8,9},{9,8},{10,11... | collective-permute-start | bytes 393224 | tf_op jit(solution)/shard_map/ppermute | solution.py:424
  49.1 1.4 %collective-permute-start.17 = (f32[256,128]{1,0:T(8,128)S(1)}, f32[256,128]{1,0:T(8,128)S(1)}, u32[]{:S(2)}, u32[]{:S(2)}) collective-permute-start(f32[256,128]{1,0:T(8,128)S(1)} %get-tuple-element.48), channel_id=1, source_target_pairs={{0,1},{1,0},{2,3},{3,2},{4,5},{5,4},{6,7},{7,6},{8,9},{9,8},{10,11... | collective-permute-start | bytes 393224 | tf_op jit(solution)/shard_map/ppermute | solution.py:424
  49.4 1.3 %collective-permute-start.18 = (f32[256,128]{1,0:T(8,128)S(1)}, f32[256,128]{1,0:T(8,128)S(1)}, u32[]{:S(2)}, u32[]{:S(2)}) collective-permute-start(f32[256,128]{1,0:T(8,128)S(1)} %get-tuple-element.49), channel_id=1, source_target_pairs={{0,1},{1,0},{2,3},{3,2},{4,5},{5,4},{6,7},{7,6},{8,9},{9,8},{10,11... | collective-permute-start | bytes 393224 | tf_op jit(solution)/shard_map/ppermute | solution.py:424
  50.9 16.6 %collective-permute-start.19 = (f32[1032,128]{1,0:T(8,128)S(1)}, f32[1032,128]{1,0:T(8,128)S(1)}, u32[]{:S(2)}, u32[]{:S(2)}) collective-permute-start(f32[1032,128]{1,0:T(8,128)S(1)} %get-tuple-element.50), channel_id=1, source_target_pairs={{8,16},{9,17},{10,18},{11,19},{12,20},{13,21},{14,22},{15,23}} | collective-permute-start | bytes 1585160 | tf_op jit(solution)/shard_map/ppermute | solution.py:485
  52.2 15.3 %collective-permute-start.20 = (f32[1024,128]{1,0:T(8,128)S(1)}, f32[1024,128]{1,0:T(8,128)S(1)}, u32[]{:S(2)}, u32[]{:S(2)}) collective-permute-start(f32[1024,128]{1,0:T(8,128)S(1)} %get-tuple-element.51), channel_id=1, source_target_pairs={{24,16},{25,17},{26,18},{27,19},{28,20},{29,21},{30,22},{31,23}} | collective-permute-start | bytes 1572872 | tf_op jit(solution)/shard_map/ppermute | solution.py:485
  58.4 9.1 %collective-permute-start.22 = (s32[1,128]{1,0:T(1,128)S(1)}, s32[1,128]{1,0:T(1,128)S(1)}, u32[]{:S(2)}, u32[]{:S(2)}) collective-permute-start(s32[1,128]{1,0:T(1,128)S(1)} %shard_map.119), channel_id=1, source_target_pairs={{8,16},{9,17},{10,18},{11,19},{12,20},{13,21},{14,22},{15,23}} | collective-permute-start | bytes 1544 | tf_op jit(solution)/shard_map/ppermute | solution.py:490
  68.4 2.5 %collective-permute-start.23 = (f32[1024,128]{1,0:T(8,128)S(1)}, f32[1024,128]{1,0:T(8,128)S(1)}, u32[]{:S(2)}, u32[]{:S(2)}) collective-permute-start(f32[1024,128]{1,0:T(8,128)S(1)} %get-tuple-element.54), channel_id=1, source_target_pairs={{0,1},{1,0},{2,3},{3,2},{4,5},{5,4},{6,7},{7,6},{8,9},{9,8},{10,11... | collective-permute-start | bytes 1572872 | tf_op jit(solution)/shard_map/ppermute | solution.py:393
  71.7 2.7 %collective-permute-start.24 = (f32[1024,256]{1,0:T(8,128)S(1)}, f32[1024,256]{1,0:T(8,128)S(1)}, u32[]{:S(2)}, u32[]{:S(2)}) collective-permute-start(f32[1024,256]{1,0:T(8,128)S(1)} %get-tuple-element.56), channel_id=1, source_target_pairs={{0,1},{1,0},{2,3},{3,2},{4,5},{5,4},{6,7},{7,6},{8,9},{9,8},{10,11... | collective-permute-start | bytes 3145736 | tf_op jit(solution)/shard_map/ppermute | solution.py:399
